TPU v7x, 128 devices: a whole 4x4x4 slice. The times are simulated.
128 devices in a mesh: wide: 16 (over y, z), narrow: 8 (over x, core).
Axes of the slice: x: 4, y: 4, z: 4, core: 2. Of those that a mesh axis runs over, the one named last changes fastest.
Arguments:
- token_ids: int32 [512, 2, 64], P(('wide', 'narrow')), may hold values from 0 to 501759, as said below
- lengths: int32 [512, 2], P(('wide', 'narrow')), may hold values from 16 to 64
- groups: int32 [512], P(('wide', 'narrow')), may hold values from 0 to 15
- table: bfloat16 [501760, 768], P(('wide', 'narrow')), may hold values from -6 to 6
- w_qkv: bfloat16 [1, 768, 2304], P(None, ('wide', 'narrow')), may hold values from -0.21875 to 0.21875
- w_out: bfloat16 [1, 768, 768], P(None, ('wide', 'narrow')), may hold values from -0.625 to 0.625
- w_up: bfloat16 [1, 768, 3072], P(None, ('wide', 'narrow')), may hold values from -0.21875 to 0.21875
- w_down: bfloat16 [1, 3072, 768], P(None, ('wide', 'narrow')), may hold values from -0.109375 to 0.109375
- gains: bfloat16 [1, 2, 768], P(None, None, ('wide', 'narrow')), may hold values from 0.5 to 1.5
- biases: bfloat16 [1, 10, 768], P(None, None, ('wide', 'narrow')), may hold values from -1.25 to 1.25
Outputs:
- loss_terms: float32 [512, 2], P(('wide', 'narrow'))
- token_grads: float32 [512, 2, 64, 768], P(('wide', 'narrow'))
- table_grads: float32 [501760, 768], P(('wide', 'narrow'))
- qkv_grads: float32 [1, 768, 2304], P(None, ('wide', 'narrow'))
- out_grads: float32 [1, 768, 768], P(None, ('wide', 'narrow'))
- up_grads: float32 [1, 768, 3072], P(None, ('wide', 'narrow'))
- down_grads: float32 [1, 3072, 768], P(None, ('wide', 'narrow'))
- gain_grads: float32 [1, 2, 768], P(None, None, ('wide', 'narrow'))
- bias_grads: float32 [1, 10, 768], P(None, None, ('wide', 'narrow'))
Inputs may be any that keep to these rules, and one draw needn't show every extreme that they name: `token_ids`: split the ids into aligned blocks of 2 * 4 * 64 (the tokens of 4 pairs) and the vocabulary into shards of 3920 consecutive rows: no block has more than 8 ids in one shard, and in every draw one shard holds exactly 8 ids of every block.
All inputs are finite; a program needn't handle non-finite values.
Results may differ from a plain program's by a relative error of at most 0.0095.
Values may be sent and summed in bfloat16 or wider, within the bound.
A program may use at most 192 MiB of HBM per device.

v0:
```python
import jax
import jax.numpy as jnp
from jax import lax
from jax.sharding import PartitionSpec as P

HEAD_DIM = 64
SEQ = 64
LAYERS = 1


logit_scale = 10.0
margin = 0.3
norm_eps = 1e-12
pool_eps = 1e-06
far_low = -1e30


def passed_along(value, axis, by):
    devices = lax.axis_size(axis)
    return lax.ppermute(value, axis, [(i, (i + by) % devices) for i in range(devices)])


def joined(value, axis, combine):
    everything = jax.tree.map(lambda part: lax.all_gather(part, axis), value)
    leading = jax.tree.map(lambda part: part[0], everything)

    def hop(k, so_far):
        return combine(so_far, jax.tree.map(lambda part: part[k], everything))

    return lax.fori_loop(1, lax.axis_size(axis), hop, leading)


def layer_norm(inputs, gain_row, bias_row):
    centred = inputs - jnp.mean(inputs, axis=-1, keepdims=True)
    inverse = lax.rsqrt(jnp.mean(centred * centred, axis=-1, keepdims=True) + norm_eps)
    return centred * inverse * gain_row + bias_row


def pooling(states, sent_lengths):
    token_mask = (jnp.arange(SEQ)[None, :] < sent_lengths[:, None]).astype(jnp.float32)
    mean_vec = (
        jnp.sum(states * token_mask[:, :, None], axis=1) / sent_lengths.astype(jnp.float32)[:, None]
    )
    return mean_vec * lax.rsqrt(jnp.sum(mean_vec * mean_vec, axis=-1, keepdims=True) + pool_eps)


def gelu_exact(inputs):
    return jax.nn.gelu(inputs, approximate=False)


def contract_rows(first_part, second_part):
    return lax.dot_general(
        first_part, second_part, (((0,), (0,)), ((), ())), preferred_element_type=jnp.float32
    )


def contract_cols(first_part, second_part):
    return lax.dot_general(
        first_part, second_part, (((1,), (1,)), ((), ())), preferred_element_type=jnp.float32
    )


def exact_rows(first_part, second_part):
    return lax.dot_general(
        first_part,
        second_part,
        (((0,), (0,)), ((), ())),
        precision=lax.Precision.HIGHEST,
        preferred_element_type=jnp.float32,
    )


def exact_cols(first_part, second_part):
    return lax.dot_general(
        first_part,
        second_part,
        (((1,), (1,)), ((), ())),
        precision=lax.Precision.HIGHEST,
        preferred_element_type=jnp.float32,
    )


def exact_dot(first_part, second_part):
    return jnp.dot(
        first_part, second_part, precision=lax.Precision.HIGHEST, preferred_element_type=jnp.float32
    )


def split_heads(qkv_low, sent_count, model_width):
    qkv_parts = qkv_low.reshape(sent_count, SEQ, 3, model_width // HEAD_DIM, HEAD_DIM)
    return (qkv_parts[:, :, 0], qkv_parts[:, :, 1], qkv_parts[:, :, 2])


def masked_scores(query, key_part, key_ok):
    scores = (
        jnp.einsum("sqhd,skhd->shqk", query, key_part, preferred_element_type=jnp.float32) * 0.125
    )
    return jnp.where(key_ok[:, None, None, :], scores, far_low)


def layer_forward(hidden, layer_params, key_ok):
    qkv_w, out_w, up_w, down_w, gain_rows, bias_rows = layer_params
    gain_rows = gain_rows.astype(jnp.float32)
    bias_rows = bias_rows.astype(jnp.float32)
    model_width = out_w.shape[1]
    sent_count = key_ok.shape[0]
    hidden_low = hidden.astype(jnp.bfloat16)
    qkv_bias = jnp.concatenate([bias_rows[0], jnp.zeros_like(bias_rows[0]), bias_rows[1]])
    qkv_low = (jnp.dot(hidden_low, qkv_w, preferred_element_type=jnp.float32) + qkv_bias).astype(
        jnp.bfloat16
    )
    query, key_part, value_part = split_heads(qkv_low, sent_count, model_width)
    scores = masked_scores(query, key_part, key_ok)
    score_peak = jnp.max(scores, axis=-1, keepdims=True)
    score_lse = score_peak + jnp.log(jnp.sum(jnp.exp(scores - score_peak), axis=-1, keepdims=True))
    attn_probs = jnp.exp(scores - score_lse)
    context = jnp.einsum(
        "shqk,skhd->sqhd",
        attn_probs.astype(jnp.bfloat16),
        value_part,
        preferred_element_type=jnp.float32,
    )
    context_low = context.reshape(-1, model_width).astype(jnp.bfloat16)
    resid_one = hidden + (
        jnp.dot(context_low, out_w, preferred_element_type=jnp.float32) + bias_rows[2]
    )
    norm_one = layer_norm(resid_one, gain_rows[0], bias_rows[3])
    norm_low = norm_one.astype(jnp.bfloat16)
    pre_act = jnp.dot(norm_low, up_w, preferred_element_type=jnp.float32) + bias_rows[6:].reshape(
        -1
    )
    act_low = gelu_exact(pre_act).astype(jnp.bfloat16)
    resid_two = norm_one + (
        jnp.dot(act_low, down_w, preferred_element_type=jnp.float32) + bias_rows[4]
    )
    output = layer_norm(resid_two, gain_rows[1], bias_rows[5])
    return (
        output,
        (
            hidden_low,
            qkv_low,
            score_lse,
            context_low,
            resid_one,
            norm_low,
            pre_act,
            act_low,
            resid_two,
        ),
    )


def layer_backward(grad_out, layer_params, saved, key_ok):
    qkv_w, out_w, up_w, down_w, gain_rows, bias_rows = layer_params
    gain_rows = gain_rows.astype(jnp.float32)
    bias_rows = bias_rows.astype(jnp.float32)
    (
        hidden_low,
        qkv_low,
        score_lse,
        context_low,
        resid_one,
        norm_low,
        pre_act,
        act_low,
        resid_two,
    ) = saved
    model_width = out_w.shape[1]
    sent_count = key_ok.shape[0]
    second_back = jax.vjp(layer_norm, resid_two, gain_rows[1], bias_rows[5])[1]
    d_resid_two, d_gain_two, d_shift_two = second_back(grad_out)
    d_ffn = d_resid_two.astype(jnp.bfloat16)
    d_down = contract_rows(act_low, d_ffn)
    gelu_back = jax.vjp(gelu_exact, pre_act)[1]
    d_pre = gelu_back(contract_cols(d_ffn, down_w))[0].astype(jnp.bfloat16)
    d_up = contract_rows(norm_low, d_pre)
    d_norm_one = d_resid_two + contract_cols(d_pre, up_w)
    first_back = jax.vjp(layer_norm, resid_one, gain_rows[0], bias_rows[3])[1]
    d_resid_one, d_gain_one, d_shift_one = first_back(d_norm_one)
    d_attn = d_resid_one.astype(jnp.bfloat16)
    d_out = contract_rows(context_low, d_attn)
    d_context = contract_cols(d_attn, out_w).astype(jnp.bfloat16)
    d_context = d_context.reshape(sent_count, SEQ, model_width // HEAD_DIM, HEAD_DIM)
    query, key_part, value_part = split_heads(qkv_low, sent_count, model_width)
    attn_probs = jnp.exp(masked_scores(query, key_part, key_ok) - score_lse)
    d_value = jnp.einsum(
        "shqk,sqhd->skhd",
        attn_probs.astype(jnp.bfloat16),
        d_context,
        preferred_element_type=jnp.float32,
    )
    d_probs = jnp.einsum(
        "sqhd,skhd->shqk", d_context, value_part, preferred_element_type=jnp.float32
    )
    d_scores = attn_probs * (d_probs - jnp.sum(attn_probs * d_probs, axis=-1, keepdims=True))
    d_scores = d_scores.astype(jnp.bfloat16)
    d_query = (
        jnp.einsum("shqk,skhd->sqhd", d_scores, key_part, preferred_element_type=jnp.float32)
        * 0.125
    )
    d_key = (
        jnp.einsum("shqk,sqhd->skhd", d_scores, query, preferred_element_type=jnp.float32) * 0.125
    )
    d_qkv = (
        jnp.stack([d_query, d_key, d_value], axis=2)
        .reshape(-1, 3 * model_width)
        .astype(jnp.bfloat16)
    )
    d_qkv_w = contract_rows(hidden_low, d_qkv)
    d_hidden = d_resid_one + contract_cols(d_qkv, qkv_w)
    column_sums = jnp.sum(d_qkv.astype(jnp.float32), axis=0)
    d_gains = jnp.stack([d_gain_one, d_gain_two])
    vector_rows = jnp.stack(
        [
            column_sums[:model_width],
            column_sums[2 * model_width :],
            jnp.sum(d_attn.astype(jnp.float32), axis=0),
            d_shift_one,
            jnp.sum(d_ffn.astype(jnp.float32), axis=0),
            d_shift_two,
        ]
    )
    up_rows = jnp.sum(d_pre.astype(jnp.float32), axis=0).reshape(4, model_width)
    d_biases = jnp.concatenate([vector_rows, up_rows])
    return (d_hidden, (d_qkv_w, d_out, d_up, d_down, d_gains, d_biases))


def pair_scores(source, block_rows, own_index, block_begin):
    column_index = block_begin + jnp.arange(block_rows.shape[0])
    same_pair = (own_index[:, None] == column_index[None, :]).astype(jnp.float32)
    raw_scores = logit_scale * exact_cols(source, block_rows) - logit_scale * margin * same_pair
    return (raw_scores, same_pair)


def lse_parts(raw_scores, live_pairs, axis_num):
    masked = jnp.where(live_pairs, raw_scores, far_low)
    peak_val = jnp.max(masked, axis=axis_num)
    summed = jnp.sum(
        jnp.where(live_pairs, jnp.exp(masked - jnp.expand_dims(peak_val, axis_num)), 0.0),
        axis=axis_num,
    )
    return (peak_val, summed)


def lse_join(first_part, second_part):
    peak_val = jnp.maximum(first_part[0], second_part[0])
    summed = first_part[1] * jnp.exp(first_part[0] - peak_val) + second_part[1] * jnp.exp(
        second_part[0] - peak_val
    )
    return (peak_val, summed)


def pair_mix(raw_scores, live_pairs, same_pair, row_lse, col_lse, pair_weight):
    row_part = jnp.where(live_pairs, jnp.exp(raw_scores - row_lse[:, None]), 0.0)
    col_part = jnp.where(live_pairs, jnp.exp(raw_scores - col_lse[None, :]), 0.0)
    return pair_weight * (row_part + col_part) - 2.0 * pair_weight * same_pair


def shards(token_ids, lengths, groups, table, w_qkv, w_out, w_up, w_down, gains, biases):
    pair_count = token_ids.shape[0]
    sent_count = 2 * pair_count
    vocab_rows = table.shape[0]
    model_width = table.shape[1]
    flat_ids = token_ids.reshape(-1)
    token_count = flat_ids.shape[0]
    device_total = lax.axis_size(("wide", "narrow"))
    rank_at = lax.axis_index(("wide", "narrow"))
    slot_cap = max(2, 2 * token_count // device_total)
    owner_of = flat_ids // vocab_rows
    local_of = flat_ids - owner_of * vocab_rows
    owner_hits = (owner_of[:, None] == jnp.arange(device_total)[None, :]).astype(jnp.int32)
    rank_in = jnp.sum(jnp.cumsum(owner_hits, axis=0) * owner_hits, axis=1) - 1
    slot_of = owner_of * slot_cap + rank_in
    id_slots = jnp.full((device_total * slot_cap,), -1, jnp.int32).at[slot_of].set(local_of)
    id_slots = id_slots.reshape(device_total, slot_cap)
    asked = lax.all_to_all(id_slots, ("wide", "narrow"), split_axis=0, concat_axis=0, tiled=True)
    valid = asked >= 0
    found = jnp.take(table, jnp.clip(asked, 0, vocab_rows - 1), axis=0)
    found = jnp.where(valid[..., None], found, jnp.zeros((), table.dtype))
    returned = lax.all_to_all(found, ("wide", "narrow"), split_axis=0, concat_axis=0, tiled=True)
    hidden = returned.reshape(-1, model_width)[slot_of].astype(jnp.float32)
    sent_lengths = lengths.reshape(-1)
    key_ok = jnp.arange(SEQ)[None, :] < sent_lengths[:, None]

    def fetch(layer_at):
        return (
            lax.all_gather(w_qkv[layer_at], ("wide", "narrow"), axis=0, tiled=True),
            lax.all_gather(w_out[layer_at], ("wide", "narrow"), axis=0, tiled=True),
            lax.all_gather(w_up[layer_at], ("wide", "narrow"), axis=0, tiled=True),
            lax.all_gather(w_down[layer_at], ("wide", "narrow"), axis=0, tiled=True),
            lax.all_gather(gains[layer_at], ("wide", "narrow"), axis=1, tiled=True),
            lax.all_gather(biases[layer_at], ("wide", "narrow"), axis=1, tiled=True),
        )

    fetched = []
    layer_at = 0
    layer_params = fetch(layer_at)
    fetched.append(layer_params)
    hidden, saved = layer_forward(hidden, layer_params, key_ok)
    saves = [saved]
    states = hidden.reshape(sent_count, SEQ, model_width)
    pooled, pool_back = jax.vjp(lambda inner_states: pooling(inner_states, sent_lengths), states)
    pair_rows = pooled.reshape(pair_count, 2, model_width)
    source = pair_rows[:, 0]
    target = pair_rows[:, 1]
    group_vals = groups.astype(jnp.float32)
    own_index = rank_at * pair_count + jnp.arange(pair_count)
    total_pairs = pair_count * device_total
    pair_weight = 1.0 / (2.0 * total_pairs)
    diagonal = logit_scale * jnp.sum(source * target, axis=1) - logit_scale * margin
    wide_count = lax.axis_size("wide")
    wide_at = lax.axis_index("wide")
    narrow_at = lax.axis_index("narrow")
    home_rows, home_groups = (
        lax.all_gather(target, "narrow", axis=0, tiled=True),
        lax.all_gather(group_vals, "narrow", axis=0, tiled=True),
    )
    span = home_rows.shape[0]

    def forward_step(carry, cycle_step):
        block_rows, block_groups, col_peak, col_total, row_peak, row_total = carry
        block_begin = (wide_at - cycle_step) % wide_count * span
        raw_scores, same_pair = pair_scores(source, block_rows, own_index, block_begin)
        live_pairs = group_vals[:, None] == block_groups[None, :]
        row_peak, row_total = lse_join((row_peak, row_total), lse_parts(raw_scores, live_pairs, 1))
        col_peak, col_total = lse_join((col_peak, col_total), lse_parts(raw_scores, live_pairs, 0))
        block_rows, block_groups, col_peak, col_total = passed_along(
            (block_rows, block_groups, col_peak, col_total), "wide", 1
        )
        return ((block_rows, block_groups, col_peak, col_total, row_peak, row_total), None)

    start_carry = (
        home_rows,
        home_groups,
        jnp.full((span,), far_low, jnp.float32),
        jnp.zeros((span,), jnp.float32),
        jnp.full((pair_count,), far_low, jnp.float32),
        jnp.zeros((pair_count,), jnp.float32),
    )
    end_carry = lax.scan(forward_step, start_carry, jnp.arange(wide_count))[0]
    row_lse = end_carry[4] + jnp.log(end_carry[5])
    col_peak, col_total = joined((end_carry[2], end_carry[3]), "narrow", lse_join)
    home_lse = col_peak + jnp.log(col_total)
    own_col = lax.dynamic_slice_in_dim(home_lse, narrow_at * pair_count, pair_count)

    def backward_step(carry, cycle_step):
        block_rows, block_groups, block_lse, block_grad, source_grad = carry
        block_begin = (wide_at - cycle_step) % wide_count * span
        raw_scores, same_pair = pair_scores(source, block_rows, own_index, block_begin)
        live_pairs = group_vals[:, None] == block_groups[None, :]
        mix_vals = pair_mix(raw_scores, live_pairs, same_pair, row_lse, block_lse, pair_weight)
        source_grad = source_grad + logit_scale * exact_dot(mix_vals, block_rows)
        block_grad = block_grad + logit_scale * exact_rows(mix_vals, source)
        block_rows, block_groups, block_lse, block_grad = passed_along(
            (block_rows, block_groups, block_lse, block_grad), "wide", 1
        )
        return ((block_rows, block_groups, block_lse, block_grad, source_grad), None)

    back_carry = (
        home_rows,
        home_groups,
        home_lse,
        jnp.zeros((span, model_width), jnp.float32),
        jnp.zeros((pair_count, model_width), jnp.float32),
    )
    back_end = lax.scan(backward_step, back_carry, jnp.arange(wide_count))[0]
    source_grad = back_end[4]
    target_grad = lax.psum_scatter(back_end[3], "narrow", scatter_dimension=0, tiled=True)
    loss_terms = jnp.stack([row_lse - diagonal, own_col - diagonal], axis=1)
    pooled_grad = jnp.stack([source_grad, target_grad], axis=1).reshape(sent_count, model_width)
    d_hidden = pool_back(pooled_grad)[0].reshape(token_count, model_width)
    shard_lists = [[], [], [], [], [], []]
    for layer_at in reversed(range(LAYERS)):
        layer_params = fetch(layer_at)
        d_hidden, layer_grads = layer_backward(d_hidden, layer_params, saves[layer_at], key_ok)
        grad_shards = (
            lax.psum_scatter(layer_grads[0], ("wide", "narrow"), scatter_dimension=0, tiled=True),
            lax.psum_scatter(layer_grads[1], ("wide", "narrow"), scatter_dimension=0, tiled=True),
            lax.psum_scatter(layer_grads[2], ("wide", "narrow"), scatter_dimension=0, tiled=True),
            lax.psum_scatter(layer_grads[3], ("wide", "narrow"), scatter_dimension=0, tiled=True),
            lax.psum_scatter(layer_grads[4], ("wide", "narrow"), scatter_dimension=1, tiled=True),
            lax.psum_scatter(layer_grads[5], ("wide", "narrow"), scatter_dimension=1, tiled=True),
        )
        for member_at in range(6):
            shard_lists[member_at].insert(0, grad_shards[member_at])
    sent_rows = d_hidden.astype(jnp.bfloat16)
    grad_slots = (
        jnp.zeros((device_total * slot_cap, model_width), jnp.bfloat16).at[slot_of].set(sent_rows)
    )
    grad_slots = grad_slots.reshape(device_total, slot_cap, model_width)
    arrived = lax.all_to_all(
        grad_slots, ("wide", "narrow"), split_axis=0, concat_axis=0, tiled=True
    )
    target_slot = jnp.where(asked >= 0, asked, vocab_rows).reshape(-1)
    table_grads = (
        jnp.zeros((vocab_rows, model_width), jnp.float32)
        .at[target_slot]
        .add(arrived.reshape(-1, model_width).astype(jnp.float32), mode="drop")
    )
    token_grads = d_hidden.reshape(pair_count, 2, SEQ, model_width)
    stacked = [jnp.stack(member_list) for member_list in shard_lists]
    return (
        loss_terms,
        token_grads,
        table_grads,
        stacked[0],
        stacked[1],
        stacked[2],
        stacked[3],
        stacked[4],
        stacked[5],
    )


def solution(mesh):
    in_specs = (
        P(("wide", "narrow"), None, None),
        P(("wide", "narrow"), None),
        P(("wide", "narrow")),
        P(("wide", "narrow"), None),
        P(None, ("wide", "narrow"), None),
        P(None, ("wide", "narrow"), None),
        P(None, ("wide", "narrow"), None),
        P(None, ("wide", "narrow"), None),
        P(None, None, ("wide", "narrow")),
        P(None, None, ("wide", "narrow")),
    )
    out_specs = (
        P(("wide", "narrow"), None),
        P(("wide", "narrow"), None, None, None),
        P(("wide", "narrow"), None),
        P(None, ("wide", "narrow"), None),
        P(None, ("wide", "narrow"), None),
        P(None, ("wide", "narrow"), None),
        P(None, ("wide", "narrow"), None),
        P(None, None, ("wide", "narrow")),
        P(None, None, ("wide", "narrow")),
    )
    return jax.shard_map(shards, mesh=mesh, in_specs=in_specs, out_specs=out_specs, check_vma=False)
```

profile of v0, /device:TPU:1, one launch (start us, length us, event | category | flops | bytes accessed | tf_op | source)
XLA Modules:
  0.0 2410.7 jit_solution(13230628991026564270)
XLA Ops:
  18.1 11.5 all-to-all-start
  53.9 49.2 %all-gather.1 = bf16[1,10,768]{1,0,2:T(2,128)(2,1)S(1)} all-gather(bf16[1,10,6]{1,0,2:T(2,128)(2,1)S(1)} %copy.101), channel_id=3, replica_groups=mesh['wide'=16,'narrow'=8] {'wide','narrow'}, dimensions={2}, use_global_device_ids=true | all-gather | bytes 15480 | tf_op jit(solution)/shard_map/all_gather | solution.py:292
  107.0 12.5 all-reduce
  121.1 35.5 %all-gather.3 = bf16[1,2,768]{1,0,2:T(2,128)(2,1)S(1)} all-gather(bf16[1,2,6]{1,0,2:T(2,128)(2,1)S(1)} %copy.110), channel_id=5, replica_groups=mesh['wide'=16,'narrow'=8] {'wide','narrow'}, dimensions={2}, use_global_device_ids=true | all-gather | bytes 3096 | tf_op jit(solution)/shard_map/all_gather | solution.py:291
  157.5 12.8 slice_reduce_fusion
  215.5 16.0 all-gather.18.cloned.1.call-done
  231.5 22.5 multiply_convert_fusion
  254.0 45.0 %all-gather.20.cloned.1.call-done = bf16[1,3072,768]{2,1,0:T(8,128)(2,1)} async-done(((bf16[1,24,768]{2,1,0:T(8,128)(2,1)}), bf16[1,3072,768]{2,1,0:T(8,128)(2,1)}) %all-gather.20.cloned.1.call-update) | async-done | bytes 4718608 | tf_op jit(solution)/shard_map/all_gather | solution.py:290
  308.8 17.0 all-gather.6
  325.9 472.5 %while.62 = (s32[]{:T(128)}, f32[32,768]{1,0:T(8,128)S(1)}, f32[32]{0:T(128)}, f32[32]{0:T(128)S(1)}, f32[32]{0:T(128)S(1)}, /*index=5*/f32[4]{0:T(128)}, f32[4]...) while((s32[]{:T(128)}, f32[32,768]{1,0:T(8,128)S(1)}, ...), condition=%wide.region_17.18_spmd.clone, body=%wide.region_12.17_spmd.clone.sunk | while | flops 1181772 | bytes 705584 | solution.py:340
  338.8 8.9 collective-permute-start.3
  357.9 10.5 collective-permute-start.2
  368.4 8.9 collective-permute-start.3
  387.5 10.5 collective-permute-start.2
  398.1 8.9 collective-permute-start.3
  417.2 10.5 collective-permute-start.2
  427.7 8.9 collective-permute-start.3
  446.8 10.5 collective-permute-start.2
  457.3 8.9 collective-permute-start.3
  476.4 10.5 collective-permute-start.2
  486.9 8.9 collective-permute-start.3
  506.0 10.5 collective-permute-start.2
  516.5 8.9 collective-permute-start.3
  535.6 10.5 collective-permute-start.2
  546.1 8.9 collective-permute-start.3
  565.2 10.5 collective-permute-start.2
  575.8 8.9 collective-permute-start.3
  594.8 10.5 collective-permute-start.2
  605.4 8.9 collective-permute-start.3
  624.5 10.5 collective-permute-start.2
  635.0 8.9 collective-permute-start.3
  654.1 10.5 collective-permute-start.2
  683.7 10.5 collective-permute-start.2
  694.2 8.9 collective-permute-start.3
  713.3 10.5 collective-permute-start.2
  742.9 10.5 collective-permute-start.2
  772.5 10.5 collective-permute-start.2
  798.9 13.4 all-reduce.13
  815.2 529.9 %while.63 = (s32[]{:T(128)}, f32[32,768]{1,0:T(8,128)S(1)}, f32[32]{0:T(128)}, f32[32]{0:T(128)}, f32[32,768]{1,0:T(8,128)S(1)}, /*index=5*/f32[4,768]{1,0:T(4,1...) while((s32[]{:T(128)}, f32[32,768]{1,0:T(8,128)S(1)}, ...), condition=%wide.region_22.23_spmd.clone, body=%wide.region_21.22_spmd.clone.sunk | while | flops 3599028 | bytes 1429536 | solution.py:366
  829.9 8.9 collective-permute-start.7
  863.1 8.9 collective-permute-start.7
  896.3 8.9 collective-permute-start.7
  929.5 8.9 collective-permute-start.7
  962.7 8.9 collective-permute-start.7
  995.9 8.9 collective-permute-start.7
  1029.0 8.9 collective-permute-start.7
  1062.2 8.9 collective-permute-start.7
  1095.4 8.9 collective-permute-start.7
  1128.6 8.9 collective-permute-start.7
  1161.8 8.9 collective-permute-start.7
  1195.0 8.9 collective-permute-start.7
  1228.2 8.9 collective-permute-start.7
  1261.3 8.9 collective-permute-start.7
  1294.5 8.9 collective-permute-start.7
  1327.7 8.9 collective-permute-start.7
  1347.9 50.2 %all-reduce.17.cloned.1.call-done = f32[32,768]{1,0:T(8,128)} async-done(((f32[32,768]{1,0:T(8,128)}), f32[32,768]{1,0:T(8,128)}) %all-reduce.17.cloned.1.call-update) | async-done | bytes 98320
  1415.3 11.4 convert_reduce_fusion.1
  1483.9 375.0 %fusion.107 = (f32[8,2304]{1,0:T(8,128)S(1)}, f32[8,768]{1,0:T(8,128)S(1)}, f32[8,3072]{1,0:T(8,128)S(1)}) fusion(f32[768,2304]{1,0:T(8,128)} %fusion.118, f32[768,768]{1,0:T(8,128)S(1)} %fusion.119, f32[768,3072]{1,0:T(8,128)} %fusion.103), kind=kCustom, calls=%all-reduce-scatter.3 | all-reduce-scatter fusion | flops 6291457 | bytes 19070976
  1870.7 13.5 collective-permute-start.62
  2107.9 72.5 %all-reduce.12 = (f32[2,768]{1,0:T(2,128)S(1)}, f32[10,768]{1,0:T(8,128)S(1)}) all-reduce(f32[2,768]{1,0:T(2,128)S(1)} %pad_maximum_fusion.2, f32[10,768]{1,0:T(8,128)S(1)} %concatenate.7), channel_id=16, replica_groups=mesh['wide'=16,'narrow'=8] {'wide','narrow'}, use_global_device_ids=true, to_apply=%region_38.39.clone | all-reduce | flops 9216 | bytes 73728
  2223.1 27.2 %concatenate.9 = f32[262,768]{1,0:T(8,128)S(1)} concatenate(f32[6,768]{1,0:T(8,128)} %copy-done.77, f32[8,768]{1,0:T(8,128)} %copy-done.75, f32[8,768]{1,0:T(8,128)} %copy-done.76, f32[8,768]{1,0:T(8,128)} %copy-done.78, f32[8,768]{1,0:T(8,128)} %copy-done.79, f32[8,768]{1,0:T(8,128)} %copy-done.80, f32[8,768]{1,0:T(8,128)} %copy-done.81, f32[8,768]{1,0:T(8,128)} %copy-done.82, ...), dimensions={0} | concatenate | bytes 1609728
  2263.7 54.1 %concatenate.8 = f32[262,2304]{1,0:T(8,128)} concatenate(f32[6,2304]{1,0:T(8,128)} %copy-done.44, f32[8,2304]{1,0:T(8,128)S(1)} %collective-permute-done.38, f32[8,2304]{1,0:T(8,128)} %copy-done.42, f32[8,2304]{1,0:T(8,128)} %copy-done.43, f32[8,2304]{1,0:T(8,128)} %copy-done.45, f32[8,2304]{1,0:T(8,128)} %copy-done.46, f32[8,2304]{1,0:T(8,128)} %copy-done.47, ...), dimensions={0} | concatenate | bytes 4829184
  2334.8 54.2 %concatenate.10 = f32[262,3072]{1,0:T(8,128)} concatenate(f32[6,3072]{1,0:T(8,128)S(1)} %collective-permute-done.103, f32[8,3072]{1,0:T(8,128)S(1)} %collective-permute-done.102, f32[8,3072]{1,0:T(8,128)S(1)} %collective-permute-done.101, f32[8,3072]{1,0:T(8,128)S(1)} %collective-permute-done.100, f32[8,3072]{1,0:T(8,128)S(1)} %collective-permute-done.99, ...), dimensions={0} | concatenate | bytes 6438912
  2390.6 12.8 scatter_custom_fusion.2
  (1163 shorter events, 1056.0 us)
Async XLA Ops:
  7.2 169.9 %all-gather.14.cloned.1.call-start = ((), (), s32[]{:S(2)}) async-start(), calls=%async_computation.5 | async-start | bytes 7133184 | tf_op jit(solution)/shard_map/all_gather | solution.py:287
  8.7 202.1 %all-gather.16.cloned.1.call-start = ((), (), s32[]{:S(2)}) async-start(), calls=%async_computation.6 | async-start | bytes 2377728 | tf_op jit(solution)/shard_map/all_gather | solution.py:288
  10.1 221.4 %all-gather.18.cloned.1.call-start = ((), (), s32[]{:S(2)}) async-start(), calls=%async_computation.7 | async-start | bytes 9510912 | tf_op jit(solution)/shard_map/all_gather | solution.py:289
  29.6 269.4 %all-gather.20.cloned.1.call-start = ((), (), s32[]{:S(2)}) async-start(), calls=%async_computation.8 | async-start | bytes 4755456 | tf_op jit(solution)/shard_map/all_gather | solution.py:290
  49.1 125.9 %all-to-all-start.1 = ((bf16[128,8,768]{2,1,0:T(8,128)(2,1)}), bf16[128,8,768]{2,1,0:T(8,128)(2,1)S(1)}, u32[]{:S(2)}, u32[]{:S(2)}) async-start(bf16[128,8,768]{2,1,0:T(8,128)(2,1)} %fusion.61), calls=%async_computation.1 | async-start | bytes 3145728 | tf_op jit(solution)/shard_map/all_to_all | solution.py:280
  53.7 1344.4 %all-reduce.17.cloned.1.call-start = ((), (), s32[]{:S(2)}) async-start(), calls=%async_computation.9 | async-start | bytes 196608
  328.0 26.3 %collective-permute-start = (f32[32,768]{1,0:T(8,128)S(1)}, f32[32,768]{1,0:T(8,128)S(1)}, u32[]{:S(2)}, u32[]{:S(2)}) collective-permute-start(f32[32,768]{1,0:T(8,128)S(1)} %copy.212), channel_id=1, source_target_pairs={{0,8},{8,16},{16,24},{24,32},{32,40},{40,48},{48,56},{56,64},{64,7... | collective-permute-start | bytes 294920 | tf_op jit(solution)/shard_map/while/body/eval_jaxpr/ppermute | solution.py:20
  354.9 28.9 %collective-permute-start = (f32[32,768]{1,0:T(8,128)S(1)}, f32[32,768]{1,0:T(8,128)S(1)}, u32[]{:S(2)}, u32[]{:S(2)}) collective-permute-start(f32[32,768]{1,0:T(8,128)S(1)} %copy.212), channel_id=1, source_target_pairs={{0,8},{8,16},{16,24},{24,32},{32,40},{40,48},{48,56},{56,64},{64,7... | collective-permute-start | bytes 294920 | tf_op jit(solution)/shard_map/while/body/eval_jaxpr/ppermute | solution.py:20
  384.5 28.9 %collective-permute-start = (f32[32,768]{1,0:T(8,128)S(1)}, f32[32,768]{1,0:T(8,128)S(1)}, u32[]{:S(2)}, u32[]{:S(2)}) collective-permute-start(f32[32,768]{1,0:T(8,128)S(1)} %copy.212), channel_id=1, source_target_pairs={{0,8},{8,16},{16,24},{24,32},{32,40},{40,48},{48,56},{56,64},{64,7... | collective-permute-start | bytes 294920 | tf_op jit(solution)/shard_map/while/body/eval_jaxpr/ppermute | solution.py:20
  414.1 28.9 %collective-permute-start = (f32[32,768]{1,0:T(8,128)S(1)}, f32[32,768]{1,0:T(8,128)S(1)}, u32[]{:S(2)}, u32[]{:S(2)}) collective-permute-start(f32[32,768]{1,0:T(8,128)S(1)} %copy.212), channel_id=1, source_target_pairs={{0,8},{8,16},{16,24},{24,32},{32,40},{40,48},{48,56},{56,64},{64,7... | collective-permute-start | bytes 294920 | tf_op jit(solution)/shard_map/while/body/eval_jaxpr/ppermute | solution.py:20
  443.8 28.9 %collective-permute-start = (f32[32,768]{1,0:T(8,128)S(1)}, f32[32,768]{1,0:T(8,128)S(1)}, u32[]{:S(2)}, u32[]{:S(2)}) collective-permute-start(f32[32,768]{1,0:T(8,128)S(1)} %copy.212), channel_id=1, source_target_pairs={{0,8},{8,16},{16,24},{24,32},{32,40},{40,48},{48,56},{56,64},{64,7... | collective-permute-start | bytes 294920 | tf_op jit(solution)/shard_map/while/body/eval_jaxpr/ppermute | solution.py:20
  473.4 28.9 %collective-permute-start = (f32[32,768]{1,0:T(8,128)S(1)}, f32[32,768]{1,0:T(8,128)S(1)}, u32[]{:S(2)}, u32[]{:S(2)}) collective-permute-start(f32[32,768]{1,0:T(8,128)S(1)} %copy.212), channel_id=1, source_target_pairs={{0,8},{8,16},{16,24},{24,32},{32,40},{40,48},{48,56},{56,64},{64,7... | collective-permute-start | bytes 294920 | tf_op jit(solution)/shard_map/while/body/eval_jaxpr/ppermute | solution.py:20
  503.0 28.9 %collective-permute-start = (f32[32,768]{1,0:T(8,128)S(1)}, f32[32,768]{1,0:T(8,128)S(1)}, u32[]{:S(2)}, u32[]{:S(2)}) collective-permute-start(f32[32,768]{1,0:T(8,128)S(1)} %copy.212), channel_id=1, source_target_pairs={{0,8},{8,16},{16,24},{24,32},{32,40},{40,48},{48,56},{56,64},{64,7... | collective-permute-start | bytes 294920 | tf_op jit(solution)/shard_map/while/body/eval_jaxpr/ppermute | solution.py:20
  532.6 28.9 %collective-permute-start = (f32[32,768]{1,0:T(8,128)S(1)}, f32[32,768]{1,0:T(8,128)S(1)}, u32[]{:S(2)}, u32[]{:S(2)}) collective-permute-start(f32[32,768]{1,0:T(8,128)S(1)} %copy.212), channel_id=1, source_target_pairs={{0,8},{8,16},{16,24},{24,32},{32,40},{40,48},{48,56},{56,64},{64,7... | collective-permute-start | bytes 294920 | tf_op jit(solution)/shard_map/while/body/eval_jaxpr/ppermute | solution.py:20
  562.2 28.9 %collective-permute-start = (f32[32,768]{1,0:T(8,128)S(1)}, f32[32,768]{1,0:T(8,128)S(1)}, u32[]{:S(2)}, u32[]{:S(2)}) collective-permute-start(f32[32,768]{1,0:T(8,128)S(1)} %copy.212), channel_id=1, source_target_pairs={{0,8},{8,16},{16,24},{24,32},{32,40},{40,48},{48,56},{56,64},{64,7... | collective-permute-start | bytes 294920 | tf_op jit(solution)/shard_map/while/body/eval_jaxpr/ppermute | solution.py:20
  591.8 28.9 %collective-permute-start = (f32[32,768]{1,0:T(8,128)S(1)}, f32[32,768]{1,0:T(8,128)S(1)}, u32[]{:S(2)}, u32[]{:S(2)}) collective-permute-start(f32[32,768]{1,0:T(8,128)S(1)} %copy.212), channel_id=1, source_target_pairs={{0,8},{8,16},{16,24},{24,32},{32,40},{40,48},{48,56},{56,64},{64,7... | collective-permute-start | bytes 294920 | tf_op jit(solution)/shard_map/while/body/eval_jaxpr/ppermute | solution.py:20
  621.4 28.9 %collective-permute-start = (f32[32,768]{1,0:T(8,128)S(1)}, f32[32,768]{1,0:T(8,128)S(1)}, u32[]{:S(2)}, u32[]{:S(2)}) collective-permute-start(f32[32,768]{1,0:T(8,128)S(1)} %copy.212), channel_id=1, source_target_pairs={{0,8},{8,16},{16,24},{24,32},{32,40},{40,48},{48,56},{56,64},{64,7... | collective-permute-start | bytes 294920 | tf_op jit(solution)/shard_map/while/body/eval_jaxpr/ppermute | solution.py:20
  651.1 28.9 %collective-permute-start = (f32[32,768]{1,0:T(8,128)S(1)}, f32[32,768]{1,0:T(8,128)S(1)}, u32[]{:S(2)}, u32[]{:S(2)}) collective-permute-start(f32[32,768]{1,0:T(8,128)S(1)} %copy.212), channel_id=1, source_target_pairs={{0,8},{8,16},{16,24},{24,32},{32,40},{40,48},{48,56},{56,64},{64,7... | collective-permute-start | bytes 294920 | tf_op jit(solution)/shard_map/while/body/eval_jaxpr/ppermute | solution.py:20
  680.7 28.9 %collective-permute-start = (f32[32,768]{1,0:T(8,128)S(1)}, f32[32,768]{1,0:T(8,128)S(1)}, u32[]{:S(2)}, u32[]{:S(2)}) collective-permute-start(f32[32,768]{1,0:T(8,128)S(1)} %copy.212), channel_id=1, source_target_pairs={{0,8},{8,16},{16,24},{24,32},{32,40},{40,48},{48,56},{56,64},{64,7... | collective-permute-start | bytes 294920 | tf_op jit(solution)/shard_map/while/body/eval_jaxpr/ppermute | solution.py:20
  710.3 28.9 %collective-permute-start = (f32[32,768]{1,0:T(8,128)S(1)}, f32[32,768]{1,0:T(8,128)S(1)}, u32[]{:S(2)}, u32[]{:S(2)}) collective-permute-start(f32[32,768]{1,0:T(8,128)S(1)} %copy.212), channel_id=1, source_target_pairs={{0,8},{8,16},{16,24},{24,32},{32,40},{40,48},{48,56},{56,64},{64,7... | collective-permute-start | bytes 294920 | tf_op jit(solution)/shard_map/while/body/eval_jaxpr/ppermute | solution.py:20
  739.9 28.9 %collective-permute-start = (f32[32,768]{1,0:T(8,128)S(1)}, f32[32,768]{1,0:T(8,128)S(1)}, u32[]{:S(2)}, u32[]{:S(2)}) collective-permute-start(f32[32,768]{1,0:T(8,128)S(1)} %copy.212), channel_id=1, source_target_pairs={{0,8},{8,16},{16,24},{24,32},{32,40},{40,48},{48,56},{56,64},{64,7... | collective-permute-start | bytes 294920 | tf_op jit(solution)/shard_map/while/body/eval_jaxpr/ppermute | solution.py:20
  769.5 28.9 %collective-permute-start = (f32[32,768]{1,0:T(8,128)S(1)}, f32[32,768]{1,0:T(8,128)S(1)}, u32[]{:S(2)}, u32[]{:S(2)}) collective-permute-start(f32[32,768]{1,0:T(8,128)S(1)} %copy.212), channel_id=1, source_target_pairs={{0,8},{8,16},{16,24},{24,32},{32,40},{40,48},{48,56},{56,64},{64,7... | collective-permute-start | bytes 294920 | tf_op jit(solution)/shard_map/while/body/eval_jaxpr/ppermute | solution.py:20
  848.5 25.0 %collective-permute-start.5 = (f32[32]{0:T(128)}, f32[32]{0:T(128)}, u32[]{:S(2)}, u32[]{:S(2)}) collective-permute-start(f32[32]{0:T(128)} %copy.244), channel_id=1, source_target_pairs={{0,8},{8,16},{16,24},{24,32},{32,40},{40,48},{48,56},{56,64},{64,7... | collective-permute-start | bytes 392 | tf_op jit(solution)/shard_map/while/body/eval_jaxpr/ppermute | solution.py:20
  881.6 25.0 %collective-permute-start.5 = (f32[32]{0:T(128)}, f32[32]{0:T(128)}, u32[]{:S(2)}, u32[]{:S(2)}) collective-permute-start(f32[32]{0:T(128)} %copy.244), channel_id=1, source_target_pairs={{0,8},{8,16},{16,24},{24,32},{32,40},{40,48},{48,56},{56,64},{64,7... | collective-permute-start | bytes 392 | tf_op jit(solution)/shard_map/while/body/eval_jaxpr/ppermute | solution.py:20
  914.8 25.0 %collective-permute-start.5 = (f32[32]{0:T(128)}, f32[32]{0:T(128)}, u32[]{:S(2)}, u32[]{:S(2)}) collective-permute-start(f32[32]{0:T(128)} %copy.244), channel_id=1, source_target_pairs={{0,8},{8,16},{16,24},{24,32},{32,40},{40,48},{48,56},{56,64},{64,7... | collective-permute-start | bytes 392 | tf_op jit(solution)/shard_map/while/body/eval_jaxpr/ppermute | solution.py:20
  948.0 25.0 %collective-permute-start.5 = (f32[32]{0:T(128)}, f32[32]{0:T(128)}, u32[]{:S(2)}, u32[]{:S(2)}) collective-permute-start(f32[32]{0:T(128)} %copy.244), channel_id=1, source_target_pairs={{0,8},{8,16},{16,24},{24,32},{32,40},{40,48},{48,56},{56,64},{64,7... | collective-permute-start | bytes 392 | tf_op jit(solution)/shard_map/while/body/eval_jaxpr/ppermute | solution.py:20
  981.2 25.0 %collective-permute-start.5 = (f32[32]{0:T(128)}, f32[32]{0:T(128)}, u32[]{:S(2)}, u32[]{:S(2)}) collective-permute-start(f32[32]{0:T(128)} %copy.244), channel_id=1, source_target_pairs={{0,8},{8,16},{16,24},{24,32},{32,40},{40,48},{48,56},{56,64},{64,7... | collective-permute-start | bytes 392 | tf_op jit(solution)/shard_map/while/body/eval_jaxpr/ppermute | solution.py:20
  1014.4 25.0 %collective-permute-start.5 = (f32[32]{0:T(128)}, f32[32]{0:T(128)}, u32[]{:S(2)}, u32[]{:S(2)}) collective-permute-start(f32[32]{0:T(128)} %copy.244), channel_id=1, source_target_pairs={{0,8},{8,16},{16,24},{24,32},{32,40},{40,48},{48,56},{56,64},{64,7... | collective-permute-start | bytes 392 | tf_op jit(solution)/shard_map/while/body/eval_jaxpr/ppermute | solution.py:20
  1047.6 25.0 %collective-permute-start.5 = (f32[32]{0:T(128)}, f32[32]{0:T(128)}, u32[]{:S(2)}, u32[]{:S(2)}) collective-permute-start(f32[32]{0:T(128)} %copy.244), channel_id=1, source_target_pairs={{0,8},{8,16},{16,24},{24,32},{32,40},{40,48},{48,56},{56,64},{64,7... | collective-permute-start | bytes 392 | tf_op jit(solution)/shard_map/while/body/eval_jaxpr/ppermute | solution.py:20
  1080.8 25.0 %collective-permute-start.5 = (f32[32]{0:T(128)}, f32[32]{0:T(128)}, u32[]{:S(2)}, u32[]{:S(2)}) collective-permute-start(f32[32]{0:T(128)} %copy.244), channel_id=1, source_target_pairs={{0,8},{8,16},{16,24},{24,32},{32,40},{40,48},{48,56},{56,64},{64,7... | collective-permute-start | bytes 392 | tf_op jit(solution)/shard_map/while/body/eval_jaxpr/ppermute | solution.py:20
  1113.9 25.0 %collective-permute-start.5 = (f32[32]{0:T(128)}, f32[32]{0:T(128)}, u32[]{:S(2)}, u32[]{:S(2)}) collective-permute-start(f32[32]{0:T(128)} %copy.244), channel_id=1, source_target_pairs={{0,8},{8,16},{16,24},{24,32},{32,40},{40,48},{48,56},{56,64},{64,7... | collective-permute-start | bytes 392 | tf_op jit(solution)/shard_map/while/body/eval_jaxpr/ppermute | solution.py:20
  1147.1 25.0 %collective-permute-start.5 = (f32[32]{0:T(128)}, f32[32]{0:T(128)}, u32[]{:S(2)}, u32[]{:S(2)}) collective-permute-start(f32[32]{0:T(128)} %copy.244), channel_id=1, source_target_pairs={{0,8},{8,16},{16,24},{24,32},{32,40},{40,48},{48,56},{56,64},{64,7... | collective-permute-start | bytes 392 | tf_op jit(solution)/shard_map/while/body/eval_jaxpr/ppermute | solution.py:20
  1180.3 25.0 %collective-permute-start.5 = (f32[32]{0:T(128)}, f32[32]{0:T(128)}, u32[]{:S(2)}, u32[]{:S(2)}) collective-permute-start(f32[32]{0:T(128)} %copy.244), channel_id=1, source_target_pairs={{0,8},{8,16},{16,24},{24,32},{32,40},{40,48},{48,56},{56,64},{64,7... | collective-permute-start | bytes 392 | tf_op jit(solution)/shard_map/while/body/eval_jaxpr/ppermute | solution.py:20
  1213.5 25.0 %collective-permute-start.5 = (f32[32]{0:T(128)}, f32[32]{0:T(128)}, u32[]{:S(2)}, u32[]{:S(2)}) collective-permute-start(f32[32]{0:T(128)} %copy.244), channel_id=1, source_target_pairs={{0,8},{8,16},{16,24},{24,32},{32,40},{40,48},{48,56},{56,64},{64,7... | collective-permute-start | bytes 392 | tf_op jit(solution)/shard_map/while/body/eval_jaxpr/ppermute | solution.py:20
  1246.7 25.0 %collective-permute-start.5 = (f32[32]{0:T(128)}, f32[32]{0:T(128)}, u32[]{:S(2)}, u32[]{:S(2)}) collective-permute-start(f32[32]{0:T(128)} %copy.244), channel_id=1, source_target_pairs={{0,8},{8,16},{16,24},{24,32},{32,40},{40,48},{48,56},{56,64},{64,7... | collective-permute-start | bytes 392 | tf_op jit(solution)/shard_map/while/body/eval_jaxpr/ppermute | solution.py:20
  1279.9 25.0 %collective-permute-start.5 = (f32[32]{0:T(128)}, f32[32]{0:T(128)}, u32[]{:S(2)}, u32[]{:S(2)}) collective-permute-start(f32[32]{0:T(128)} %copy.244), channel_id=1, source_target_pairs={{0,8},{8,16},{16,24},{24,32},{32,40},{40,48},{48,56},{56,64},{64,7... | collective-permute-start | bytes 392 | tf_op jit(solution)/shard_map/while/body/eval_jaxpr/ppermute | solution.py:20
  1313.1 25.0 %collective-permute-start.5 = (f32[32]{0:T(128)}, f32[32]{0:T(128)}, u32[]{:S(2)}, u32[]{:S(2)}) collective-permute-start(f32[32]{0:T(128)} %copy.244), channel_id=1, source_target_pairs={{0,8},{8,16},{16,24},{24,32},{32,40},{40,48},{48,56},{56,64},{64,7... | collective-permute-start | bytes 392 | tf_op jit(solution)/shard_map/while/body/eval_jaxpr/ppermute | solution.py:20
  1345.7 1057.7 %reduce-scatter.10.cloned.1.call-start = ((), (), s32[]{:S(2)}) async-start(), calls=%async_computation.4 | async-start | bytes 9510912 | tf_op jit(solution)/shard_map/reduce_scatter | solution.py:380
  1868.1 26.1 %collective-permute-start.64 = (f32[8,768]{1,0:T(8,128)S(1)}, f32[8,768]{1,0:T(8,128)S(1)}, u32[]{:S(2)}, u32[]{:S(2)}) collective-permute-start(f32[8,768]{1,0:T(8,128)S(1)} %get-tuple-element.657), channel_id=1, source_target_pairs={{0,25},{1,26},{2,27},{3,28},{4,29},{5,30},{6,31},{7,32},{8,33},{9,... | collective-permute-start | bytes 73736
  1869.4 26.1 %collective-permute-start.63 = (f32[8,768]{1,0:T(8,128)S(1)}, f32[8,768]{1,0:T(8,128)S(1)}, u32[]{:S(2)}, u32[]{:S(2)}) collective-permute-start(f32[8,768]{1,0:T(8,128)S(1)} %get-tuple-element.657), channel_id=1, source_target_pairs={{0,24},{1,25},{2,26},{3,27},{4,28},{5,29},{6,30},{7,31},{8,32},{9,... | collective-permute-start | bytes 73736
  1870.7 28.0 %collective-permute-start.62 = (f32[8,768]{1,0:T(8,128)S(1)}, f32[8,768]{1,0:T(8,128)S(1)}, u32[]{:S(2)}, u32[]{:S(2)}) collective-permute-start(f32[8,768]{1,0:T(8,128)S(1)} %get-tuple-element.657), channel_id=1, source_target_pairs={{0,23},{1,24},{2,25},{3,26},{4,27},{5,28},{6,29},{7,30},{8,31},{9,... | collective-permute-start | bytes 73736
  1998.9 29.7 %collective-permute-start.20 = (f32[8,2304]{1,0:T(8,128)S(1)}, f32[8,2304]{1,0:T(8,128)}, u32[]{:S(2)}, u32[]{:S(2)}) collective-permute-start(f32[8,2304]{1,0:T(8,128)S(1)} %get-tuple-element.656), channel_id=1, source_target_pairs={{0,13},{1,14},{2,15},{3,16},{4,17},{5,18},{6,19},{7,20},{8,21},{9,... | collective-permute-start | bytes 221192
  2003.2 28.8 %collective-permute-start.19 = (f32[8,2304]{1,0:T(8,128)S(1)}, f32[8,2304]{1,0:T(8,128)}, u32[]{:S(2)}, u32[]{:S(2)}) collective-permute-start(f32[8,2304]{1,0:T(8,128)S(1)} %get-tuple-element.656), channel_id=1, source_target_pairs={{0,12},{1,13},{2,14},{3,15},{4,16},{5,17},{6,18},{7,19},{8,20},{9,... | collective-permute-start | bytes 221192
  2006.6 29.3 %collective-permute-start.18 = (f32[8,2304]{1,0:T(8,128)S(1)}, f32[8,2304]{1,0:T(8,128)}, u32[]{:S(2)}, u32[]{:S(2)}) collective-permute-start(f32[8,2304]{1,0:T(8,128)S(1)} %get-tuple-element.656), channel_id=1, source_target_pairs={{0,11},{1,12},{2,13},{3,14},{4,15},{5,16},{6,17},{7,18},{8,19},{9,... | collective-permute-start | bytes 221192
  2010.5 29.8 %collective-permute-start.17 = (f32[8,2304]{1,0:T(8,128)S(1)}, f32[8,2304]{1,0:T(8,128)}, u32[]{:S(2)}, u32[]{:S(2)}) collective-permute-start(f32[8,2304]{1,0:T(8,128)S(1)} %get-tuple-element.656), channel_id=1, source_target_pairs={{0,10},{1,11},{2,12},{3,13},{4,14},{5,15},{6,16},{7,17},{8,18},{9,... | collective-permute-start | bytes 221192
  2012.5 31.1 %collective-permute-start.16 = (f32[8,2304]{1,0:T(8,128)S(1)}, f32[8,2304]{1,0:T(8,128)}, u32[]{:S(2)}, u32[]{:S(2)}) collective-permute-start(f32[8,2304]{1,0:T(8,128)S(1)} %get-tuple-element.656), channel_id=1, source_target_pairs={{0,9},{1,10},{2,11},{3,12},{4,13},{5,14},{6,15},{7,16},{8,17},{9,1... | collective-permute-start | bytes 221192
  2024.8 365.8 %all-to-all-start.2 = ((bf16[128,8,768]{2,1,0:T(8,128)(2,1)}), bf16[128,8,768]{2,1,0:T(8,128)(2,1)S(1)}, u32[]{:S(2)}, u32[]{:S(2)}) async-start(bf16[128,8,768]{2,1,0:T(8,128)(2,1)} %bitcast.35), calls=%async_computation.2 | async-start | bytes 3145728 | tf_op jit(solution)/shard_map/all_to_all | solution.py:391
  2028.6 25.1 %collective-permute-start.15 = (f32[8,2304]{1,0:T(8,128)S(1)}, f32[8,2304]{1,0:T(8,128)S(1)}, u32[]{:S(2)}, u32[]{:S(2)}) collective-permute-start(f32[8,2304]{1,0:T(8,128)S(1)} %get-tuple-element.656), channel_id=1, source_target_pairs={{0,8},{1,9},{2,10},{3,11},{4,12},{5,13},{6,14},{7,15},{8,16},{9,17... | collective-permute-start | bytes 221192
  2059.5 27.2 %collective-permute-start.102 = (f32[8,3072]{1,0:T(8,128)S(1)}, f32[8,3072]{1,0:T(8,128)S(1)}, u32[]{:S(2)}, u32[]{:S(2)}) collective-permute-start(f32[8,3072]{1,0:T(8,128)S(1)} %get-tuple-element.658), channel_id=1, source_target_pairs={{0,31},{1,32},{2,33},{3,34},{4,35},{5,36},{6,37},{7,38},{8,39},{9,... | collective-permute-start | bytes 294920
  2090.6 89.8 %collective-permute-start.96 = (f32[8,3072]{1,0:T(8,128)S(1)}, f32[8,3072]{1,0:T(8,128)S(1)}, u32[]{:S(2)}, u32[]{:S(2)}) collective-permute-start(f32[8,3072]{1,0:T(8,128)S(1)} %get-tuple-element.658), channel_id=1, source_target_pairs={{0,25},{1,26},{2,27},{3,28},{4,29},{5,30},{6,31},{7,32},{8,33},{9,... | collective-permute-start | bytes 294920
  2092.0 94.1 %collective-permute-start.95 = (f32[8,3072]{1,0:T(8,128)S(1)}, f32[8,3072]{1,0:T(8,128)S(1)}, u32[]{:S(2)}, u32[]{:S(2)}) collective-permute-start(f32[8,3072]{1,0:T(8,128)S(1)} %get-tuple-element.658), channel_id=1, source_target_pairs={{0,24},{1,25},{2,26},{3,27},{4,28},{5,29},{6,30},{7,31},{8,32},{9,... | collective-permute-start | bytes 294920
  2093.3 97.9 %collective-permute-start.94 = (f32[8,3072]{1,0:T(8,128)S(1)}, f32[8,3072]{1,0:T(8,128)S(1)}, u32[]{:S(2)}, u32[]{:S(2)}) collective-permute-start(f32[8,3072]{1,0:T(8,128)S(1)} %get-tuple-element.658), channel_id=1, source_target_pairs={{0,23},{1,24},{2,25},{3,26},{4,27},{5,28},{6,29},{7,30},{8,31},{9,... | collective-permute-start | bytes 294920
  2101.1 94.5 %collective-permute-start.93 = (f32[8,3072]{1,0:T(8,128)S(1)}, f32[8,3072]{1,0:T(8,128)S(1)}, u32[]{:S(2)}, u32[]{:S(2)}) collective-permute-start(f32[8,3072]{1,0:T(8,128)S(1)} %get-tuple-element.658), channel_id=1, source_target_pairs={{0,22},{1,23},{2,24},{3,25},{4,26},{5,27},{6,28},{7,29},{8,30},{9,... | collective-permute-start | bytes 294920
  2104.1 93.4 %collective-permute-start.92 = (f32[8,3072]{1,0:T(8,128)S(1)}, f32[8,3072]{1,0:T(8,128)S(1)}, u32[]{:S(2)}, u32[]{:S(2)}) collective-permute-start(f32[8,3072]{1,0:T(8,128)S(1)} %get-tuple-element.658), channel_id=1, source_target_pairs={{0,21},{1,22},{2,23},{3,24},{4,25},{5,26},{6,27},{7,28},{8,29},{9,... | collective-permute-start | bytes 294920
  2203.4 46.9 %collective-permute-start.86 = (f32[8,3072]{1,0:T(8,128)S(1)}, f32[8,3072]{1,0:T(8,128)}, u32[]{:S(2)}, u32[]{:S(2)}) collective-permute-start(f32[8,3072]{1,0:T(8,128)S(1)} %get-tuple-element.658), channel_id=1, source_target_pairs={{0,15},{1,16},{2,17},{3,18},{4,19},{5,20},{6,21},{7,22},{8,23},{9,... | collective-permute-start | bytes 294920
  2208.3 44.0 %collective-permute-start.85 = (f32[8,3072]{1,0:T(8,128)S(1)}, f32[8,3072]{1,0:T(8,128)}, u32[]{:S(2)}, u32[]{:S(2)}) collective-permute-start(f32[8,3072]{1,0:T(8,128)S(1)} %get-tuple-element.658), channel_id=1, source_target_pairs={{0,14},{1,15},{2,16},{3,17},{4,18},{5,19},{6,20},{7,21},{8,22},{9,... | collective-permute-start | bytes 294920
  2212.1 43.0 %collective-permute-start.84 = (f32[8,3072]{1,0:T(8,128)S(1)}, f32[8,3072]{1,0:T(8,128)}, u32[]{:S(2)}, u32[]{:S(2)}) collective-permute-start(f32[8,3072]{1,0:T(8,128)S(1)} %get-tuple-element.658), channel_id=1, source_target_pairs={{0,13},{1,14},{2,15},{3,16},{4,17},{5,18},{6,19},{7,20},{8,21},{9,... | collective-permute-start | bytes 294920
  2215.1 42.6 %collective-permute-start.83 = (f32[8,3072]{1,0:T(8,128)S(1)}, f32[8,3072]{1,0:T(8,128)}, u32[]{:S(2)}, u32[]{:S(2)}) collective-permute-start(f32[8,3072]{1,0:T(8,128)S(1)} %get-tuple-element.658), channel_id=1, source_target_pairs={{0,12},{1,13},{2,14},{3,15},{4,16},{5,17},{6,18},{7,19},{8,20},{9,... | collective-permute-start | bytes 294920
  2219.3 40.3 %collective-permute-start.82 = (f32[8,3072]{1,0:T(8,128)S(1)}, f32[8,3072]{1,0:T(8,128)}, u32[]{:S(2)}, u32[]{:S(2)}) collective-permute-start(f32[8,3072]{1,0:T(8,128)S(1)} %get-tuple-element.658), channel_id=1, source_target_pairs={{0,11},{1,12},{2,13},{3,14},{4,15},{5,16},{6,17},{7,18},{8,19},{9,... | collective-permute-start | bytes 294920
  2250.3 67.6 %collective-permute-start.81 = (f32[8,3072]{1,0:T(8,128)S(1)}, f32[8,3072]{1,0:T(8,128)}, u32[]{:S(2)}, u32[]{:S(2)}) collective-permute-start(f32[8,3072]{1,0:T(8,128)S(1)} %get-tuple-element.658), channel_id=1, source_target_pairs={{0,10},{1,11},{2,12},{3,13},{4,14},{5,15},{6,16},{7,17},{8,18},{9,... | collective-permute-start | bytes 294920
  2252.2 67.7 %collective-permute-start.80 = (f32[8,3072]{1,0:T(8,128)S(1)}, f32[8,3072]{1,0:T(8,128)}, u32[]{:S(2)}, u32[]{:S(2)}) collective-permute-start(f32[8,3072]{1,0:T(8,128)S(1)} %get-tuple-element.658), channel_id=1, source_target_pairs={{0,9},{1,10},{2,11},{3,12},{4,13},{5,14},{6,15},{7,16},{8,17},{9,1... | collective-permute-start | bytes 294920
  2255.1 68.0 %collective-permute-start.79 = (f32[8,3072]{1,0:T(8,128)S(1)}, f32[8,3072]{1,0:T(8,128)}, u32[]{:S(2)}, u32[]{:S(2)}) collective-permute-start(f32[8,3072]{1,0:T(8,128)S(1)} %get-tuple-element.658), channel_id=1, source_target_pairs={{0,8},{1,9},{2,10},{3,11},{4,12},{5,13},{6,14},{7,15},{8,16},{9,17... | collective-permute-start | bytes 294920
  2257.7 68.8 %collective-permute-start.78 = (f32[8,3072]{1,0:T(8,128)S(1)}, f32[8,3072]{1,0:T(8,128)}, u32[]{:S(2)}, u32[]{:S(2)}) collective-permute-start(f32[8,3072]{1,0:T(8,128)S(1)} %get-tuple-element.658), channel_id=1, source_target_pairs={{0,7},{1,8},{2,9},{3,10},{4,11},{5,12},{6,13},{7,14},{8,15},{9,16}... | collective-permute-start | bytes 294920
  2259.6 68.9 %collective-permute-start.77 = (f32[8,3072]{1,0:T(8,128)S(1)}, f32[8,3072]{1,0:T(8,128)}, u32[]{:S(2)}, u32[]{:S(2)}) collective-permute-start(f32[8,3072]{1,0:T(8,128)S(1)} %get-tuple-element.658), channel_id=1, source_target_pairs={{0,6},{1,7},{2,8},{3,9},{4,10},{5,11},{6,12},{7,13},{8,14},{9,15},... | collective-permute-start | bytes 294920
  (304 other events, 8480.8 us)
Sparse Core Ops, SparseCore 0:
  11.5 81.8 all-gather.13
  96.9 62.6 all-gather.15
  163.3 68.1 all-gather.17
  234.4 64.5 all-gather.19
  1345.9 52.1 all-reduce.16
  1414.7 221.9 reduce-scatter.9
where the time goes:
time: 2430 us; the launch traced here: 2410 us
  starting transfers between devices  924 us (38%)
  blocking collectives  575 us (24%)
  waiting for transfers between devices  325 us (13%)
  local copies, waits for them, and re-layouts  319 us (13%)
  matrix products  151 us (6%)
  other arithmetic  74.6 us (3%)
    ppermute x128, starting transfers between devices, passed_along(): lax.ppermute(value, axis, [(i, (i + by) % devices) for i in range(devices)])  616 us
    unnamed x4, blocking collectives  473 us
    unnamed x97, starting transfers between devices  288 us
    ppermute x128, waiting for transfers between devices, passed_along(): lax.ppermute(value, axis, [(i, (i + by) % devices) for i in range(devices)])  198 us
    unnamed x300, local copies, waits for them, and re-layouts  162 us
    unnamed x103, waiting for transfers between devices  57.3 us
    all_gather x1, blocking collectives, fetch(): lax.all_gather(biases[layer_at], ('wide', 'narrow'), axis=1, tiled=True)  49.2 us
    while x80, local copies, waits for them, and re-layouts  49 us
  transfers between devices with their start and end apart: 233, of which 39 were waited for; matrix products, arithmetic and copies ran while one was open for 35% of the time, Pallas kernels for 0%

commit v1 on v0

--- a/solution.py
+++ b/solution.py
@@ -1,6 +1,10 @@
+import functools
+
 import jax
 import jax.numpy as jnp
 from jax import lax
+from jax.experimental import pallas as pl
+from jax.experimental.pallas import tpu as pltpu
 from jax.sharding import PartitionSpec as P
 
 HEAD_DIM = 64
@@ -15,19 +19,320 @@
 far_low = -1e30
 
 
-def passed_along(value, axis, by):
-    devices = lax.axis_size(axis)
-    return lax.ppermute(value, axis, [(i, (i + by) % devices) for i in range(devices)])
-
-
-def joined(value, axis, combine):
-    everything = jax.tree.map(lambda part: lax.all_gather(part, axis), value)
-    leading = jax.tree.map(lambda part: part[0], everything)
-
-    def hop(k, so_far):
-        return combine(so_far, jax.tree.map(lambda part: part[k], everything))
-
-    return lax.fori_loop(1, lax.axis_size(axis), hop, leading)
+MESH = pl.DeviceIdType.MESH
+RING = 4
+ORDERS = ((0, 1, 2), (1, 2, 0), (2, 0, 1))
+UNIT = 48
+
+
+def where_am_i():
+    wide = lax.axis_index("wide")
+    narrow = lax.axis_index("narrow")
+    return [narrow // 2, wide // RING, wide % RING], narrow % 2
+
+
+def device_at(spot, core):
+    return (spot[1] * RING + spot[2], spot[0] * 2 + core)
+
+
+def moved(spot, dim, by):
+    there = list(spot)
+    there[dim] = (spot[dim] + by) % RING
+    return there
+
+
+def block_of(ref, part, core, order, spans):
+    return ref.at[(part, core, order) + tuple(pl.ds(*spans[d]) for d in range(3))]
+
+
+def greet(spot, core):
+    barrier = pltpu.get_barrier_semaphore()
+    others = [(moved(spot, d, by), core) for d in range(3) for by in (1, -1)] + [(spot, 1 - core)]
+    for there, c in others:
+        pl.semaphore_signal(barrier, inc=1, device_id=device_at(there, c), device_id_type=MESH)
+    pl.semaphore_wait(barrier, len(others))
+
+
+def gather_kernel(rounds, own_ref, out_ref, send_sem, recv_sem, local_sem):
+    spot, core = where_am_i()
+    sent = []
+    greet(spot, core)
+
+    def push(r, o, event, spans, there, c=None, src=None):
+        c = core if c is None else c
+        dst = block_of(out_ref, r, core, o, spans)
+        copy = pltpu.make_async_remote_copy(
+            src_ref=dst if src is None else src,
+            dst_ref=dst,
+            send_sem=send_sem.at[r, o, event],
+            recv_sem=recv_sem.at[r, o, event],
+            device_id=device_at(there, c),
+            device_id_type=MESH,
+        )
+        copy.start()
+        sent.append(copy)
+
+    def landed(r, o, event, spans, c=None):
+        c = core if c is None else c
+        dst = block_of(out_ref, r, c, o, spans)
+        pltpu.make_async_copy(dst, dst, recv_sem.at[r, o, event]).wait()
+
+    def spans_for(o, phase, at, half=None):
+        order = ORDERS[o]
+        spans = {}
+        for k, d in enumerate(order):
+            if k < phase:
+                spans[d] = (0, RING)
+            elif k == phase:
+                spans[d] = (at, 1)
+            else:
+                spans[d] = (spot[d], 1)
+        if half is not None:
+            spans[order[0]] = (2 * half, 2)
+        return spans
+
+    every = [(r, o) for r in range(rounds) for o in range(3)]
+    locals_ = []
+    for r, o in every:
+        d = ORDERS[o][0]
+        here = spans_for(o, 0, spot[d])
+        mine = block_of(out_ref, r, core, o, here)
+        src = own_ref.at[r, o]
+        copy = pltpu.make_async_copy(src, mine, local_sem.at[r, o])
+        copy.start()
+        locals_.append(copy)
+        push(r, o, 0, here, moved(spot, d, 1), src=src)
+        push(r, o, 1, here, moved(spot, d, -1), src=src)
+    for r, o in every:
+        d = ORDERS[o][0]
+        before = spans_for(o, 0, (spot[d] - 1) % RING)
+        landed(r, o, 0, before)
+        push(r, o, 2, before, moved(spot, d, 1))
+
+    def spread(r, o, phase):
+        d = ORDERS[o][phase]
+        here = spans_for(o, phase, spot[d])
+        first = 3 + 4 * (phase - 1)
+        push(r, o, first, here, moved(spot, d, 1))
+        push(r, o, first + 1, here, moved(spot, d, -1))
+
+    def share(r, o, event, spans):
+        push(r, o, event, spans, spot, 1 - core)
+
+    def relay(r, o, phase):
+        d = ORDERS[o][phase]
+        first = 3 + 4 * (phase - 1)
+        left, right = (spot[d] - 1) % RING, (spot[d] + 1) % RING
+        landed(r, o, first, spans_for(o, phase, left))
+        push(r, o, first + 2, spans_for(o, phase, left, 0), moved(spot, d, 1))
+        landed(r, o, first + 1, spans_for(o, phase, right))
+        push(r, o, first + 3, spans_for(o, phase, right, 1), moved(spot, d, -1))
+        share(r, o, 11 + 3 * (phase - 1) + 1, spans_for(o, phase, left))
+        share(r, o, 11 + 3 * (phase - 1) + 2, spans_for(o, phase, right))
+
+    def finish(r, o, phase):
+        d = ORDERS[o][phase]
+        first = 3 + 4 * (phase - 1)
+        across = (spot[d] + 2) % RING
+        landed(r, o, first + 2, spans_for(o, phase, across, 0))
+        landed(r, o, first + 3, spans_for(o, phase, across, 1))
+        share(r, o, 11 + 3 * (phase - 1) + 3, spans_for(o, phase, across))
+
+    for (r, o), copy in zip(every, locals_):
+        d = ORDERS[o][0]
+        landed(r, o, 1, spans_for(o, 0, (spot[d] + 1) % RING))
+        landed(r, o, 2, spans_for(o, 0, (spot[d] + 2) % RING))
+        copy.wait()
+        spread(r, o, 1)
+        share(r, o, 11, spans_for(o, 1, spot[ORDERS[o][1]]))
+    for r, o in every:
+        relay(r, o, 1)
+    for r, o in every:
+        finish(r, o, 1)
+        spread(r, o, 2)
+    for r in range(rounds):
+        for o in range(3):
+            relay(r, o, 2)
+        for o in range(3):
+            finish(r, o, 2)
+    for r, o in every:
+        for phase in (1, 2):
+            d = ORDERS[o][phase]
+            if phase == 1:
+                landed(r, o, 11, spans_for(o, 1, spot[d]), 1 - core)
+            base = 11 + 3 * (phase - 1)
+            landed(r, o, base + 1, spans_for(o, phase, (spot[d] - 1) % RING), 1 - core)
+            landed(r, o, base + 2, spans_for(o, phase, (spot[d] + 1) % RING), 1 - core)
+            landed(r, o, base + 3, spans_for(o, phase, (spot[d] + 2) % RING), 1 - core)
+    for copy in sent:
+        copy.wait_send()
+
+
+def gather_units(own, collective_id, name, space=pl.ANY):
+    rounds, _, rows, _ = own.shape
+    return pl.pallas_call(
+        functools.partial(gather_kernel, rounds),
+        out_shape=jax.ShapeDtypeStruct((rounds, 2, 3, RING, RING, RING, rows, 128), own.dtype),
+        in_specs=[pl.BlockSpec(memory_space=pltpu.VMEM)],
+        out_specs=pl.BlockSpec(memory_space=space),
+        scratch_shapes=[
+            pltpu.SemaphoreType.DMA((rounds, 3, 18)),
+            pltpu.SemaphoreType.DMA((rounds, 3, 18)),
+            pltpu.SemaphoreType.DMA((rounds, 3)),
+        ],
+        compiler_params=pltpu.CompilerParams(
+            collective_id=collective_id,
+            has_side_effects=True,
+            vmem_limit_bytes=60 * 1024 * 1024,
+        ),
+        name=name,
+    )(own.reshape(rounds, 3, 1, 1, 1, rows, 128))
+
+
+def reduce_kernel(part_ref, out_ref, d2d, *rest):
+    bufs, (send_sem, recv_sem) = rest[:-2], rest[-2:]
+    spot, core = where_am_i()
+    sent = []
+    greet(spot, core)
+    every = [(r, o) for r in range(3) for o in range(3)]
+
+    def copy_to(src, dst, r, o, event, there, c):
+        copy = pltpu.make_async_remote_copy(
+            src_ref=src,
+            dst_ref=dst,
+            send_sem=send_sem.at[r, o, event],
+            recv_sem=recv_sem.at[r, o, event],
+            device_id=device_at(there, c),
+            device_id_type=MESH,
+        )
+        copy.start()
+        sent.append(copy)
+
+    def landed(dst, r, o, event):
+        pltpu.make_async_copy(dst, dst, recv_sem.at[r, o, event]).wait()
+
+    def spans_for(o, phase, at, half=None):
+        order = ORDERS[o]
+        spans = {}
+        for k, d in enumerate(order):
+            if k < phase:
+                spans[d] = (spot[d], 1)
+            elif k == phase:
+                spans[d] = (at, 1)
+            else:
+                spans[d] = (0, RING)
+        if half is not None:
+            spans[order[phase + 1]] = (2 * half, 2)
+        return spans
+
+    def mine(r, o, spans):
+        return block_of(part_ref, r, core, o, spans)
+
+    def slot(r, o, phase, which):
+        return bufs[(o * 3 + phase) * 2 + which // 2].at[r, which % 2]
+
+    def add_into(into, others):
+        sizes = into.shape[:3]
+        total = sizes[0] * sizes[1] * sizes[2]
+
+        def one(i, _):
+            at = (i // (sizes[1] * sizes[2]), i // sizes[2] % sizes[1], i % sizes[2])
+            value = into[at].astype(jnp.float32)
+            for other in others:
+                value = value + other[at].astype(jnp.float32)
+            into[at] = value.astype(jnp.bfloat16)
+            return 0
+
+        lax.fori_loop(0, total, one, 0)
+
+    whole = {d: (0, RING) for d in range(3)}
+
+    def first(r, o, phase):
+        d = ORDERS[o][phase]
+        across = (spot[d] + 2) % RING
+        event = 1 + 4 * phase
+        if phase < 2:
+            for half, by in ((0, 1), (1, -1)):
+                copy_to(mine(r, o, spans_for(o, phase, across, half)), slot(r, o, phase, half), r, o, event + half, moved(spot, d, by), core)
+        else:
+            copy_to(mine(r, o, spans_for(o, phase, across)), slot(r, o, phase, 0), r, o, event, moved(spot, d, 1), core)
+
+    def second(r, o, phase):
+        d = ORDERS[o][phase]
+        event = 1 + 4 * phase
+        for half, by in ((0, 1), (1, -1)):
+            at = (spot[d] + by) % RING
+            if phase < 2 or half == 0:
+                view = slot(r, o, phase, half)
+                landed(view, r, o, event + half)
+                add_into(mine(r, o, spans_for(o, phase, at, half if phase < 2 else None)), [view])
+            copy_to(mine(r, o, spans_for(o, phase, at)), slot(r, o, phase, 2 + half), r, o, event + 2 + half, moved(spot, d, by), core)
+
+    def third(r, o, phase):
+        d = ORDERS[o][phase]
+        event = 1 + 4 * phase
+        a, b = slot(r, o, phase, 2), slot(r, o, phase, 3)
+        landed(a, r, o, event + 2)
+        landed(b, r, o, event + 3)
+        here = mine(r, o, spans_for(o, phase, spot[d]))
+        if phase < 2:
+            add_into(here, [a, b])
+        else:
+            total = here[0, 0, 0].astype(jnp.float32) + a[0, 0, 0].astype(jnp.float32)
+            out_ref[r, o] = total + b[0, 0, 0].astype(jnp.float32)
+
+    rounds = (2, 1, 0)
+    for r in rounds:
+        for o in range(3):
+            copy_to(block_of(part_ref, r, 1 - core, o, whole), d2d.at[r, o], r, o, 0, spot, 1 - core)
+    for r in rounds:
+        for o in range(3):
+            landed(d2d.at[r, o], r, o, 0)
+            add_into(mine(r, o, whole), [d2d.at[r, o]])
+            first(r, o, 0)
+    for phase in range(3):
+        for r in rounds:
+            for o in range(3):
+                second(r, o, phase)
+        for r in rounds:
+            for o in range(3):
+                third(r, o, phase)
+                if phase < 2:
+                    first(r, o, phase + 1)
+    for copy in sent:
+        copy.wait_send()
+
+
+def reduce_grads(parts):
+    bf = jnp.bfloat16
+    bufs = []
+    for o in range(3):
+        for phase in range(3):
+            order = ORDERS[o]
+            sizes = [RING] * 3
+            for k in range(phase + 1):
+                sizes[order[k]] = 1
+            half = list(sizes)
+            if phase < 2:
+                half[order[phase + 1]] = 2
+            for s in (half, sizes):
+                bufs.append(pltpu.VMEM((3, 2, *s, UNIT, 128), bf))
+    return pl.pallas_call(
+        reduce_kernel,
+        out_shape=jax.ShapeDtypeStruct((3, 3, UNIT, 128), jnp.float32),
+        in_specs=[pl.BlockSpec(memory_space=pltpu.VMEM)],
+        out_specs=pl.BlockSpec(memory_space=pltpu.VMEM),
+        scratch_shapes=[
+            pltpu.VMEM((3, 3, RING, RING, RING, UNIT, 128), bf),
+            *bufs,
+            pltpu.SemaphoreType.DMA((3, 3, 13)),
+            pltpu.SemaphoreType.DMA((3, 3, 13)),
+        ],
+        compiler_params=pltpu.CompilerParams(
+            collective_id=2, has_side_effects=True, vmem_limit_bytes=62 * 1024 * 1024
+        ),
+        name="reduce_grads",
+    )(parts)
 
 
 def layer_norm(inputs, gain_row, bias_row):
@@ -225,35 +530,54 @@
     return (d_hidden, (d_qkv_w, d_out, d_up, d_down, d_gains, d_biases))
 
 
-def pair_scores(source, block_rows, own_index, block_begin):
-    column_index = block_begin + jnp.arange(block_rows.shape[0])
-    same_pair = (own_index[:, None] == column_index[None, :]).astype(jnp.float32)
-    raw_scores = logit_scale * exact_cols(source, block_rows) - logit_scale * margin * same_pair
-    return (raw_scores, same_pair)
-
-
-def lse_parts(raw_scores, live_pairs, axis_num):
-    masked = jnp.where(live_pairs, raw_scores, far_low)
-    peak_val = jnp.max(masked, axis=axis_num)
-    summed = jnp.sum(
-        jnp.where(live_pairs, jnp.exp(masked - jnp.expand_dims(peak_val, axis_num)), 0.0),
-        axis=axis_num,
-    )
-    return (peak_val, summed)
-
-
-def lse_join(first_part, second_part):
-    peak_val = jnp.maximum(first_part[0], second_part[0])
-    summed = first_part[1] * jnp.exp(first_part[0] - peak_val) + second_part[1] * jnp.exp(
-        second_part[0] - peak_val
-    )
-    return (peak_val, summed)
-
-
-def pair_mix(raw_scores, live_pairs, same_pair, row_lse, col_lse, pair_weight):
-    row_part = jnp.where(live_pairs, jnp.exp(raw_scores - row_lse[:, None]), 0.0)
-    col_part = jnp.where(live_pairs, jnp.exp(raw_scores - col_lse[None, :]), 0.0)
-    return pair_weight * (row_part + col_part) - 2.0 * pair_weight * same_pair
+def own_units(w_qkv, w_out, w_up, w_down, core):
+    first = jnp.concatenate([w_qkv, w_out], axis=1)
+    both = jnp.stack([first, w_up]).reshape(2, 6, 2, 3, RING, 128)
+    out_going = both.transpose(4, 2, 0, 3, 1, 5).reshape(8, 2, 3, 6, 128)
+    rows = lax.all_to_all(out_going, "narrow", split_axis=0, concat_axis=0, tiled=True)
+    units = rows.transpose(1, 2, 0, 3, 4).reshape(2, 3, UNIT, 128)
+    halves = w_down.reshape(24, 2, 3, 128).transpose(1, 2, 0, 3)
+    keep = lax.dynamic_index_in_dim(halves, core, 0, keepdims=False)
+    give = lax.dynamic_index_in_dim(halves, 1 - core, 0, keepdims=False)
+    got = swapped(give)
+    low_rows = jnp.where(core == 0, keep, got)
+    high_rows = jnp.where(core == 0, got, keep)
+    down = jnp.concatenate([low_rows, high_rows], axis=1)
+    return jnp.concatenate([units, down[None]], axis=0)
+
+
+def swapped(value):
+    return lax.ppermute(value, "narrow", [(i, i ^ 1) for i in range(8)])
+
+
+def whole_weights(gathered):
+    first, up = (
+        gathered[r].transpose(3, 4, 5, 0, 1, 2, 6).reshape(768, 3072) for r in range(2)
+    )
+    down = gathered[2].transpose(3, 4, 2, 5, 0, 1, 6).reshape(3072, 768)
+    return first[:, :2304], first[:, 2304:], up, down
+
+
+def as_units(d_qkv, d_out, d_up, d_down):
+    first = jnp.concatenate([d_qkv, d_out], axis=1)
+    shape = (RING, RING, UNIT, 2, 3, RING, 128)
+    parts = [m.reshape(shape).transpose(3, 4, 5, 0, 1, 2, 6) for m in (first, d_up)]
+    down = d_down.reshape(RING, RING, RING, UNIT, 2, 3, 128).transpose(4, 5, 2, 0, 1, 3, 6)
+    return jnp.stack(parts + [down]).astype(jnp.bfloat16)
+
+
+def own_rows(reduced, core):
+    out_going = reduced[:2].reshape(2, 3, 8, 6, 128).transpose(2, 0, 1, 3, 4)
+    rows = lax.all_to_all(out_going, "narrow", split_axis=0, concat_axis=0, tiled=True)
+    rows = rows.reshape(RING, 2, 2, 3, 6, 128).transpose(2, 4, 1, 3, 0, 5).reshape(2, 6, 3072)
+    halves = reduced[2].reshape(3, 2, 24, 128).transpose(1, 0, 2, 3)
+    keep = lax.dynamic_index_in_dim(halves, core, 0, keepdims=False)
+    give = lax.dynamic_index_in_dim(halves, 1 - core, 0, keepdims=False)
+    got = swapped(give)
+    low_cols = jnp.where(core == 0, keep, got)
+    high_cols = jnp.where(core == 0, got, keep)
+    down = jnp.concatenate([low_cols, high_cols]).transpose(1, 0, 2).reshape(24, 768)
+    return rows[0, :, :2304], rows[0, :, 2304:], rows[1], down
 
 
 def shards(token_ids, lengths, groups, table, w_qkv, w_out, w_up, w_down, gains, biases):
@@ -282,107 +606,48 @@
     sent_lengths = lengths.reshape(-1)
     key_ok = jnp.arange(SEQ)[None, :] < sent_lengths[:, None]
 
-    def fetch(layer_at):
-        return (
-            lax.all_gather(w_qkv[layer_at], ("wide", "narrow"), axis=0, tiled=True),
-            lax.all_gather(w_out[layer_at], ("wide", "narrow"), axis=0, tiled=True),
-            lax.all_gather(w_up[layer_at], ("wide", "narrow"), axis=0, tiled=True),
-            lax.all_gather(w_down[layer_at], ("wide", "narrow"), axis=0, tiled=True),
-            lax.all_gather(gains[layer_at], ("wide", "narrow"), axis=1, tiled=True),
-            lax.all_gather(biases[layer_at], ("wide", "narrow"), axis=1, tiled=True),
-        )
-
-    fetched = []
-    layer_at = 0
-    layer_params = fetch(layer_at)
-    fetched.append(layer_params)
+    core = lax.axis_index("narrow") % 2
+    everywhere = ("wide", "narrow")
+    all_groups = lax.all_gather(groups, everywhere, axis=0, tiled=True)
+    vectors = lax.all_gather(
+        jnp.concatenate([gains[0], biases[0]]), everywhere, axis=1, tiled=True
+    )
+    own = own_units(w_qkv[0], w_out[0], w_up[0], w_down[0], core)
+    gathered = gather_units(own, 1, "gather_weights")
+    layer_params = whole_weights(gathered) + (vectors[:2], vectors[2:])
     hidden, saved = layer_forward(hidden, layer_params, key_ok)
-    saves = [saved]
     states = hidden.reshape(sent_count, SEQ, model_width)
     pooled, pool_back = jax.vjp(lambda inner_states: pooling(inner_states, sent_lengths), states)
-    pair_rows = pooled.reshape(pair_count, 2, model_width)
-    source = pair_rows[:, 0]
-    target = pair_rows[:, 1]
-    group_vals = groups.astype(jnp.float32)
-    own_index = rank_at * pair_count + jnp.arange(pair_count)
+    gathered_rows = gather_units(pooled.reshape(1, 3, 16, 128), 3, "gather_pooled")
+    pair_rows = gathered_rows[0].transpose(3, 4, 2, 0, 1, 5, 6).reshape(-1, 2, model_width)
+    source, target = pair_rows[:, 0], pair_rows[:, 1]
     total_pairs = pair_count * device_total
     pair_weight = 1.0 / (2.0 * total_pairs)
     diagonal = logit_scale * jnp.sum(source * target, axis=1) - logit_scale * margin
-    wide_count = lax.axis_size("wide")
-    wide_at = lax.axis_index("wide")
-    narrow_at = lax.axis_index("narrow")
-    home_rows, home_groups = (
-        lax.all_gather(target, "narrow", axis=0, tiled=True),
-        lax.all_gather(group_vals, "narrow", axis=0, tiled=True),
-    )
-    span = home_rows.shape[0]
-
-    def forward_step(carry, cycle_step):
-        block_rows, block_groups, col_peak, col_total, row_peak, row_total = carry
-        block_begin = (wide_at - cycle_step) % wide_count * span
-        raw_scores, same_pair = pair_scores(source, block_rows, own_index, block_begin)
-        live_pairs = group_vals[:, None] == block_groups[None, :]
-        row_peak, row_total = lse_join((row_peak, row_total), lse_parts(raw_scores, live_pairs, 1))
-        col_peak, col_total = lse_join((col_peak, col_total), lse_parts(raw_scores, live_pairs, 0))
-        block_rows, block_groups, col_peak, col_total = passed_along(
-            (block_rows, block_groups, col_peak, col_total), "wide", 1
-        )
-        return ((block_rows, block_groups, col_peak, col_total, row_peak, row_total), None)
-
-    start_carry = (
-        home_rows,
-        home_groups,
-        jnp.full((span,), far_low, jnp.float32),
-        jnp.zeros((span,), jnp.float32),
-        jnp.full((pair_count,), far_low, jnp.float32),
-        jnp.zeros((pair_count,), jnp.float32),
-    )
-    end_carry = lax.scan(forward_step, start_carry, jnp.arange(wide_count))[0]
-    row_lse = end_carry[4] + jnp.log(end_carry[5])
-    col_peak, col_total = joined((end_carry[2], end_carry[3]), "narrow", lse_join)
-    home_lse = col_peak + jnp.log(col_total)
-    own_col = lax.dynamic_slice_in_dim(home_lse, narrow_at * pair_count, pair_count)
-
-    def backward_step(carry, cycle_step):
-        block_rows, block_groups, block_lse, block_grad, source_grad = carry
-        block_begin = (wide_at - cycle_step) % wide_count * span
-        raw_scores, same_pair = pair_scores(source, block_rows, own_index, block_begin)
-        live_pairs = group_vals[:, None] == block_groups[None, :]
-        mix_vals = pair_mix(raw_scores, live_pairs, same_pair, row_lse, block_lse, pair_weight)
-        source_grad = source_grad + logit_scale * exact_dot(mix_vals, block_rows)
-        block_grad = block_grad + logit_scale * exact_rows(mix_vals, source)
-        block_rows, block_groups, block_lse, block_grad = passed_along(
-            (block_rows, block_groups, block_lse, block_grad), "wide", 1
-        )
-        return ((block_rows, block_groups, block_lse, block_grad, source_grad), None)
-
-    back_carry = (
-        home_rows,
-        home_groups,
-        home_lse,
-        jnp.zeros((span, model_width), jnp.float32),
-        jnp.zeros((pair_count, model_width), jnp.float32),
-    )
-    back_end = lax.scan(backward_step, back_carry, jnp.arange(wide_count))[0]
-    source_grad = back_end[4]
-    target_grad = lax.psum_scatter(back_end[3], "narrow", scatter_dimension=0, tiled=True)
-    loss_terms = jnp.stack([row_lse - diagonal, own_col - diagonal], axis=1)
+    same_pair = jnp.eye(total_pairs, dtype=jnp.float32)
+    raw = logit_scale * exact_cols(source, target) - logit_scale * margin * same_pair
+    live = all_groups[:, None] == all_groups[None, :]
+    masked = jnp.where(live, raw, far_low)
+    row_lse = jax.nn.logsumexp(masked, axis=1)
+    col_lse = jax.nn.logsumexp(masked, axis=0)
+    mix = (
+        pair_weight * (jnp.exp(masked - row_lse[:, None]) + jnp.exp(masked - col_lse[None, :]))
+        - 2.0 * pair_weight * same_pair
+    )
+    begin = rank_at * pair_count
+    own_mix = lax.dynamic_slice_in_dim(mix, begin, pair_count, 0)
+    own_cols = lax.dynamic_slice_in_dim(mix, begin, pair_count, 1)
+    source_grad = logit_scale * exact_dot(own_mix, target)
+    target_grad = logit_scale * exact_rows(own_cols, source)
+    terms = jnp.stack([row_lse - diagonal, col_lse - diagonal], axis=1)
+    loss_terms = lax.dynamic_slice_in_dim(terms, begin, pair_count, 0)
     pooled_grad = jnp.stack([source_grad, target_grad], axis=1).reshape(sent_count, model_width)
     d_hidden = pool_back(pooled_grad)[0].reshape(token_count, model_width)
-    shard_lists = [[], [], [], [], [], []]
-    for layer_at in reversed(range(LAYERS)):
-        layer_params = fetch(layer_at)
-        d_hidden, layer_grads = layer_backward(d_hidden, layer_params, saves[layer_at], key_ok)
-        grad_shards = (
-            lax.psum_scatter(layer_grads[0], ("wide", "narrow"), scatter_dimension=0, tiled=True),
-            lax.psum_scatter(layer_grads[1], ("wide", "narrow"), scatter_dimension=0, tiled=True),
-            lax.psum_scatter(layer_grads[2], ("wide", "narrow"), scatter_dimension=0, tiled=True),
-            lax.psum_scatter(layer_grads[3], ("wide", "narrow"), scatter_dimension=0, tiled=True),
-            lax.psum_scatter(layer_grads[4], ("wide", "narrow"), scatter_dimension=1, tiled=True),
-            lax.psum_scatter(layer_grads[5], ("wide", "narrow"), scatter_dimension=1, tiled=True),
-        )
-        for member_at in range(6):
-            shard_lists[member_at].insert(0, grad_shards[member_at])
+    d_hidden, layer_grads = layer_backward(d_hidden, layer_params, saved, key_ok)
+    reduced = reduce_grads(as_units(*layer_grads[:4]))
+    d_matrices = own_rows(reduced, core)
+    d_vectors = lax.psum(jnp.concatenate(layer_grads[4:]), everywhere)
+    d_vectors = lax.dynamic_slice_in_dim(d_vectors, rank_at * 6, 6, 1)
     sent_rows = d_hidden.astype(jnp.bfloat16)
     grad_slots = (
         jnp.zeros((device_total * slot_cap, model_width), jnp.bfloat16).at[slot_of].set(sent_rows)
@@ -398,17 +663,16 @@
         .add(arrived.reshape(-1, model_width).astype(jnp.float32), mode="drop")
     )
     token_grads = d_hidden.reshape(pair_count, 2, SEQ, model_width)
-    stacked = [jnp.stack(member_list) for member_list in shard_lists]
     return (
         loss_terms,
         token_grads,
         table_grads,
-        stacked[0],
-        stacked[1],
-        stacked[2],
-        stacked[3],
-        stacked[4],
-        stacked[5],
+        d_matrices[0][None],
+        d_matrices[1][None],
+        d_matrices[2][None],
+        d_matrices[3][None],
+        d_vectors[None, :2],
+        d_vectors[None, 2:],
     )
 
 

time: 2430 us -> 698 us (0.29)
  starting transfers between devices: 924 us -> 37.5 us
  blocking collectives: 575 us -> 175 us
  waiting for transfers between devices: 325 us -> 0.58 us
  Pallas kernels: 0 us -> 142 us
  local copies, waits for them, and re-layouts: 319 us -> 198 us
  matrix products: 151 us -> 81.2 us
    ppermute x128 -> x2, starting transfers between devices: 616 us -> 2.67 us  [swapped(): return lax.ppermute(value, 'narrow', [(i, i ^ 1) for i in range(8)])]
    unnamed x4 -> x1, blocking collectives: 473 us -> 63.8 us
    unnamed x97 -> x0, starting transfers between devices: 288 us -> none
    ppermute x128 -> x2, waiting for transfers between devices: 198 us -> 0.01 us  [swapped(): return lax.ppermute(value, 'narrow', [(i, i ^ 1) for i in range(8)])]
    unnamed x300 -> x98, local copies, waits for them, and re-layouts: 162 us -> 12.1 us
    pallas_call x0 -> x3, Pallas kernels: none -> 142 us  [the longest x2 90.8 us: gather_units(): pl.pallas_call(functools.partial(gather_kernel, rounds), out_shape=jax.Sh...]
    reshape x0 -> x12, local copies, waits for them, and re-layouts: none -> 82.4 us  [the longest x4 29.1 us: as_units(): m.reshape(shape).transpose(3, 4, 5, 0, 1, 2, 6)]
    psum x0 -> x1, blocking collectives: none -> 74.1 us  [shards(): d_vectors = lax.psum(jnp.concatenate(layer_grads[4:]), everywhere)]
  transfers between devices with their start and end apart: 233 -> 7, of which waited for: 39 -> 1; matrix products, arithmetic and copies ran while one was open for 35% -> 14% of each run, Pallas kernels for 0% -> 9%
where the time goes in v1:
time: 698 us; the launch traced here: 689 us
  local copies, waits for them, and re-layouts  198 us (28%)
  blocking collectives  175 us (25%)
  Pallas kernels  142 us (20%)
  matrix products  81.2 us (12%)
  other arithmetic  53.1 us (8%)
  starting transfers between devices  37.5 us (5%)
    pallas_call x2, Pallas kernels, gather_units(): pl.pallas_call(functools.partial(gather_kernel, rounds), out_shape=jax.Sh...  90.8 us
    psum x1, blocking collectives, shards(): d_vectors = lax.psum(jnp.concatenate(layer_grads[4:]), everywhere)  74.1 us
    unnamed x1, blocking collectives  63.8 us
    pallas_call x1, Pallas kernels, reduce_grads(): pl.pallas_call(reduce_kernel, out_shape=jax.ShapeDtypeStruct((3, 3, UNIT,...  51.5 us
    all_gather x1, blocking collectives, shards(): lax.all_gather(jnp.concatenate([gains[0], biases[0]]), everywhere, axis=1...  36.9 us
    reshape x4, local copies, waits for them, and re-layouts, as_units(): m.reshape(shape).transpose(3, 4, 5, 0, 1, 2, 6)  29.1 us
    dot_general x4, matrix products, contract_cols(): lax.dot_general(first_part, second_part, (((1,), (1,)), ((), ())), prefer...  22.4 us
    dot_general x1, matrix products, layer_forward(): jnp.dot(norm_low, up_w, preferred_element_type=jnp.float32)  20.1 us
  transfers between devices with their start and end apart: 7, of which 1 were waited for; matrix products, arithmetic and copies ran while one was open for 14% of the time, Pallas kernels for 9%

profile of v1, /device:TPU:1, one launch (start us, length us, event | category | flops | bytes accessed | tf_op | source)
XLA Modules:
  0.0 689.0 jit_solution(7735860489632882669)
XLA Ops:
  1.6 1.5 collective-permute-start
  6.3 2.4 scatter_custom_fusion
  9.5 10.2 %all-to-all-start = ((s32[128,1,8]{2,1,0:T(1,128)}), s32[128,1,8]{2,1,0:T(1,128)S(1)}, u32[]{:S(2)}, u32[]{:S(2)}) async-start(s32[128,1,8]{2,1,0:T(1,128)} %bitcast.5), calls=%async_computation | async-start | bytes 131072 | tf_op jit(solution)/shard_map/all_to_all | solution.py:600
  21.2 36.9 %all-gather = bf16[128,6,12]{2,1,0:T(8,128)(2,1)S(1)} all-gather(bf16[1,6,12]{2,1,0:T(8,128)(2,1)S(1)} %maximum_bitcast_fusion.3), channel_id=1, replica_groups=mesh['wide'=16,'narrow'=8] {'wide','narrow'}, dimensions={0}, use_global_device_ids=true | all-gather | bytes 18576 | tf_op jit(solution)/shard_map/all_gather | solution.py:612
  60.5 63.8 %all-reduce = s32[512]{0:T(512)S(1)} all-reduce(s32[512]{0:T(512)S(1)} %dynamic-update-slice), channel_id=1, replica_groups=mesh['wide'=16,'narrow'=8] {'wide','narrow'}, use_global_device_ids=true, to_apply=%add | all-reduce | flops 512 | bytes 4096
  124.3 4.1 all-to-all-start.2
  128.9 8.0 %gather_fusion = bf16[1024,768]{1,0:T(8,128)(2,1)S(1)} fusion(bf16[3920,768]{1,0:T(8,128)(2,1)} %param.13, s32[1024]{0:T(1024)S(1)} %broadcast_clamp_fusion), kind=kCustom, calls=%fused_computation | custom fusion | bytes 3149824 | tf_op jit(solution)/shard_map/jit(_take)/gather | solution.py:602
  138.3 6.8 all-to-all-start.1
  147.9 62.6 %gather_weights.1 = bf16[3,2,3,4,4,4,48,128]{7,6,5,4,3,2,1,0:T(8,128)(2,1)} custom-call(bf16[3,3,1,1,1,48,128]{6,5,4,3,2,1,0:T(8,128)(2,1)} %maximum_bitcast_fusion.own_ref), custom_call_target="tpu_custom_call" | custom-call | tf_op jit(solution)/shard_map/gather_weights/pallas_call | solution.py:173
  210.5 10.8 %slice_bitcast_fusion = (bf16[4,4,4,48,2,3,128]{6,3,1,0,2,5,4:T(8,128)(2,1)S(1)}, bf16[4,4,48,2,3,4,128]{6,2,1,0,5,4,3:T(8,128)(2,1)}, bf16[4,4,48,2,3,4,128]{6,2,1,0,5,4,3:T(8,128)(2,1)}) fusion(bf16[3,2,3,4,4,4,48,128]{7,6,5,4,3,2,1,0:T(8,128)(2,1)} %gather_weights.1), kind=kLoop, calls=%fused_computation.36 | loop fusion | bytes 28311552 | tf_op jit(solution)/shard_map/transpose | solution.py:557
  221.3 6.7 copy.143
  228.1 12.9 %reshape.594 = bf16[3072,768]{1,0:T(8,128)(2,1)} reshape(bf16[4,4,4,48,2,3,128]{6,5,4,3,2,1,0:T(4,128)(2,1)} %copy.143) | data formatting | bytes 9437184 | tf_op jit(solution)/shard_map/reshape | solution.py:557
  240.9 8.2 %copy.142 = bf16[4,4,48,2,3,4,128]{6,5,4,3,2,1,0:T(4,128)(2,1)} copy(bf16[4,4,48,2,3,4,128]{6,2,1,0,5,4,3:T(8,128)(2,1)} %get-tuple-element.77) | data formatting | bytes 9437184 | tf_op jit(solution)/shard_map/transpose | solution.py:555
  249.1 8.8 %reshape.593 = bf16[768,3072]{1,0:T(8,128)(2,1)} reshape(bf16[4,4,48,2,3,4,128]{6,5,4,3,2,1,0:T(4,128)(2,1)} %copy.142) | data formatting | bytes 9437184 | tf_op jit(solution)/shard_map/reshape | solution.py:555
  257.8 8.2 %copy.132 = bf16[4,4,48,2,3,4,128]{6,5,4,3,2,1,0:T(4,128)(2,1)} copy(bf16[4,4,48,2,3,4,128]{6,2,1,0,5,4,3:T(8,128)(2,1)} %get-tuple-element.78) | data formatting | bytes 9437184 | tf_op jit(solution)/shard_map/transpose | solution.py:555
  266.0 8.8 %reshape.591 = bf16[768,3072]{1,0:T(8,128)(2,1)} reshape(bf16[4,4,48,2,3,4,128]{6,5,4,3,2,1,0:T(4,128)(2,1)} %copy.132) | data formatting | bytes 9437184 | tf_op jit(solution)/shard_map/reshape | solution.py:555
  274.8 2.0 gather_fusion.1
  277.7 5.4 fusion.8
  283.1 2.8 copy.135
  285.9 4.4 reshape.592
  290.4 3.9 fusion.103
  294.2 1.9 copy.178
  296.2 2.0 copy.179
  298.1 2.8 fusion.13
  303.4 2.4 copy.141
  305.8 3.5 convert_element_type.114
  309.3 2.8 fusion.106
  312.4 20.1 %multiply_convert_fusion = (bf16[512,3072]{1,0:T(8,128)(2,1)S(1)}, f32[512,3072]{1,0:T(8,128)}, f32[512,3072]{1,0:T(8,128)}) fusion(f32[3072]{0:T(1024)S(1)} %add.284, bf16[768,3072]{1,0:T(8,128)(2,1)} %reshape.593, f32[512,768]{1,0:T(8,128)S(1)} %get-tuple-element.105, f32[768]{0:T(1024)S(1)} %get-tuple-element.56, f32[768]{0:T(1024)S(1)} %get-tuple-element.61, ...), kind=kOutput, calls=%fused_computation.12 | convolution fusion | flops 2521694208 | bytes 22042624 | tf_op jit(solution)/shard_map/dot_general | solution.py:434
  332.6 2.8 fusion.107
  338.0 28.1 %gather_pooled.1 = f32[1,2,3,4,4,4,16,128]{7,6,5,4,3,2,1,0:T(8,128)} custom-call(f32[1,3,1,1,1,16,128]{6,5,4,3,2,1,0:T(8,128)} %divide_multiply_fusion.own_ref), custom_call_target="tpu_custom_call" | custom-call | tf_op jit(solution)/shard_map/gather_pooled/pallas_call | solution.py:173
  366.2 4.1 copy.144
  370.3 5.2 reshape.596
  375.5 5.5 fusion.104
  381.1 2.9 fusion.99
  388.1 2.1 fusion.26
  390.2 2.2 fusion.101
  393.2 9.7 %convert_reduce_fusion.1 = (f32[3072]{0:T(1024)}, bf16[512,3072]{1,0:T(8,128)(2,1)S(1)}) fusion(f32[512,3072]{1,0:T(8,128)} %get-tuple-element.75, f32[512,3072]{1,0:T(8,128)} %get-tuple-element.106, f32[3072]{0:T(1024)S(1)} %add.284, bf16[512,768]{1,0:T(8,128)(2,1)S(1)} %get-tuple-element.65, bf16[3072,768]{1,0:T(8,128)(2,1)} %reshape.594), kind=kOutput, calls=%fused_computation.10 | convolution fusion | flops 2442654720 | bytes 21258240 | tf_op jit(solution)/shard_map/dot_general | solution.py:363
  402.9 3.7 multiply_reduce_fusion.2
  406.6 4.8 convolution_convert_fusion.1
  414.0 1.8 convolution_convert_fusion.4
  415.8 3.0 convolution_convert_fusion.5
  418.8 3.8 reshape.660
  422.6 2.8 convolution_bitcast_fusion
  425.4 1.9 multiply_reduce_fusion
  432.3 4.5 convolution_convert_fusion
  436.8 3.7 convert_reduce_fusion
  440.4 7.0 %copy.153 = bf16[8,64,3,12,64]{1,0,4,3,2:T(8,128)(2,1)} copy(bf16[8,64,3,12,64]{4,1,3,0,2:T(8,128)(2,1)} %get-tuple-element.69) | data formatting | bytes 4718592 | tf_op jit(solution)/shard_map/convert_element_type | solution.py:512
  447.4 7.5 %convert_element_type.129 = bf16[512,2304]{0,1:T(8,128)(2,1)} reshape(bf16[8,64,3,12,64]{1,0,4,3,2:T(8,128)(2,1)} %copy.153) | data formatting | bytes 4718592 | tf_op jit(solution)/shard_map/convert_element_type | solution.py:512
  454.9 6.1 add_add_fusion.4
  461.0 2.0 convolution_convert_fusion.2
  463.0 9.6 %reshape.602 = bf16[4,4,48,2,3,4,128]{6,5,4,3,2,1,0:T(4,128)(2,1)} reshape(bf16[768,3072]{1,0:T(8,128)(2,1)} %convolution_convert_fusion.1) | data formatting | bytes 9437184 | tf_op jit(solution)/shard_map/reshape | solution.py:564
  472.7 5.7 copy.240
  478.3 11.3 %reshape.603 = bf16[4,4,4,48,2,3,128]{6,5,4,3,2,1,0:T(4,128)(2,1)} reshape(bf16[3072,768]{1,0:T(8,128)(2,1)} %convolution_convert_fusion) | data formatting | bytes 9437184 | tf_op jit(solution)/shard_map/reshape | solution.py:565
  489.6 6.3 copy.239
  495.9 2.8 pad_maximum_fusion.1
  498.8 10.1 %reshape.601 = bf16[4,4,48,2,3,4,128]{6,5,4,3,2,1,0:T(4,128)(2,1)} reshape(bf16[768,3072]{1,0:T(8,128)(2,1)} %pad_maximum_fusion.1) | data formatting | bytes 9437184 | tf_op jit(solution)/shard_map/reshape | solution.py:564
  508.9 3.7 copy.241
  513.9 5.8 pad_maximum_fusion.part_ref
  519.7 51.5 %reduce_grads.1 = f32[3,3,48,128]{3,2,1,0:T(8,128)} custom-call(bf16[3,2,3,4,4,4,48,128]{7,6,5,4,3,2,1,0:T(8,128)(2,1)} %pad_maximum_fusion.part_ref), custom_call_target="tpu_custom_call" | custom-call | tf_op jit(solution)/shard_map/reduce_grads/pallas_call | solution.py:320
  573.8 6.8 all-to-all-start.4
  580.7 4.8 scatter_custom_fusion.1
  586.1 7.0 %all-to-all-start.3 = ((bf16[128,8,768]{2,1,0:T(8,128)(2,1)}), bf16[128,8,768]{2,1,0:T(8,128)(2,1)}, u32[]{:S(2)}, u32[]{:S(2)}) async-start(bf16[128,8,768]{2,1,0:T(8,128)(2,1)} %bitcast.261), calls=%async_computation.3 | async-start | bytes 3145728 | tf_op jit(solution)/shard_map/all_to_all | solution.py:656
  594.8 74.1 %psum.7 = f32[12,768]{1,0:T(8,128)S(1)} all-reduce(f32[12,768]{1,0:T(8,128)S(1)} %concatenate.33), channel_id=1, replica_groups=mesh['wide'=16,'narrow'=8] {'wide','narrow'}, use_global_device_ids=true, to_apply=%region_33.34 | all-reduce | flops 9216 | bytes 73728 | tf_op jit(solution)/shard_map/psum | solution.py:649
  675.6 13.2 %scatter_custom_fusion.2 = f32[3920,768]{1,0:T(8,128)} fusion(s32[1024]{0:T(1024)} %bitcast.292, f32[]{:T(128)} %constant.73.clone.1, bf16[128,8,768]{2,1,0:T(8,128)(2,1)} %all-to-all-done.3), kind=kCustom, calls=%fused_computation.26 | custom fusion | flops 1572864 | bytes 13615616 | tf_op jit(solution)/shard_map/scatter-add | solution.py:663
  (246 shorter events, 44.5 us)
Async XLA Ops:
  0.6 57.7 %copy-start.34 = (s32[4,2]{0,1:T(2,128)S(1)}, s32[4,2]{0,1:T(2,128)}, u32[]{:S(2)}) copy-start(s32[4,2]{0,1:T(2,128)} %param.11) | copy-start | bytes 100
  0.7 58.0 %copy-start.25 = (bf16[1,6,3072]{2,1,0:T(8,128)(2,1)S(1)}, bf16[1,6,3072]{2,1,0:T(8,128)(2,1)}, u32[]{:S(2)}) copy-start(bf16[1,6,3072]{2,1,0:T(8,128)(2,1)} %param.16) | copy-start | bytes 110596
  0.7 58.1 %copy-start.29 = (bf16[1,6,768]{2,1,0:T(8,128)(2,1)S(1)}, bf16[1,6,768]{2,1,0:T(8,128)(2,1)}, u32[]{:S(2)}) copy-start(bf16[1,6,768]{2,1,0:T(8,128)(2,1)} %param.15) | copy-start | bytes 27652
  0.7 58.1 %copy-start.26 = (bf16[1,6,2304]{2,1,0:T(8,128)(2,1)S(1)}, bf16[1,6,2304]{2,1,0:T(8,128)(2,1)}, u32[]{:S(2)}) copy-start(bf16[1,6,2304]{2,1,0:T(8,128)(2,1)} %param.14) | copy-start | bytes 82948
  0.7 59.6 %copy-start.35 = (s32[4]{0:T(128)S(1)}, s32[4]{0:T(128)}, u32[]{:S(2)}) copy-start(s32[4]{0:T(128)} %param.12) | copy-start | bytes 52
  1.6 145.5 %collective-permute-start = (bf16[3,24,128]{2,1,0:T(8,128)(2,1)S(1)}, bf16[3,24,128]{2,1,0:T(8,128)(2,1)S(1)}, u32[]{:S(2)}, u32[]{:S(2)}) collective-permute-start(bf16[3,24,128]{2,1,0:T(8,128)(2,1)S(1)} %bitcast.282), channel_id=1, source_target_pairs={{0,1},{1,0},{2,3},{3,2},{4,5},{5,4},{6,7},{7,6},{8,9},{9,8},{10,11... | collective-permute-start | bytes 55304 | tf_op jit(solution)/shard_map/ppermute | solution.py:550
  6.3 138.7 %copy-start.31 = (s32[512,1]{0,1:T(1,128)}, s32[512,1]{0,1:T(1,128)S(1)}, u32[]{:S(2)}) copy-start(s32[512,1]{0,1:T(1,128)S(1)} %compare_select_fusion.2) | copy-start | bytes 6148
  9.5 114.8 %all-to-all-start = ((s32[128,1,8]{2,1,0:T(1,128)}), s32[128,1,8]{2,1,0:T(1,128)S(1)}, u32[]{:S(2)}, u32[]{:S(2)}) async-start(s32[128,1,8]{2,1,0:T(1,128)} %bitcast.5), calls=%async_computation | async-start | bytes 131072 | tf_op jit(solution)/shard_map/all_to_all | solution.py:600
  124.3 14.0 %all-to-all-start.2 = ((bf16[8,2,3,6,128]{4,1,3,2,0:T(2,128)(2,1)}), bf16[8,2,3,6,128]{4,1,3,2,0:T(2,128)(2,1)S(1)}, u32[]{:S(2)}, u32[]{:S(2)}) async-start(bf16[8,2,3,6,128]{4,1,3,2,0:T(2,128)(2,1)} %bitcast.14), calls=%async_computation.2 | async-start | bytes 147456 | tf_op jit(solution)/shard_map/all_to_all | solution.py:537
  138.3 136.5 %all-to-all-start.1 = ((bf16[128,8,768]{2,1,0:T(8,128)(2,1)}), bf16[128,8,768]{2,1,0:T(8,128)(2,1)S(1)}, u32[]{:S(2)}, u32[]{:S(2)}) async-start(bf16[128,8,768]{2,1,0:T(8,128)(2,1)} %fusion.32), calls=%async_computation.1 | async-start | bytes 3145728 | tf_op jit(solution)/shard_map/all_to_all | solution.py:604
  276.8 0.9 copy-start.20
  301.0 1.4 copy-start.9
  309.3 23.2 %slice-start.4 = ((s8[4718592]{0:T(1024)(128)(4,1)}), s8[4194304]{0:T(1024)(128)(4,1)S(1)}, s32[]{:S(2)}) async-start(s8[4718592]{0:T(1024)(128)(4,1)} %bitcast.264), calls=%async_computation.9 | async-start | bytes 8388608
  312.1 20.4 %copy-start.11 = (f32[512,768]{1,0:T(8,128)}, f32[512,768]{1,0:T(8,128)S(1)}, u32[]{:S(2)}) copy-start(f32[512,768]{1,0:T(8,128)S(1)} %get-tuple-element.105) | copy-start | bytes 4718596
  312.4 20.1 %slice-start.5 = ((s8[4718592]{0:T(1024)(128)(4,1)}), s8[524288]{0:T(1024)(128)(4,1)S(1)}, s32[]{:S(2)}) async-start(s8[4718592]{0:T(1024)(128)(4,1)} %bitcast.264), calls=%async_computation.10 | async-start | bytes 1048576
  332.5 2.8 copy-start.36
  335.3 1.1 copy-start
  381.0 4.8 copy-start.6
  381.0 5.8 copy-start.2
  388.0 5.1 copy-start.22
  390.2 12.8 %slice-start.2 = ((s8[4718592]{0:T(1024)(128)(4,1)}), s8[4194304]{0:T(1024)(128)(4,1)S(1)}, s32[]{:S(2)}) async-start(s8[4718592]{0:T(1024)(128)(4,1)} %bitcast.262), calls=%async_computation.7 | async-start | bytes 8388608
  393.2 9.7 %copy-start.18 = (bf16[512,768]{1,0:T(8,128)(2,1)}, bf16[512,768]{1,0:T(8,128)(2,1)S(1)}, u32[]{:S(2)}) copy-start(bf16[512,768]{1,0:T(8,128)(2,1)S(1)} %get-tuple-element.65) | copy-start | bytes 2359300
  393.2 9.7 %copy-start.12 = (f32[512,768]{1,0:T(8,128)S(1)}, f32[512,768]{1,0:T(8,128)}, u32[]{:S(2)}) copy-start(f32[512,768]{1,0:T(8,128)} %copy-done.11) | copy-start | bytes 4718596
  393.2 9.7 %slice-start.3 = ((s8[4718592]{0:T(1024)(128)(4,1)}), s8[524288]{0:T(1024)(128)(4,1)S(1)}, s32[]{:S(2)}) async-start(s8[4718592]{0:T(1024)(128)(4,1)} %bitcast.262), calls=%async_computation.8 | async-start | bytes 1048576
  411.4 2.6 copy-start.17
  412.1 1.2 copy-start.13
  422.6 2.8 copy-start.8
  422.6 2.8 copy-start.10
  427.3 1.4 copy-start.4
  428.7 1.4 copy-start.5
  430.2 1.1 copy-start.19
  430.2 2.1 copy-start.37
  447.4 7.5 %copy-start.14 = (f32[512,768]{1,0:T(8,128)S(1)}, f32[512,768]{1,0:T(8,128)}, u32[]{:S(2)}) copy-start(f32[512,768]{1,0:T(8,128)} %copy-done.13) | copy-start | bytes 4718596
  454.9 6.1 copy-start.15
  454.9 6.1 copy-start.21
  489.6 6.3 copy-start.16
  498.8 13.8 %slice-start = ((s8[4718592]{0:T(1024)(128)(4,1)}), s8[524288]{0:T(1024)(128)(4,1)S(1)}, s32[]{:S(2)}) async-start(s8[4718592]{0:T(1024)(128)(4,1)} %bitcast.255), calls=%async_computation.5 | async-start | bytes 1048576
  508.8 3.7 slice-start.1
  508.8 5.0 copy-start.1
  571.3 14.2 %copy-start.24 = (f32[3,12,64]{2,1,0:T(8,128)S(1)}, f32[3,12,64]{2,1,0:T(8,128)}, u32[]{:S(2)}) copy-start(f32[3,12,64]{2,1,0:T(8,128)} %get-tuple-element.68) | copy-start | bytes 27652
  573.8 12.2 %all-to-all-start.4 = ((f32[8,2,3,6,128]{4,1,3,2,0:T(2,128)}), f32[8,2,3,6,128]{4,1,3,2,0:T(2,128)S(1)}, u32[]{:S(2)}, u32[]{:S(2)}) async-start(f32[8,2,3,6,128]{4,1,3,2,0:T(2,128)} %copy.159), calls=%async_computation.4 | async-start | bytes 294912 | tf_op jit(solution)/shard_map/all_to_all | solution.py:571
  580.6 12.5 %copy-start.23 = (f32[8,768]{1,0:T(8,128)S(1)}, f32[8,768]{1,0:T(8,128)}, u32[]{:S(2)}) copy-start(f32[8,768]{1,0:T(8,128)} %copy-done.22) | copy-start | bytes 73732
  580.6 12.7 %copy-start.27 = (f32[768]{0:T(1024)S(1)}, f32[768]{0:T(1024)}, u32[]{:S(2)}) copy-start(f32[768]{0:T(1024)} %get-tuple-element.64) | copy-start | bytes 9220
  580.6 12.7 %copy-start.30 = (f32[3072]{0:T(1024)S(1)}, f32[3072]{0:T(1024)}, u32[]{:S(2)}) copy-start(f32[3072]{0:T(1024)} %get-tuple-element.62) | copy-start | bytes 36868
  580.6 12.7 %copy-start.33 = (f32[768]{0:T(1024)S(1)}, f32[768]{0:T(1024)}, u32[]{:S(2)}) copy-start(f32[768]{0:T(1024)} %get-tuple-element.45) | copy-start | bytes 9220
  580.7 12.7 %copy-start.32 = (f32[768]{0:T(1024)S(1)}, f32[768]{0:T(1024)}, u32[]{:S(2)}) copy-start(f32[768]{0:T(1024)} %get-tuple-element.49) | copy-start | bytes 9220
  580.7 12.7 %copy-start.28 = (f32[768]{0:T(1024)S(1)}, f32[768]{0:T(1024)}, u32[]{:S(2)}) copy-start(f32[768]{0:T(1024)} %get-tuple-element.66) | copy-start | bytes 9220
  580.7 89.0 %copy-start.3 = (f32[512,1,768]{2,1,0:T(1,128)S(1)}, f32[512,1,768]{2,1,0:T(1,128)}, u32[]{:S(2)}) copy-start(f32[512,1,768]{2,1,0:T(1,128)} %copy-done.2) | copy-start | bytes 4718596
  580.7 89.0 %copy-start.7 = (f32[512,1,768]{2,1,0:T(1,128)S(1)}, f32[512,1,768]{2,1,0:T(1,128)}, u32[]{:S(2)}) copy-start(f32[512,1,768]{2,1,0:T(1,128)} %copy-done.6) | copy-start | bytes 4718596
  586.1 89.5 %all-to-all-start.3 = ((bf16[128,8,768]{2,1,0:T(8,128)(2,1)}), bf16[128,8,768]{2,1,0:T(8,128)(2,1)}, u32[]{:S(2)}, u32[]{:S(2)}) async-start(bf16[128,8,768]{2,1,0:T(8,128)(2,1)} %bitcast.261), calls=%async_computation.3 | async-start | bytes 3145728 | tf_op jit(solution)/shard_map/all_to_all | solution.py:656
  593.6 78.3 %collective-permute-start.1 = (f32[3,24,128]{2,1,0:T(8,128)S(1)}, f32[3,24,128]{2,1,0:T(8,128)}, u32[]{:S(2)}, u32[]{:S(2)}) collective-permute-start(f32[3,24,128]{2,1,0:T(8,128)S(1)} %dynamic-slice_bitcast_fusion), channel_id=1, source_target_pairs={{0,1},{1,0},{2,3},{3,2},{4,5},{5,4},{6,7},{7,6},{8,9},{9,8},{10,11... | collective-permute-start | bytes 110600 | tf_op jit(solution)/shard_map/ppermute | solution.py:550

commit v2 on v1

v2 whole, which is shorter than its diff:
```python
import functools

import jax
import jax.numpy as jnp
from jax import lax
from jax.experimental import pallas as pl
from jax.experimental.pallas import tpu as pltpu
from jax.sharding import PartitionSpec as P

HEAD_DIM = 64
SEQ = 64


logit_scale = 10.0
margin = 0.3
norm_eps = 1e-12
pool_eps = 1e-06
far_low = -1e30


MESH = pl.DeviceIdType.MESH
RING = 4
ORDERS = ((0, 1, 2), (1, 2, 0), (2, 0, 1))
UNIT = 48


def where_am_i():
    wide = lax.axis_index("wide")
    narrow = lax.axis_index("narrow")
    return [narrow // 2, wide // RING, wide % RING], narrow % 2


def device_at(spot, core):
    return (spot[1] * RING + spot[2], spot[0] * 2 + core)


def moved(spot, dim, by):
    there = list(spot)
    there[dim] = (spot[dim] + by) % RING
    return there


def block_of(ref, part, core, order, spans):
    return ref.at[(part, core, order) + tuple(pl.ds(*spans[d]) for d in range(3))]


def greet(spot, core):
    barrier = pltpu.get_barrier_semaphore()
    others = [(moved(spot, d, by), core) for d in range(3) for by in (1, -1)] + [(spot, 1 - core)]
    for there, c in others:
        pl.semaphore_signal(barrier, inc=1, device_id=device_at(there, c), device_id_type=MESH)
    pl.semaphore_wait(barrier, len(others))


class Gather:
    def __init__(self, out, send_sem, recv_sem, spot, core, dims):
        self.out, self.send_sem, self.recv_sem = out, send_sem, recv_sem
        self.spot, self.core, self.dims = spot, core, dims
        self.sent = []

    def block(self, r, o, spans, core):
        return self.out.at[(r, core, o) + tuple(pl.ds(*spans[d]) for d in self.dims)]

    def push(self, r, o, event, spans, there, core=None, src=None):
        dst = self.block(r, o, spans, self.core)
        copy = pltpu.make_async_remote_copy(
            src_ref=dst if src is None else src,
            dst_ref=dst,
            send_sem=self.send_sem.at[r, o, event],
            recv_sem=self.recv_sem.at[r, o, event],
            device_id=device_at(there, self.core if core is None else core),
            device_id_type=MESH,
        )
        copy.start()
        self.sent.append(copy)

    def landed(self, r, o, event, spans, core=None):
        dst = self.block(r, o, spans, self.core if core is None else core)
        pltpu.make_async_copy(dst, dst, self.recv_sem.at[r, o, event]).wait()

    def spans(self, o, phase, at, half=None):
        order = ORDERS[o]
        spans = {}
        for k, d in enumerate(order):
            if k < phase:
                spans[d] = (0, RING)
            elif k == phase:
                spans[d] = (at, 1)
            else:
                spans[d] = (self.spot[d], 1)
        if half is not None:
            spans[order[0]] = (2 * half, 2)
        return spans

    def ring(self, o, phase):
        d = ORDERS[o][phase]
        v = self.spot[d]
        up, down = moved(self.spot, d, 1), moved(self.spot, d, -1)
        return v, (v - 1) % RING, (v + 1) % RING, (v + 2) % RING, up, down

    def begin(self, r, o, src):
        v, low, high, far, up, down = self.ring(o, 0)
        here = self.spans(o, 0, v)
        self.push(r, o, 0, here, up, src=src)
        self.push(r, o, 1, here, down, src=src)

    def pass_on(self, r, o):
        v, low, high, far, up, down = self.ring(o, 0)
        self.landed(r, o, 0, self.spans(o, 0, low))
        self.push(r, o, 2, self.spans(o, 0, low), up)

    def first_done(self, r, o):
        v, low, high, far, up, down = self.ring(o, 0)
        self.landed(r, o, 1, self.spans(o, 0, high))
        self.landed(r, o, 2, self.spans(o, 0, far))
        self.share(r, o, 11, self.spans(o, 1, self.spot[ORDERS[o][1]]))

    def share(self, r, o, event, spans):
        self.push(r, o, event, spans, self.spot, 1 - self.core)

    def spread(self, r, o, phase):
        v, low, high, far, up, down = self.ring(o, phase)
        event = 3 + 4 * (phase - 1)
        here = self.spans(o, phase, v)
        self.push(r, o, event, here, up)
        self.push(r, o, event + 1, here, down)

    def relay(self, r, o, phase):
        v, low, high, far, up, down = self.ring(o, phase)
        event, shared = 3 + 4 * (phase - 1), 11 + 3 * (phase - 1)
        self.landed(r, o, event, self.spans(o, phase, low))
        self.push(r, o, event + 2, self.spans(o, phase, low, 0), up)
        self.landed(r, o, event + 1, self.spans(o, phase, high))
        self.push(r, o, event + 3, self.spans(o, phase, high, 1), down)
        self.share(r, o, shared + 1, self.spans(o, phase, low))
        self.share(r, o, shared + 2, self.spans(o, phase, high))

    def finish(self, r, o, phase):
        v, low, high, far, up, down = self.ring(o, phase)
        event, shared = 3 + 4 * (phase - 1), 11 + 3 * (phase - 1)
        self.landed(r, o, event + 2, self.spans(o, phase, far, 0))
        self.landed(r, o, event + 3, self.spans(o, phase, far, 1))
        self.share(r, o, shared + 3, self.spans(o, phase, far))

    def shared_done(self, r, o):
        other = 1 - self.core
        self.landed(r, o, 11, self.spans(o, 1, self.spot[ORDERS[o][1]]), other)
        for phase in (1, 2):
            v, low, high, far, up, down = self.ring(o, phase)
            shared = 11 + 3 * (phase - 1)
            for k, at in enumerate((low, high, far)):
                self.landed(r, o, shared + 1 + k, self.spans(o, phase, at), other)

    def drain(self):
        for copy in self.sent:
            copy.wait_send()


def mm(a, b):
    return jnp.dot(a, b, preferred_element_type=jnp.float32)


def mm_nt(a, b):
    return lax.dot_general(a, b, (((1,), (1,)), ((), ())), preferred_element_type=jnp.float32)


def mm_tn(a, b):
    return lax.dot_general(a, b, (((0,), (0,)), ((), ())), preferred_element_type=jnp.float32)


def head_mask():
    row = lax.broadcasted_iota(jnp.int32, (256, 256), 0) // HEAD_DIM
    col = lax.broadcasted_iota(jnp.int32, (256, 256), 1) // HEAD_DIM
    return row == col


def spread_heads(part, mask):
    four = jnp.concatenate([part] * 4, axis=0)
    return jnp.where(mask, four, jnp.zeros((), four.dtype))


def gather_heads(wide_part, mask):
    kept = jnp.where(mask, wide_part, 0.0)
    return (kept[:64] + kept[64:128]) + (kept[128:192] + kept[192:])


def panel(w, r, n2):
    c, o, x = n2 // 6, n2 // 2 % 3, n2 % 2 * 2
    pair = [w[r, c, o, x + k].reshape(768, 128) for k in range(2)]
    return jnp.concatenate(pair, axis=1)


def down_panel(w, cb, y):
    c, o = cb // 3, cb % 3
    return jnp.concatenate([w[2, c, o, x, y, z] for z in range(RING) for x in range(RING)], axis=0)


def split_low(value):
    high = value.astype(jnp.bfloat16)
    return high, (value - high.astype(jnp.float32)).astype(jnp.bfloat16)


def forward_kernel(
    lens_ref, own_ref, tile_ref, x_ref,
    w_out, vec_out, h1_out, h2_out, inv_out, nl_out, act_out, gp_out, qkv_out, prob_out, ctx_out, dpool_out, loss_out,
    w, vecs, tiles, h1, h2, inv, nl, act, gp, qkv, prob, ctx, resid, pooled, rnorm, pool_own, pool_swap, pool_all,
    left3, right3, stats,
    send_sem, recv_sem, local_sem, pool_send, pool_recv, tile_send, tile_recv, swap_sem, load_sem, save_sem,
):
    spot, core = where_am_i()
    bf, f32 = jnp.bfloat16, jnp.float32
    greet(spot, core)
    g = Gather(w_out, send_sem, recv_sem, spot, core, (0, 1, 2))
    every = [(r, o) for r in range(3) for o in range(3)]
    keep = []
    for r, o in every:
        here = g.spans(o, 0, spot[ORDERS[o][0]])
        copy = pltpu.make_async_copy(own_ref.at[r, o], g.block(r, o, here, core), local_sem.at[r, o])
        copy.start()
        keep.append(copy)
        g.begin(r, o, own_ref.at[r, o])
    tiles[pl.ds(spot[1], 1), pl.ds(spot[2], 1)] = tile_ref[...]
    tile_sent = []

    def tile_push(event, at, there):
        ref = tiles.at[at]
        copy = pltpu.make_async_remote_copy(
            src_ref=ref, dst_ref=ref, send_sem=tile_send.at[event], recv_sem=tile_recv.at[event],
            device_id=device_at(there, core), device_id_type=MESH,
        )
        copy.start()
        tile_sent.append(copy)

    def tile_landed(event, at):
        ref = tiles.at[at]
        pltpu.make_async_copy(ref, ref, tile_recv.at[event]).wait()

    def tile_at(phase, v):
        return (pl.ds(v, 1), pl.ds(spot[2], 1)) if phase == 0 else (pl.ds(0, RING), pl.ds(v, 1))

    def tile_step(phase, step):
        d = phase + 1
        v = spot[d]
        up, down = moved(spot, d, 1), moved(spot, d, -1)
        if step == 0:
            tile_push(3 * phase, tile_at(phase, v), up)
            tile_push(3 * phase + 1, tile_at(phase, v), down)
        elif step == 1:
            tile_landed(3 * phase, tile_at(phase, (v - 1) % RING))
            tile_push(3 * phase + 2, tile_at(phase, (v - 1) % RING), up)
        else:
            tile_landed(3 * phase + 1, tile_at(phase, (v + 1) % RING))
            tile_landed(3 * phase + 2, tile_at(phase, (v + 2) % RING))

    tile_step(0, 0)
    for r, o in every:
        g.pass_on(r, o)
    tile_step(0, 1)
    for (r, o), copy in zip(every, keep):
        copy.wait()
        g.first_done(r, o)
        g.spread(r, o, 1)
    tile_step(0, 2)
    tile_step(1, 0)
    for r, o in every:
        g.relay(r, o, 1)
    tile_step(1, 1)
    for r, o in every:
        g.finish(r, o, 1)
        g.spread(r, o, 2)
    tile_step(1, 2)

    row_at = lax.broadcasted_iota(jnp.int32, (128, 768), 0)
    col_at = lax.broadcasted_iota(jnp.int32, (128, 768), 1)
    all_vec = jnp.zeros((16, 768), f32)
    all_grp = jnp.zeros((16, 512), f32)
    for slab in range(16):
        part = tiles[slab // RING, slab % RING]
        pick = (col_at == row_at + UNIT * slab) & (row_at < UNIT)
        all_vec = all_vec + mm(part, pick.astype(bf))
        pick = (col_at == row_at + 32 * slab) & (row_at < 32)
        all_grp = all_grp + mm(part, pick[:, :512].astype(bf))
    vecs[...] = all_vec
    group_row = all_grp[12:13]
    saves = []

    def save(scratch, out, at):
        copy = pltpu.make_async_copy(scratch, out, save_sem.at[at])
        copy.start()
        saves.append(copy)

    def load(r, o, c):
        return pltpu.make_async_copy(w_out.at[r, c, o], w.at[r, c, o], load_sem.at[r, c, o])

    def arrive(r):
        for o in range(3):
            g.relay(r, o, 2)
        for o in range(3):
            g.finish(r, o, 2)
            load(r, o, core).start()

    def arrived(r):
        for o in range(3):
            g.shared_done(r, o)
            load(r, o, 1 - core).start()
        for o in range(3):
            load(r, o, 0).wait()
            load(r, o, 1).wait()

    save(vecs, vec_out, 0)
    arrive(0)
    arrived(0)
    mask = head_mask()

    def qkv_step(n2, _):
        kind, p = n2 // 3, n2 % 3
        rows = vecs[2:4, :]
        bias = jnp.where(kind == 0, rows[0:1], jnp.where(kind == 2, rows[1:2], 0.0))
        bias = jnp.where(p == 0, bias[:, :256], jnp.where(p == 1, bias[:, 256:512], bias[:, 512:]))
        qkv[n2] = (mm(x_ref[...], panel(w, 0, n2)) + bias).astype(bf)
        return 0

    lax.fori_loop(0, 9, qkv_step, 0)
    save(qkv, qkv_out, 1)
    arrive(1)

    def attend(s, _):
        rows = pl.ds(pl.multiple_of(s * SEQ, SEQ), SEQ)
        slot = lax.broadcasted_iota(jnp.int32, (SEQ, 256), 0)
        live = slot < lens_ref[s]
        for p in range(3):
            query, key_part, value = qkv[p, rows, :], qkv[3 + p, rows, :], qkv[6 + p, rows, :]
            scores = mm_nt(key_part, spread_heads(query, mask)) * 0.125
            scores = jnp.where(live, scores, far_low)
            powers = jnp.exp(scores - jnp.max(scores, axis=0, keepdims=True))
            probs = powers / jnp.sum(powers, axis=0, keepdims=True)
            prob[s, p] = probs
            ctx[p, rows, :] = gather_heads(mm_tn(probs.astype(bf), value), mask).astype(bf)
        return 0

    lax.fori_loop(0, 8, attend, 0)
    save(prob, prob_out, 2)
    save(ctx, ctx_out, 3)
    context = jnp.concatenate([ctx[0], ctx[1], ctx[2]], axis=1)
    for p in range(3):
        resid[:, 256 * p : 256 * p + 256] = mm(context, panel(w, 0, 9 + p))

    def norm_one_step(s, _):
        rows = pl.ds(pl.multiple_of(s * SEQ, SEQ), SEQ)
        value = x_ref[rows, :].astype(f32) + (resid[rows, :] + vecs[4:5, :])
        centred = value - jnp.mean(value, axis=1, keepdims=True)
        inverse = lax.rsqrt(jnp.mean(centred * centred, axis=1, keepdims=True) + norm_eps)
        scaled = centred * inverse
        h1[rows, :] = scaled
        inv[0, rows, :] = jnp.broadcast_to(inverse, (SEQ, 128))
        normed = scaled * vecs[0:1, :] + vecs[5:6, :]
        nl[rows, :] = normed.astype(bf)
        resid[rows, :] = normed + vecs[6:7, :]
        return 0

    lax.fori_loop(0, 8, norm_one_step, 0)
    save(h1, h1_out, 4)
    save(nl, nl_out, 5)
    arrived(1)
    arrive(2)

    def up_step(n2, _):
        weight = panel(w, 1, n2)
        q, p = n2 // 3, n2 % 3
        rows = vecs[8:12, :]
        bias = jnp.where(q == 0, rows[0:1], jnp.where(q == 1, rows[1:2], jnp.where(q == 2, rows[2:3], rows[3:4])))
        bias = jnp.where(p == 0, bias[:, :256], jnp.where(p == 1, bias[:, 256:512], bias[:, 512:]))
        for half in range(4):
            part = pl.ds(128 * half, 128)
            pre = mm(nl[part, :], weight) + bias
            upper = 0.5 + 0.5 * lax.erf(pre * 0.7071067811865476)
            act[n2, part, :] = (pre * upper).astype(bf)
            gp[n2, part, :] = upper + pre * (jnp.exp(-0.5 * pre * pre) * 0.3989422804014327)
        return 0

    lax.fori_loop(0, 12, up_step, 0)
    save(act, act_out, 6)
    save(gp, gp_out, 7)
    arrived(2)

    def down_step(y, _):
        hidden = jnp.concatenate([act[3 * y], act[3 * y + 1], act[3 * y + 2]], axis=1)
        for p in range(3):
            weight = jnp.concatenate([down_panel(w, 2 * p, y), down_panel(w, 2 * p + 1, y)], axis=1)
            cols = slice(256 * p, 256 * p + 256)
            resid[:, cols] = resid[:, cols] + mm(hidden, weight)
        return 0

    lax.fori_loop(0, RING, down_step, 0)

    def norm_two_step(s, _):
        rows = pl.ds(pl.multiple_of(s * SEQ, SEQ), SEQ)
        value = resid[rows, :]
        centred = value - jnp.mean(value, axis=1, keepdims=True)
        inverse = lax.rsqrt(jnp.mean(centred * centred, axis=1, keepdims=True) + norm_eps)
        scaled = centred * inverse
        h2[rows, :] = scaled
        inv[1, rows, :] = jnp.broadcast_to(inverse, (SEQ, 128))
        state = scaled * vecs[1:2, :] + vecs[7:8, :]
        live = lax.broadcasted_iota(jnp.int32, (SEQ, 768), 0) < lens_ref[s]
        mean_vec = jnp.sum(jnp.where(live, state, 0.0), axis=0, keepdims=True) / lens_ref[s].astype(f32)
        r = lax.rsqrt(jnp.sum(mean_vec * mean_vec, axis=1, keepdims=True) + pool_eps)
        pooled[s] = mean_vec * r
        rnorm[s] = jnp.broadcast_to(r, (1, 768))
        return 0

    lax.fori_loop(0, 8, norm_two_step, 0)
    save(h2, h2_out, 8)
    save(inv, inv_out, 9)

    sources = jnp.concatenate([pooled[2 * i] for i in range(4)], axis=0)
    targets = jnp.concatenate([pooled[2 * i + 1] for i in range(4)], axis=0)
    first = core == 0
    pad = jnp.zeros((4, 768), f32)
    pool_own[0] = jnp.concatenate([jnp.where(first, targets, sources), pad], axis=0)
    swap = pltpu.make_async_remote_copy(
        src_ref=pool_own.at[0], dst_ref=pool_swap, send_sem=swap_sem.at[0], recv_sem=swap_sem.at[1],
        device_id=device_at(spot, 1 - core), device_id_type=MESH,
    )
    swap.start()
    swap.wait()
    got = pool_swap[0:4, :]
    kind = jnp.concatenate(
        [jnp.where(first, sources, got), jnp.where(first, got, targets)], axis=0
    )
    q = Gather(pool_all, pool_send, pool_recv, spot, core, (1, 2, 0))
    for o in range(3):
        unit = jnp.concatenate([kind[:, 256 * o : 256 * o + 128], kind[:, 256 * o + 128 : 256 * o + 256]], axis=0)
        here = (pl.ds(spot[1], 1), pl.ds(spot[2], 1), pl.ds(spot[0], 1))
        pool_all[(0, core, o) + here] = unit.reshape(1, 1, 1, 16, 128)
    for o in range(3):
        q.begin(0, o, None)
    for o in range(3):
        q.pass_on(0, o)
    for o in range(3):
        q.first_done(0, o)
        q.spread(0, o, 1)
    for o in range(3):
        q.relay(0, o, 1)
    for o in range(3):
        q.finish(0, o, 1)
        q.spread(0, o, 2)
    for o in range(3):
        q.relay(0, o, 2)
    for o in range(3):
        q.finish(0, o, 2)
    for o in range(3):
        q.shared_done(0, o)

    for k, out in ((0, left3), (1, right3)):
        for o in range(3):
            for h in range(2):
                block = pool_all[0, k, o, :, :, :, 8 * h : 8 * h + 8, :].reshape(512, 128)
                high, low = split_low(block)
                at = 256 * o + 128 * h
                parts = (high, high, low) if k == 0 else (high, low, high)
                for i in range(3):
                    out[:, 768 * i + at : 768 * i + at + 128] = parts[i]
    pair_row = lax.broadcasted_iota(jnp.int32, (512, 256), 0)
    pair_col = lax.broadcasted_iota(jnp.int32, (512, 256), 1)
    names = lax.broadcasted_iota(jnp.int32, (16, 512), 0).astype(f32)
    member = (names == group_row).astype(bf)

    def column_lse(rows3, cols3, into):
        for p in range(2):
            cut = slice(256 * p, 256 * p + 256)
            scores = logit_scale * mm_nt(rows3[...], cols3[cut, :])
            scores = scores - jnp.where(pair_row == pair_col + 256 * p, logit_scale * margin, 0.0)
            alike = mm_tn(member, member[:, cut]) > 0.5
            scores = jnp.where(alike, scores, far_low)
            peak = jnp.max(scores, axis=0, keepdims=True)
            total = jnp.sum(jnp.exp(scores - peak), axis=0, keepdims=True)
            stats[into : into + 1, cut] = peak + jnp.log(total)

    column_lse(left3, right3, 0)
    column_lse(right3, left3, 1)
    chip = (spot[1] * RING + spot[2]) * RING + spot[0]
    mine = pl.ds(pl.multiple_of(chip * 8, 8), 8)
    weight = 1.0 / 1024.0
    at_row = lax.broadcasted_iota(jnp.int32, (8, 512), 0) + chip * 8
    at_col = lax.broadcasted_iota(jnp.int32, (8, 512), 1)
    own_pair = at_row == at_col
    first_rows = (lax.broadcasted_iota(jnp.int32, (16, 8), 0).astype(f32)).astype(bf)
    pick = (lax.broadcasted_iota(jnp.int32, (8, 512), 1) == at_row).astype(bf)
    own_member = mm_nt(pick, member)
    alike = mm(own_member.astype(bf), member) > 0.5
    grads = []
    terms = []
    for k, (rows3, cols3) in enumerate(((left3, right3), (right3, left3))):
        block = pool_all[0, k, :, pl.ds(spot[1], 1), pl.ds(spot[2], 1), pl.ds(spot[0], 1)]
        cut = [block[o, 0, 0, 0, 8 * h : 8 * h + 8, :] for o in range(3) for h in range(2)]
        own8 = jnp.concatenate(cut, axis=1)
        high, low = split_low(own8)
        parts = (high, high, low) if k == 0 else (high, low, high)
        scores = logit_scale * mm_nt(jnp.concatenate(parts, axis=1), cols3[...])
        scores = scores - jnp.where(own_pair, logit_scale * margin, 0.0)
        diagonal = jnp.sum(jnp.where(own_pair, scores, 0.0), axis=1, keepdims=True)
        scores = jnp.where(alike, scores, far_low)
        peak = jnp.max(scores, axis=1, keepdims=True)
        lse = peak + jnp.log(jnp.sum(jnp.exp(scores - peak), axis=1, keepdims=True))
        other = stats[k : k + 1, :]
        mix = weight * (jnp.exp(scores - lse) + jnp.exp(scores - other))
        mix = mix - jnp.where(own_pair, 2.0 * weight, 0.0)
        mix_high, mix_low = split_low(mix)
        high_at, low_at = (0, 768) if k == 0 else (0, 1536)
        high_cols, low_cols = cols3[:, high_at : high_at + 768], cols3[:, low_at : low_at + 768]
        grad = mm(mix_high, high_cols) + mm(mix_high, low_cols) + mm(mix_low, high_cols)
        grads.append(logit_scale * jnp.where(first, grad[0:4], grad[4:8]))
        terms.append(jnp.where(first, (lse - diagonal)[0:4], (lse - diagonal)[4:8]))
    lane = lax.broadcasted_iota(jnp.int32, (4, 128), 1)
    both = jnp.where(lane == 0, terms[0], jnp.where(lane == 1, terms[1], 0.0))
    loss_out[...] = jnp.concatenate([both, jnp.zeros((4, 128), f32)], axis=0)
    for s in range(8):
        d_row = grads[s % 2][s // 2 : s // 2 + 1, :]
        row = pooled[s]
        inner = jnp.sum(row * d_row, axis=1, keepdims=True)
        dpool_out[s] = rnorm[s] * (d_row - row * inner) / lens_ref[s].astype(f32)
    g.drain()
    q.drain()
    for copy in tile_sent:
        copy.wait_send()
    for copy in saves:
        copy.wait()


def forward_pass(lens, own, tile, x):
    bf, f32 = jnp.bfloat16, jnp.float32
    shapes = [
        ((3, 2, 3, RING, RING, RING, UNIT, 128), bf),
        ((16, 768), f32),
        ((512, 768), f32),
        ((512, 768), f32),
        ((2, 512, 128), f32),
        ((512, 768), bf),
        ((12, 512, 256), bf),
        ((12, 512, 256), f32),
        ((9, 512, 256), bf),
        ((8, 3, SEQ, 256), f32),
        ((3, 512, 256), bf),
        ((8, 1, 768), f32),
        ((8, 128), f32),
    ]
    anywhere = pl.BlockSpec(memory_space=pl.ANY)
    vmem = pl.BlockSpec(memory_space=pltpu.VMEM)
    dma = pltpu.SemaphoreType.DMA
    return pl.pallas_call(
        forward_kernel,
        out_shape=[jax.ShapeDtypeStruct(*s) for s in shapes],
        in_specs=[pl.BlockSpec(memory_space=pltpu.SMEM), vmem, vmem, vmem],
        out_specs=[anywhere] * 11 + [vmem] * 2,
        scratch_shapes=[
            pltpu.VMEM(*shapes[0]),
            pltpu.VMEM(*shapes[1]),
            pltpu.VMEM((RING, RING, 16, 128), bf),
            *[pltpu.VMEM(*s) for s in shapes[2:11]],
            pltpu.VMEM((512, 768), f32),
            pltpu.VMEM((8, 1, 768), f32),
            pltpu.VMEM((8, 1, 768), f32),
            pltpu.VMEM((1, 8, 768), f32),
            pltpu.VMEM((8, 768), f32),
            pltpu.VMEM((1, 2, 3, RING, RING, RING, 16, 128), f32),
            pltpu.VMEM((512, 2304), bf),
            pltpu.VMEM((512, 2304), bf),
            pltpu.VMEM((8, 512), f32),
            dma((3, 3, 18)),
            dma((3, 3, 18)),
            dma((3, 3)),
            dma((1, 3, 18)),
            dma((1, 3, 18)),
            dma((6,)),
            dma((6,)),
            dma((2,)),
            dma((3, 2, 3)),
            dma((10,)),
        ],
        compiler_params=pltpu.CompilerParams(
            collective_id=1, has_side_effects=True, vmem_limit_bytes=60 * 1024 * 1024
        ),
        name="forward_pass",
    )(lens, own.reshape(3, 3, 1, 1, 1, UNIT, 128), tile.reshape(1, 1, 16, 128), x)


class Reduce:
    def __init__(self, parts, bufs, out, send_sem, recv_sem, spot, core):
        self.parts, self.bufs, self.out = parts, bufs, out
        self.send_sem, self.recv_sem = send_sem, recv_sem
        self.spot, self.core = spot, core
        self.sent = []

    def copy(self, src, dst, r, o, event, there, core):
        copy = pltpu.make_async_remote_copy(
            src_ref=src,
            dst_ref=dst,
            send_sem=self.send_sem.at[r, o, event],
            recv_sem=self.recv_sem.at[r, o, event],
            device_id=device_at(there, core),
            device_id_type=MESH,
        )
        copy.start()
        self.sent.append(copy)

    def landed(self, dst, r, o, event):
        pltpu.make_async_copy(dst, dst, self.recv_sem.at[r, o, event]).wait()

    def spans(self, o, phase, at, half=None):
        order = ORDERS[o]
        spans = {}
        for k, d in enumerate(order):
            if k < phase:
                spans[d] = (self.spot[d], 1)
            elif k == phase:
                spans[d] = (at, 1)
            else:
                spans[d] = (0, RING)
        if half is not None:
            spans[order[phase + 1]] = (2 * half, 2)
        return spans

    def mine(self, r, o, spans):
        return block_of(self.parts, r, self.core, o, spans)

    def slot(self, r, o, phase, which):
        return self.bufs[(o * 3 + phase) * 2 + which // 2].at[r, which % 2]

    def add_into(self, into, others):
        sizes = into.shape[:3]

        def one(i, _):
            at = (i // sizes[1], i % sizes[1])
            if len(others) == 1:
                into[at] = into[at] + others[0][at]
            else:
                value = into[at].astype(jnp.float32)
                for other in others:
                    value = value + other[at].astype(jnp.float32)
                into[at] = value.astype(jnp.bfloat16)
            return 0

        lax.fori_loop(0, sizes[0] * sizes[1], one, 0)

    def first(self, r, o, phase):
        d = ORDERS[o][phase]
        across = (self.spot[d] + 2) % RING
        event = 1 + 4 * phase
        if phase < 2:
            for half, by in ((0, 1), (1, -1)):
                src = self.mine(r, o, self.spans(o, phase, across, half))
                self.copy(src, self.slot(r, o, phase, half), r, o, event + half, moved(self.spot, d, by), self.core)
        else:
            src = self.mine(r, o, self.spans(o, phase, across))
            self.copy(src, self.slot(r, o, phase, 0), r, o, event, moved(self.spot, d, 1), self.core)

    def second(self, r, o, phase):
        d = ORDERS[o][phase]
        event = 1 + 4 * phase
        for half, by in ((0, 1), (1, -1)):
            at = (self.spot[d] + by) % RING
            if phase < 2 or half == 0:
                view = self.slot(r, o, phase, half)
                self.landed(view, r, o, event + half)
                self.add_into(self.mine(r, o, self.spans(o, phase, at, half if phase < 2 else None)), [view])
            src = self.mine(r, o, self.spans(o, phase, at))
            self.copy(src, self.slot(r, o, phase, 2 + half), r, o, event + 2 + half, moved(self.spot, d, by), self.core)

    def third(self, r, o, phase):
        d = ORDERS[o][phase]
        event = 1 + 4 * phase
        a, b = self.slot(r, o, phase, 2), self.slot(r, o, phase, 3)
        self.landed(a, r, o, event + 2)
        self.landed(b, r, o, event + 3)
        here = self.mine(r, o, self.spans(o, phase, self.spot[d]))
        if phase < 2:
            self.add_into(here, [a, b])
        else:
            total = here[0, 0, 0].astype(jnp.float32) + a[0, 0, 0].astype(jnp.float32)
            self.out[r, o] = total + b[0, 0, 0].astype(jnp.float32)


def reduce_buffers(rounds):
    bufs = []
    for o in range(3):
        for phase in range(3):
            order = ORDERS[o]
            sizes = [RING] * 3
            for k in range(phase + 1):
                sizes[order[k]] = 1
            half = list(sizes)
            if phase < 2:
                half[order[phase + 1]] = 2
            for s in (half, sizes):
                bufs.append(pltpu.VMEM((rounds, 2, *s, UNIT, 128), jnp.bfloat16))
    return bufs


def norm_back(grad, scaled, inverse, gain):
    e = grad * gain
    mean_e = jnp.mean(e, axis=1, keepdims=True)
    mean_eh = jnp.mean(e * scaled, axis=1, keepdims=True)
    return inverse * (e - mean_e - scaled * mean_eh)


def backward_kernel(
    lens_ref, vec_ref, dpool_ref, x_ref,
    w_in, h1_in, h2_in, inv_in, nl_in, act_in, gp_in, qkv_in, prob_in, ctx_in,
    token_out, low_out, red_out, vec_out,
    w, h1, h2, inv, nl, act, gp, qkv, prob, ctx, parts, d2d, d_res, d_low, turned, dvec, vec_slots, *rest,
):
    bufs = rest[:18]
    send_sem, recv_sem, swap_send, swap_recv, free_sem, vec_send, vec_recv, load_sem, gp_sem, w_sem = rest[18:]
    spot, core = where_am_i()
    bf, f32 = jnp.bfloat16, jnp.float32

    def load(src, dst, at):
        copy = pltpu.make_async_copy(src, dst, load_sem.at[at])
        copy.start()
        return copy

    def load_w(r, at):
        copy = pltpu.make_async_copy(w_in.at[r], w.at[at], w_sem.at[r])
        copy.start()
        return copy

    def load_gp(y, at):
        return pltpu.make_async_copy(gp_in.at[pl.ds(3 * y, 3)], gp.at[at], gp_sem.at[at])

    get_h2, get_inv = load(h2_in, h2, 0), load(inv_in, inv, 1)
    get_act = load(act_in, act, 2)
    get_w2 = load_w(2, 0)
    load_gp(0, 0).start()
    load_gp(1, 1).start()
    get_nl = load(nl_in, nl, 3)
    get_w1 = load_w(1, 1)
    get_h1, get_ctx = load(h1_in, h1, 4), load(ctx_in, ctx, 5)
    get_qkv, get_prob = load(qkv_in, qkv, 6), load(prob_in, prob, 7)
    greet(spot, core)
    red = Reduce(parts, bufs, red_out, send_sem, recv_sem, spot, core)
    swaps = {}

    def give(r):
        if r == 0:
            pl.semaphore_wait(free_sem, 1)
        for o in range(3):
            copy = pltpu.make_async_remote_copy(
                src_ref=parts.at[r, 1 - core, o], dst_ref=d2d.at[r % 2, o],
                send_sem=swap_send.at[r, o], recv_sem=swap_recv.at[r, o],
                device_id=device_at(spot, 1 - core), device_id_type=MESH,
            )
            copy.start()
            red.sent.append(copy)

    def take(r):
        for o in range(3):
            view = d2d.at[r % 2, o]
            pltpu.make_async_copy(view, view, swap_recv.at[r, o]).wait()
            red.add_into(parts.at[r, core, o], [view])
            red.first(r, o, 0)
        if r == 2:
            pl.semaphore_signal(free_sem, inc=1, device_id=device_at(spot, 1 - core), device_id_type=MESH)

    def second(r, phase):
        for o in range(3):
            red.second(r, o, phase)

    def third(r, phase):
        for o in range(3):
            red.third(r, o, phase)
            if phase < 2:
                red.first(r, o, phase + 1)

    dvec[0] = jnp.zeros((16, 768), f32)

    def add_vec(row, value):
        dvec[0, row : row + 1, :] = dvec[0, row : row + 1, :] + value

    def total(value):
        return jnp.sum(value, axis=0, keepdims=True)

    get_h2.wait()
    get_inv.wait()

    def norm_two_step(s, _):
        rows = pl.ds(pl.multiple_of(s * SEQ, SEQ), SEQ)
        live = lax.broadcasted_iota(jnp.int32, (SEQ, 768), 0) < lens_ref[s]
        grad = jnp.where(live, jnp.broadcast_to(dpool_ref[s], (SEQ, 768)), 0.0)
        scaled = h2[rows, :]
        inverse = inv[1, rows, 0:1]
        back = norm_back(grad, scaled, inverse, vec_ref[1:2, :])
        low = back.astype(bf)
        d_res[rows, :] = back
        d_low[rows, :] = low
        add_vec(1, total(grad * scaled))
        add_vec(7, total(grad))
        add_vec(6, total(low.astype(f32)))
        return 0

    lax.fori_loop(0, 8, norm_two_step, 0)
    get_act.wait()

    def down_step(y, _):
        hidden = jnp.concatenate([act[3 * y], act[3 * y + 1], act[3 * y + 2]], axis=1)
        turned[...] = hidden.T
        for p in range(3):
            block = mm(turned[...], d_low[:, 256 * p : 256 * p + 256]).astype(bf)
            for k in range(2):
                cb = 2 * p + k
                for z in range(RING):
                    for x in range(RING):
                        at = UNIT * (RING * z + x)
                        parts[2, cb // 3, cb % 3, x, y, z] = block[at : at + UNIT, 128 * k : 128 * k + 128]
        return 0

    lax.fori_loop(0, RING, down_step, 0)
    give(2)
    get_w2.wait()

    def pre_step(y, _):
        at = y % 2
        load_gp(y, at).wait()
        columns = [
            jnp.concatenate([w[0, cb // 3, cb % 3, x, y, z] for z in range(RING) for x in range(RING)], axis=0)
            for cb in range(6)
        ]
        weight = jnp.concatenate(columns, axis=1)
        for j in range(3):
            grad = mm_nt(d_low[...], weight[256 * j : 256 * j + 256, :]) * gp[at, j]
            low = grad.astype(bf)
            act[3 * y + j] = low
            cut = slice(256 * j, 256 * j + 256)
            dvec[0, pl.ds(8 + y, 1), cut] = total(low.astype(f32))

        @pl.when(y < 2)
        def _():
            load_gp(y + 2, at).start()

        return 0

    lax.fori_loop(0, RING, pre_step, 0)
    get_w0 = load_w(0, 0)
    take(2)
    get_nl.wait()
    turned_nl = nl[...].T
    turned[:, :] = turned_nl

    def up_step(n2, _):
        block = mm(turned[...], act[n2]).astype(bf)
        c, o, x = n2 // 6, n2 // 2 % 3, n2 % 2 * 2
        for k in range(2):
            parts[1, c, o, x + k] = block[:, 128 * k : 128 * k + 128].reshape(RING, RING, UNIT, 128)
        return 0

    lax.fori_loop(0, 12, up_step, 0)
    give(1)
    second(2, 0)
    get_w1.wait()

    def six_blocks(at, n):
        blocks = []
        for k in range(6):
            m = n + k
            blocks.append(w[at, m // 12, m // 4 % 3, m % 4].reshape(768, 128))
        return jnp.concatenate(blocks, axis=1)

    def up_back_step(t, _):
        low = jnp.concatenate([act[3 * t], act[3 * t + 1], act[3 * t + 2]], axis=1)
        weight = six_blocks(1, 6 * t)
        for p in range(3):
            cut = slice(256 * p, 256 * p + 256)
            d_res[:, cut] = d_res[:, cut] + mm_nt(low, weight[cut, :])
        return 0

    lax.fori_loop(0, RING, up_back_step, 0)
    take(1)
    third(2, 0)
    get_h1.wait()

    def norm_one_step(s, _):
        rows = pl.ds(pl.multiple_of(s * SEQ, SEQ), SEQ)
        grad, scaled = d_res[rows, :], h1[rows, :]
        back = norm_back(grad, scaled, inv[0, rows, 0:1], vec_ref[0:1, :])
        low = back.astype(bf)
        d_res[rows, :] = back
        d_low[rows, :] = low
        add_vec(0, total(grad * scaled))
        add_vec(5, total(grad))
        add_vec(4, total(low.astype(f32)))
        return 0

    lax.fori_loop(0, 8, norm_one_step, 0)
    second(1, 0)
    get_ctx.wait()
    turned[...] = jnp.concatenate([ctx[0], ctx[1], ctx[2]], axis=1).T
    get_w0.wait()
    weight = six_blocks(0, 18)
    for p in range(3):
        cut = slice(256 * p, 256 * p + 256)
        block = mm(turned[...], d_low[:, cut]).astype(bf)
        for k in range(2):
            n = 18 + 2 * p + k
            parts[0, n // 12, n // 4 % 3, n % 4] = block[:, 128 * k : 128 * k + 128].reshape(RING, RING, UNIT, 128)
        ctx[p] = mm_nt(d_low[...], weight[cut, :]).astype(bf)
    second(2, 1)
    third(1, 0)
    get_qkv.wait()
    get_prob.wait()
    mask = head_mask()

    def attend_back(s, _):
        rows = pl.ds(pl.multiple_of(s * SEQ, SEQ), SEQ)
        for p in range(3):
            query, key_part, value = qkv[p, rows, :], qkv[3 + p, rows, :], qkv[6 + p, rows, :]
            wide_grad = spread_heads(ctx[p, rows, :], mask)
            probs = prob[s, p]
            d_value = mm(probs.astype(bf), wide_grad)
            d_probs = mm_nt(value, wide_grad)
            centre = jnp.sum(probs * d_probs, axis=0, keepdims=True)
            d_scores = (probs * (d_probs - centre)).astype(bf)
            d_query = gather_heads(mm_tn(d_scores, key_part), mask) * 0.125
            d_key = mm(d_scores, spread_heads(query, mask)) * 0.125
            low_query, low_value = d_query.astype(bf), d_value.astype(bf)
            qkv[p, rows, :] = low_query
            qkv[3 + p, rows, :] = d_key.astype(bf)
            qkv[6 + p, rows, :] = low_value
            cut = slice(256 * p, 256 * p + 256)
            dvec[0, 2:3, cut] = dvec[0, 2:3, cut] + total(low_query.astype(f32))
            dvec[0, 3:4, cut] = dvec[0, 3:4, cut] + total(low_value.astype(f32))
        return 0

    lax.fori_loop(0, 8, attend_back, 0)
    vec_sent = []

    def vec_push(event, src, there, c):
        copy = pltpu.make_async_remote_copy(
            src_ref=src, dst_ref=vec_slots.at[event], send_sem=vec_send.at[event], recv_sem=vec_recv.at[event],
            device_id=device_at(there, c), device_id_type=MESH,
        )
        copy.start()
        vec_sent.append(copy)

    def vec_landed(event):
        ref = vec_slots.at[event]
        pltpu.make_async_copy(ref, ref, vec_recv.at[event]).wait()

    def vec_start(d):
        vec_push(1 + 3 * d, dvec.at[d + 1], moved(spot, d, 1), core)
        vec_push(2 + 3 * d, dvec.at[d + 1], moved(spot, d, -1), core)

    def vec_relay(d):
        vec_landed(1 + 3 * d)
        vec_push(3 + 3 * d, vec_slots.at[1 + 3 * d], moved(spot, d, 1), core)

    def vec_add(d):
        vec_landed(2 + 3 * d)
        vec_landed(3 + 3 * d)
        sides = vec_slots[1 + 3 * d] + vec_slots[2 + 3 * d]
        dvec[d + 2] = (dvec[d + 1] + sides) + vec_slots[3 + 3 * d]

    vec_push(0, dvec.at[0], spot, 1 - core)
    turned[...] = x_ref[...].T

    def qkv_step(n2, _):
        block = mm(turned[...], qkv[n2]).astype(bf)
        c, o, x = n2 // 6, n2 // 2 % 3, n2 % 2 * 2
        for k in range(2):
            parts[0, c, o, x + k] = block[:, 128 * k : 128 * k + 128].reshape(RING, RING, UNIT, 128)
        return 0

    lax.fori_loop(0, 9, qkv_step, 0)
    give(0)
    third(2, 1)
    second(1, 1)
    vec_landed(0)
    dvec[1] = dvec[0] + vec_slots[0]
    vec_start(0)

    def input_step(t, _):
        low = jnp.concatenate([qkv[3 * t], qkv[3 * t + 1], qkv[3 * t + 2]], axis=1)
        weight = six_blocks(0, 6 * t)
        for p in range(3):
            cut = slice(256 * p, 256 * p + 256)
            d_res[:, cut] = d_res[:, cut] + mm_nt(low, weight[cut, :])
        return 0

    lax.fori_loop(0, 3, input_step, 0)
    token_copy = pltpu.make_async_copy(d_res, token_out, load_sem.at[8])
    token_copy.start()
    d_low[...] = d_res[...].astype(bf)
    low_copy = pltpu.make_async_copy(d_low, low_out, load_sem.at[9])
    low_copy.start()
    take(0)
    vec_relay(0)
    third(1, 1)
    second(2, 2)
    vec_add(0)
    vec_start(1)
    second(0, 0)
    vec_relay(1)
    second(1, 2)
    third(2, 2)
    third(0, 0)
    vec_add(1)
    vec_start(2)
    second(0, 1)
    vec_relay(2)
    third(1, 2)
    third(0, 1)
    vec_add(2)
    vec_out[...] = dvec[4]
    second(0, 2)
    third(0, 2)
    token_copy.wait()
    low_copy.wait()
    for copy in red.sent + vec_sent:
        copy.wait_send()


def backward_pass(lens, vectors, d_pool, x, w, h1, h2, inv, nl, act, gp, qkv, prob, ctx):
    bf, f32 = jnp.bfloat16, jnp.float32
    anywhere = pl.BlockSpec(memory_space=pl.ANY)
    vmem = pl.BlockSpec(memory_space=pltpu.VMEM)
    dma = pltpu.SemaphoreType.DMA
    scratch = [
        pltpu.VMEM((2, *w.shape[1:]), bf),
        pltpu.VMEM(h1.shape, f32),
        pltpu.VMEM(h2.shape, f32),
        pltpu.VMEM(inv.shape, f32),
        pltpu.VMEM(nl.shape, bf),
        pltpu.VMEM(act.shape, bf),
        pltpu.VMEM((2, 3, 512, 256), f32),
        pltpu.VMEM(qkv.shape, bf),
        pltpu.VMEM(prob.shape, f32),
        pltpu.VMEM(ctx.shape, bf),
        pltpu.VMEM(w.shape, bf),
        pltpu.VMEM((2, *w.shape[2:]), bf),
        pltpu.VMEM((512, 768), f32),
        pltpu.VMEM((512, 768), bf),
        pltpu.VMEM((768, 512), bf),
        pltpu.VMEM((5, 16, 768), f32),
        pltpu.VMEM((10, 16, 768), f32),
        *reduce_buffers(3),
        dma((3, 3, 13)),
        dma((3, 3, 13)),
        dma((3, 3)),
        dma((3, 3)),
        pltpu.SemaphoreType.REGULAR,
        dma((10,)),
        dma((10,)),
        dma((10,)),
        dma((2,)),
        dma((3,)),
    ]
    return pl.pallas_call(
        backward_kernel,
        out_shape=[
            jax.ShapeDtypeStruct((512, 768), f32),
            jax.ShapeDtypeStruct((512, 768), bf),
            jax.ShapeDtypeStruct((3, 3, UNIT, 128), f32),
            jax.ShapeDtypeStruct((16, 768), f32),
        ],
        in_specs=[pl.BlockSpec(memory_space=pltpu.SMEM), vmem, vmem, vmem] + [anywhere] * 10,
        out_specs=[anywhere, anywhere, vmem, vmem],
        scratch_shapes=scratch,
        compiler_params=pltpu.CompilerParams(
            collective_id=2, has_side_effects=True, vmem_limit_bytes=63 * 1024 * 1024
        ),
        name="backward_pass",
    )(lens, vectors, d_pool, x, w, h1, h2, inv, nl, act, gp, qkv, prob, ctx)


def own_units(w_qkv, w_out, w_up, w_down, gains, biases, groups, core):
    first = jnp.concatenate([w_qkv, w_out], axis=1)
    both = jnp.stack([first, w_up]).reshape(2, 6, 2, 3, RING, 128)
    out_going = both.transpose(4, 2, 0, 3, 1, 5).reshape(8, 36, 128)
    extra = jnp.concatenate([gains.reshape(-1), biases.reshape(-1), groups.astype(jnp.bfloat16)])
    extra = jnp.broadcast_to(jnp.pad(extra, (0, 52))[None, None], (8, 1, 128))
    out_going = jnp.concatenate([out_going, extra], axis=1)
    rows = lax.all_to_all(out_going, "narrow", split_axis=0, concat_axis=0, tiled=True)
    units = rows[:, :36].reshape(8, 2, 3, 6, 128).transpose(1, 2, 0, 3, 4).reshape(2, 3, UNIT, 128)
    vectors = rows[:, 36, :72].reshape(8, 12, 6).transpose(1, 0, 2).reshape(12, UNIT)
    named = rows[:, 36, 72:76].reshape(1, 32)
    tile = jnp.concatenate(
        [jnp.pad(vectors, ((0, 0), (0, 80))), jnp.pad(named, ((0, 3), (0, 96)))], axis=0
    )
    halves = w_down.reshape(24, 2, 3, 128).transpose(1, 2, 0, 3)
    keep = lax.dynamic_index_in_dim(halves, core, 0, keepdims=False)
    give = lax.dynamic_index_in_dim(halves, 1 - core, 0, keepdims=False)
    got = swapped(give)
    low_rows = jnp.where(core == 0, keep, got)
    high_rows = jnp.where(core == 0, got, keep)
    down = jnp.concatenate([low_rows, high_rows], axis=1)
    return jnp.concatenate([units, down[None]], axis=0), tile


def swapped(value):
    return lax.ppermute(value, "narrow", [(i, i ^ 1) for i in range(8)])


def own_rows(reduced, core):
    out_going = reduced[:2].reshape(2, 3, 8, 6, 128).transpose(2, 0, 1, 3, 4)
    rows = lax.all_to_all(out_going, "narrow", split_axis=0, concat_axis=0, tiled=True)
    rows = rows.reshape(RING, 2, 2, 3, 6, 128).transpose(2, 4, 1, 3, 0, 5).reshape(2, 6, 3072)
    halves = reduced[2].reshape(3, 2, 24, 128).transpose(1, 0, 2, 3)
    keep = lax.dynamic_index_in_dim(halves, core, 0, keepdims=False)
    give = lax.dynamic_index_in_dim(halves, 1 - core, 0, keepdims=False)
    got = swapped(give)
    low_cols = jnp.where(core == 0, keep, got)
    high_cols = jnp.where(core == 0, got, keep)
    down = jnp.concatenate([low_cols, high_cols]).transpose(1, 0, 2).reshape(24, 768)
    return rows[0, :, :2304], rows[0, :, 2304:], rows[1], down


def shards(token_ids, lengths, groups, table, w_qkv, w_out, w_up, w_down, gains, biases):
    pair_count = token_ids.shape[0]
    vocab_rows = table.shape[0]
    model_width = table.shape[1]
    flat_ids = token_ids.reshape(-1)
    token_count = flat_ids.shape[0]
    device_total = lax.axis_size(("wide", "narrow"))
    rank_at = lax.axis_index(("wide", "narrow"))
    slot_cap = max(2, 2 * token_count // device_total)
    owner_of = flat_ids // vocab_rows
    local_of = flat_ids - owner_of * vocab_rows
    owner_hits = (owner_of[:, None] == jnp.arange(device_total)[None, :]).astype(jnp.int32)
    rank_in = jnp.sum(jnp.cumsum(owner_hits, axis=0) * owner_hits, axis=1) - 1
    slot_of = owner_of * slot_cap + rank_in
    id_slots = jnp.full((device_total * slot_cap,), -1, jnp.int32).at[slot_of].set(local_of)
    id_slots = id_slots.reshape(device_total, slot_cap)
    asked = lax.all_to_all(id_slots, ("wide", "narrow"), split_axis=0, concat_axis=0, tiled=True)
    valid = asked >= 0
    found = jnp.take(table, jnp.clip(asked, 0, vocab_rows - 1), axis=0)
    found = jnp.where(valid[..., None], found, jnp.zeros((), table.dtype))
    returned = lax.all_to_all(found, ("wide", "narrow"), split_axis=0, concat_axis=0, tiled=True)
    sent_lengths = lengths.reshape(-1)

    core = lax.axis_index("narrow") % 2
    own, tile = own_units(w_qkv[0], w_out[0], w_up[0], w_down[0], gains[0], biases[0], groups, core)
    x_low = returned.reshape(-1, model_width)[slot_of]
    kept = forward_pass(sent_lengths, own, tile, x_low)
    gathered, vectors, h1, h2, inv, norm_low, act, gate, qkv, prob, ctx, d_pool, loss_tile = kept
    loss_terms = loss_tile[:4, :2]
    token_grads, sent_rows, reduced, d_vectors = backward_pass(
        sent_lengths, vectors, d_pool, x_low, gathered, h1, h2, inv, norm_low, act, gate, qkv, prob, ctx
    )
    d_matrices = own_rows(reduced, core)
    d_vectors = lax.dynamic_slice_in_dim(d_vectors[:12], rank_at * 6, 6, 1)
    grad_slots = (
        jnp.zeros((device_total * slot_cap, model_width), jnp.bfloat16).at[slot_of].set(sent_rows)
    )
    grad_slots = grad_slots.reshape(device_total, slot_cap, model_width)
    arrived = lax.all_to_all(
        grad_slots, ("wide", "narrow"), split_axis=0, concat_axis=0, tiled=True
    )
    target_slot = jnp.where(asked >= 0, asked, vocab_rows).reshape(-1)
    table_grads = (
        jnp.zeros((vocab_rows, model_width), jnp.float32)
        .at[target_slot]
        .add(arrived.reshape(-1, model_width).astype(jnp.float32), mode="drop")
    )
    token_grads = token_grads.reshape(pair_count, 2, SEQ, model_width)
    return (
        loss_terms,
        token_grads,
        table_grads,
        d_matrices[0][None],
        d_matrices[1][None],
        d_matrices[2][None],
        d_matrices[3][None],
        d_vectors[None, :2],
        d_vectors[None, 2:],
    )


def solution(mesh):
    in_specs = (
        P(("wide", "narrow"), None, None),
        P(("wide", "narrow"), None),
        P(("wide", "narrow")),
        P(("wide", "narrow"), None),
        P(None, ("wide", "narrow"), None),
        P(None, ("wide", "narrow"), None),
        P(None, ("wide", "narrow"), None),
        P(None, ("wide", "narrow"), None),
        P(None, None, ("wide", "narrow")),
        P(None, None, ("wide", "narrow")),
    )
    out_specs = (
        P(("wide", "narrow"), None),
        P(("wide", "narrow"), None, None, None),
        P(("wide", "narrow"), None),
        P(None, ("wide", "narrow"), None),
        P(None, ("wide", "narrow"), None),
        P(None, ("wide", "narrow"), None),
        P(None, ("wide", "narrow"), None),
        P(None, None, ("wide", "narrow")),
        P(None, None, ("wide", "narrow")),
    )
    return jax.shard_map(shards, mesh=mesh, in_specs=in_specs, out_specs=out_specs, check_vma=False)
```

time: 698 us -> 325 us (0.47); the launches traced: 689 us -> 324 us
  blocking collectives: 175 us -> 0 us
  local copies, waits for them, and re-layouts: 198 us -> 32.9 us
  matrix products: 81.2 us -> 0 us
  Pallas kernels: 142 us -> 188 us
  waiting for transfers between devices: 0.58 us -> 45.1 us
  other arithmetic: 53.1 us -> 18.3 us
    reshape x19 -> x3, local copies, waits for them, and re-layouts: 90.5 us -> 0.7 us  [the longest x1 0.6 us: shards(): sent_lengths = lengths.reshape(-1)]
    dot_general x21 -> x0, matrix products: 81.2 us -> none  [the longest x4 22.4 us: contract_cols(): lax.dot_general(first_part, second_part, (((1,), (1,)), ((), ())), prefer...]
    psum x1 -> x0, blocking collectives: 74.1 us -> none  [shards(): d_vectors = lax.psum(jnp.concatenate(layer_grads[4:]), everywhere)]
    unnamed x1 -> x0, blocking collectives: 63.8 us -> none
    pallas_call x3 -> x2, Pallas kernels: 142 us -> 188 us  [the longest x1 111 us: forward_pass(): pl.pallas_call(forward_kernel, out_shape=[jax.ShapeDtypeStruct(*s) for s...]
    transpose x6 -> x2, local copies, waits for them, and re-layouts: 38 us -> 0.07 us  [the longest x1 0.06 us: own_units(): rows[:, :36].reshape(8, 2, 3, 6, 128).transpose(1, 2, 0, 3, 4)]
    all_gather x1 -> x0, blocking collectives: 36.9 us -> none  [shards(): lax.all_gather(jnp.concatenate([gains[0], biases[0]]), everywhere, axis=1...]
    convert_element_type x7 -> x0, local copies, waits for them, and re-layouts: 23.3 us -> none  [the longest x2 14.4 us: layer_backward(): d_qkv = jnp.stack([d_query, d_key, d_value], axis=2).reshape(-1, 3 * mode...]
  transfers between devices with their start and end apart: 7 -> 7, of which waited for: 1 -> 5; matrix products, arithmetic and copies ran while one was open for 14% -> 8% of each run, Pallas kernels for 9% -> 0%
where the time goes in v2:
time: 325 us; the launch traced here: 324 us
  Pallas kernels  188 us (58%)
  waiting for transfers between devices  45.1 us (14%)
  starting transfers between devices  38.6 us (12%)
  local copies, waits for them, and re-layouts  32.9 us (10%)
  other arithmetic  18.3 us (6%)
    pallas_call x1, Pallas kernels, forward_pass(): pl.pallas_call(forward_kernel, out_shape=[jax.ShapeDtypeStruct(*s) for s...  111 us
    pallas_call x1, Pallas kernels, backward_pass(): pl.pallas_call(backward_kernel, out_shape=[jax.ShapeDtypeStruct((512, 768...  76.3 us
    all_to_all x1, waiting for transfers between devices, shards(): lax.all_to_all(found, ('wide', 'narrow'), split_axis=0, concat_axis=0, ti...  21 us
    all_to_all x1, waiting for transfers between devices, shards(): lax.all_to_all(grad_slots, ('wide', 'narrow'), split_axis=0, concat_axis=...  14.8 us
    scatter-add x1, other arithmetic, shards(): table_grads = jnp.zeros((vocab_rows, model_width), jnp.float32).at[target...  12.6 us
    all_to_all x1, starting transfers between devices, shards(): lax.all_to_all(id_slots, ('wide', 'narrow'), split_axis=0, concat_axis=0,...  11.5 us
    all_to_all x1, waiting for transfers between devices, shards(): lax.all_to_all(id_slots, ('wide', 'narrow'), split_axis=0, concat_axis=0,...  8.05 us
    all_to_all x1, starting transfers between devices, own_rows(): lax.all_to_all(out_going, 'narrow', split_axis=0, concat_axis=0, tiled=True)  8.01 us
  transfers between devices with their start and end apart: 7, of which 5 were waited for; matrix products, arithmetic and copies ran while one was open for 8% of the time, Pallas kernels for 0%

profile of v2, /device:TPU:1, one launch (start us, length us, event | category | flops | bytes accessed | tf_op | source)
XLA Modules:
  0.0 323.8 jit_solution(6562539733918149755)
XLA Ops:
  0.7 0.7 compare_and_fusion
  1.5 0.1 and.41
  1.5 0.1 and.39
  1.6 0.8 reshape.267
  2.4 0.7 broadcast_divide_fusion
  3.1 0.1 div.28
  3.2 0.1 div.26
  3.3 0.1 copy.78
  3.4 0.2 fusion.8
  3.7 0.2 fusion.7
  4.0 2.4 scatter_custom_fusion
  6.4 0.7 all_to_all.21
  7.1 11.5 %all-to-all-start.1 = ((s32[128,1,8]{2,1,0:T(1,128)}), s32[128,1,8]{2,1,0:T(1,128)S(1)}, u32[]{:S(2)}, u32[]{:S(2)}) async-start(s32[128,1,8]{2,1,0:T(1,128)} %bitcast.21), calls=%async_computation.1 | async-start | bytes 131072 | tf_op jit(solution)/shard_map/all_to_all | solution.py:1132
  18.7 0.1 reshape_squeeze.18
  18.8 0.1 copy.70
  18.9 0.1 reshape_squeeze.19
  19.2 0.1 pad_maximum_fusion.1
  19.4 0.7 copy.71
  20.0 8.0 %all-to-all-done.1 = s32[128,1,8]{2,1,0:T(1,128)S(1)} async-done(((s32[128,1,8]{2,1,0:T(1,128)}), s32[128,1,8]{2,1,0:T(1,128)S(1)}, u32[]{:S(2)}, u32[]{:S(2)}) %all-to-all-start.1) | async-done | bytes 4128 | tf_op jit(solution)/shard_map/all_to_all | solution.py:1132
  28.1 4.1 %all-to-all-start = ((bf16[8,37,128]{2,1,0:T(8,128)(2,1)}), bf16[8,37,128]{2,1,0:T(8,128)(2,1)S(1)}, u32[]{:S(2)}, u32[]{:S(2)}) async-start(bf16[8,37,128]{2,1,0:T(8,128)(2,1)} %copy.71), calls=%async_computation | async-start | bytes 163840 | tf_op jit(solution)/shard_map/all_to_all | solution.py:1081
  32.3 0.1 copy.82
  32.4 0.1 copy.84
  32.6 0.1 copy.85
  32.7 0.1 reshape.278
  32.8 8.0 %gather_fusion = bf16[1024,768]{1,0:T(8,128)(2,1)S(1)} fusion(bf16[3920,768]{1,0:T(8,128)(2,1)} %param.13, s32[1024]{0:T(1024)S(1)} %broadcast_clamp_fusion), kind=kCustom, calls=%fused_computation | custom fusion | bytes 3149824 | tf_op jit(solution)/shard_map/jit(_take)/gather | solution.py:1134
  40.7 1.4 fusion.4
  42.1 5.9 %all-to-all-start.2 = ((bf16[128,8,768]{2,1,0:T(8,128)(2,1)}), bf16[128,8,768]{2,1,0:T(8,128)(2,1)S(1)}, u32[]{:S(2)}, u32[]{:S(2)}) async-start(bf16[128,8,768]{2,1,0:T(8,128)(2,1)} %fusion.4), calls=%async_computation.2 | async-start | bytes 3145728 | tf_op jit(solution)/shard_map/all_to_all | solution.py:1136
  48.1 1.1 collective-permute-start
  49.2 0.1 copy.67
  49.3 0.6 reshape.260.lens_ref
  49.9 0.1 collective-permute-done
  50.1 0.1 slice_reduce_fusion
  50.2 0.1 reshape_squeeze.22
  50.3 0.1 reshape_squeeze.21
  50.4 0.1 reshape.265
  50.6 0.6 fusion.14.tile_ref
  51.2 0.7 maximum_bitcast_fusion.own_ref
  51.9 21.0 %all-to-all-done.2 = bf16[128,8,768]{2,1,0:T(8,128)(2,1)S(1)} async-done(((bf16[128,8,768]{2,1,0:T(8,128)(2,1)}), bf16[128,8,768]{2,1,0:T(8,128)(2,1)S(1)}, u32[]{:S(2)}, u32[]{:S(2)}) %all-to-all-start.2) | async-done | bytes 1572896 | tf_op jit(solution)/shard_map/all_to_all | solution.py:1136
  72.9 2.7 gather_fusion.1
  75.6 111.5 %forward_pass.1 = (bf16[3,2,3,4,4,4,48,128]{7,6,5,4,3,2,1,0:T(8,128)(2,1)}, f32[16,768]{1,0:T(8,128)}, f32[512,768]{1,0:T(8,128)}, f32[512,768]{1,0:T(8,128)}, f...) custom-call(s32[8]{0:T(128)} %reshape.260.lens_ref, ...), custom_call_target="tpu_custom_call" | custom-call | tf_op jit(solution)/shard_map/forward_pass/pallas_call | solution.py:551
  187.1 76.3 %backward_pass.1 = (f32[512,768]{1,0:T(8,128)}, bf16[512,768]{1,0:T(8,128)(2,1)}, f32[3,3,48,128]{3,2,1,0:T(8,128)}, f32[16,768]{1,0:T(8,128)}) custom-call(s32[8]{0:T(128)} %reshape.260.lens_ref, f32[16,768]{1,0:T(8,128)} %get-tuple-element.27.vec_ref, f32[8,1,768]{2,1,0:T(1,128)} %get-tuple-element.28.dpool_ref, bf16[512,768]{1,0:T(8,128)(2,1)} %gather_fusion.1, ...), custom_call_target="tpu_custom_call" | custom-call | tf_op jit(solution)/shard_map/backward_pass/pallas_call | solution.py:1056
  263.4 0.9 slice.51
  264.4 0.7 copy.87
  265.1 8.0 %all-to-all-start.4 = ((f32[8,2,3,6,128]{4,1,3,2,0:T(2,128)}), f32[8,2,3,6,128]{4,1,3,2,0:T(2,128)S(1)}, u32[]{:S(2)}, u32[]{:S(2)}) async-start(f32[8,2,3,6,128]{4,1,3,2,0:T(2,128)} %copy.87), calls=%async_computation.4 | async-start | bytes 294912 | tf_op jit(solution)/shard_map/all_to_all | solution.py:1104
  273.1 4.4 %scatter_custom_fusion.1 = bf16[1024,768]{1,0:T(8,128)(2,1)} fusion(s32[512]{0:T(512)S(1)} %bitcast.113, bf16[512,768]{1,0:T(8,128)(2,1)} %get-tuple-element.40, bf16[]{:T(256)} %constant.45.clone.1), kind=kCustom, calls=%fused_computation.11 | custom fusion | bytes 1573376 | tf_op jit(solution)/shard_map/scatter | solution.py:1151
  277.5 1.1 all-to-all-done.4
  278.5 6.6 %all-to-all-start.3 = ((bf16[128,8,768]{2,1,0:T(8,128)(2,1)}), bf16[128,8,768]{2,1,0:T(8,128)(2,1)S(1)}, u32[]{:S(2)}, u32[]{:S(2)}) async-start(bf16[128,8,768]{2,1,0:T(8,128)(2,1)} %bitcast.29), calls=%async_computation.3 | async-start | bytes 3145728 | tf_op jit(solution)/shard_map/all_to_all | solution.py:1154
  285.1 0.5 broadcast.280
  285.6 0.8 reduce.7
  286.5 0.1 all_to_all.24
  286.6 0.9 slice.56
  287.5 1.4 collective-permute-start.1
  288.9 0.8 dynamic-slice_bitcast_fusion.1
  289.7 1.3 fusion.20
  291.0 0.7 copy.92
  291.7 0.7 copy.93
  292.4 0.7 broadcast_in_dim_reshape.3
  293.2 0.1 reshape.274
  293.3 0.6 slice.69
  293.9 0.7 slice.68
  294.6 0.7 copy.89
  295.2 14.8 %all-to-all-done.3 = bf16[128,8,768]{2,1,0:T(8,128)(2,1)S(1)} async-done(((bf16[128,8,768]{2,1,0:T(8,128)(2,1)}), bf16[128,8,768]{2,1,0:T(8,128)(2,1)S(1)}, u32[]{:S(2)}, u32[]{:S(2)}) %all-to-all-start.3) | async-done | bytes 1572896 | tf_op jit(solution)/shard_map/all_to_all | solution.py:1154
  310.0 12.6 %scatter_custom_fusion.2 = f32[3920,768]{1,0:T(8,128)} fusion(s32[1024]{0:T(1024)S(1)} %bitcast.115, f32[]{:T(128)} %constant.84.clone.1, bf16[128,8,768]{2,1,0:T(8,128)(2,1)S(1)} %all-to-all-done.3), kind=kCustom, calls=%fused_computation.5 | custom fusion | flops 1572864 | bytes 13615108 | tf_op jit(solution)/shard_map/scatter-add | solution.py:1161
  322.7 1.1 copy.107
  (66 shorter events, 0.9 us)
Async XLA Ops:
  0.6 18.0 %copy-start.8 = (s32[4]{0:T(128)S(1)}, s32[4]{0:T(128)}, u32[]{:S(2)}) copy-start(s32[4]{0:T(128)} %param.12) | copy-start | bytes 52
  0.7 18.0 %copy-start.9 = (bf16[1,2,6]{2,1,0:T(2,128)(2,1)S(1)}, bf16[1,2,6]{2,1,0:T(2,128)(2,1)}, u32[]{:S(2)}) copy-start(bf16[1,2,6]{2,1,0:T(2,128)(2,1)} %param.18) | copy-start | bytes 76
  0.7 18.1 %copy-start.5 = (bf16[1,10,6]{1,2,0:T(8,128)(2,1)S(1)}, bf16[1,10,6]{1,2,0:T(8,128)(2,1)}, u32[]{:S(2)}) copy-start(bf16[1,10,6]{1,2,0:T(8,128)(2,1)} %param.19) | copy-start | bytes 364
  0.7 18.3 %copy-start.1 = (bf16[1,6,3072]{2,1,0:T(8,128)(2,1)S(1)}, bf16[1,6,3072]{2,1,0:T(8,128)(2,1)}, u32[]{:S(2)}) copy-start(bf16[1,6,3072]{2,1,0:T(8,128)(2,1)} %param.16) | copy-start | bytes 110596
  0.7 18.4 %copy-start.4 = (bf16[1,6,768]{2,1,0:T(8,128)(2,1)S(1)}, bf16[1,6,768]{2,1,0:T(8,128)(2,1)}, u32[]{:S(2)}) copy-start(bf16[1,6,768]{2,1,0:T(8,128)(2,1)} %param.15) | copy-start | bytes 27652
  0.7 18.4 %copy-start.2 = (bf16[1,6,2304]{2,1,0:T(8,128)(2,1)S(1)}, bf16[1,6,2304]{2,1,0:T(8,128)(2,1)}, u32[]{:S(2)}) copy-start(bf16[1,6,2304]{2,1,0:T(8,128)(2,1)} %param.14) | copy-start | bytes 82948
  7.1 20.9 %all-to-all-start.1 = ((s32[128,1,8]{2,1,0:T(1,128)}), s32[128,1,8]{2,1,0:T(1,128)S(1)}, u32[]{:S(2)}, u32[]{:S(2)}) async-start(s32[128,1,8]{2,1,0:T(1,128)} %bitcast.21), calls=%async_computation.1 | async-start | bytes 131072 | tf_op jit(solution)/shard_map/all_to_all | solution.py:1132
  28.1 14.0 %all-to-all-start = ((bf16[8,37,128]{2,1,0:T(8,128)(2,1)}), bf16[8,37,128]{2,1,0:T(8,128)(2,1)S(1)}, u32[]{:S(2)}, u32[]{:S(2)}) async-start(bf16[8,37,128]{2,1,0:T(8,128)(2,1)} %copy.71), calls=%async_computation | async-start | bytes 163840 | tf_op jit(solution)/shard_map/all_to_all | solution.py:1081
  42.1 5.9 %copy-start.3 = (bf16[1,24,768]{2,1,0:T(8,128)(2,1)S(1)}, bf16[1,24,768]{2,1,0:T(8,128)(2,1)}, u32[]{:S(2)}) copy-start(bf16[1,24,768]{2,1,0:T(8,128)(2,1)} %param.17) | copy-start | bytes 110596
  42.1 7.1 %copy-start.6 = (s32[4,2]{0,1:T(2,128)S(1)}, s32[4,2]{0,1:T(2,128)}, u32[]{:S(2)}) copy-start(s32[4,2]{0,1:T(2,128)} %param.11) | copy-start | bytes 100
  42.1 30.8 %all-to-all-start.2 = ((bf16[128,8,768]{2,1,0:T(8,128)(2,1)}), bf16[128,8,768]{2,1,0:T(8,128)(2,1)S(1)}, u32[]{:S(2)}, u32[]{:S(2)}) async-start(bf16[128,8,768]{2,1,0:T(8,128)(2,1)} %fusion.4), calls=%async_computation.2 | async-start | bytes 3145728 | tf_op jit(solution)/shard_map/all_to_all | solution.py:1136
  48.1 2.0 collective-permute-start
  265.1 13.5 %all-to-all-start.4 = ((f32[8,2,3,6,128]{4,1,3,2,0:T(2,128)}), f32[8,2,3,6,128]{4,1,3,2,0:T(2,128)S(1)}, u32[]{:S(2)}, u32[]{:S(2)}) async-start(f32[8,2,3,6,128]{4,1,3,2,0:T(2,128)} %copy.87), calls=%async_computation.4 | async-start | bytes 294912 | tf_op jit(solution)/shard_map/all_to_all | solution.py:1104
  278.5 12.5 %copy-start.7 = (f32[8,128]{1,0:T(8,128)S(1)}, f32[8,128]{1,0:T(8,128)}, u32[]{:S(2)}) copy-start(f32[8,128]{1,0:T(8,128)} %get-tuple-element.26) | copy-start | bytes 12292
  278.5 31.5 %all-to-all-start.3 = ((bf16[128,8,768]{2,1,0:T(8,128)(2,1)}), bf16[128,8,768]{2,1,0:T(8,128)(2,1)S(1)}, u32[]{:S(2)}, u32[]{:S(2)}) async-start(bf16[128,8,768]{2,1,0:T(8,128)(2,1)} %bitcast.29), calls=%async_computation.3 | async-start | bytes 3145728 | tf_op jit(solution)/shard_map/all_to_all | solution.py:1154
  287.5 4.8 %collective-permute-start.1 = (f32[3,24,128]{2,1,0:T(8,128)S(1)}, f32[3,24,128]{2,1,0:T(8,128)S(1)}, u32[]{:S(2)}, u32[]{:S(2)}) collective-permute-start(f32[3,24,128]{2,1,0:T(8,128)S(1)} %dynamic-slice_bitcast_fusion), channel_id=1, source_target_pairs={{0,1},{1,0},{2,3},{3,2},{4,5},{5,4},{6,7},{7,6},{8,9},{9,8},{10,11... | collective-permute-start | bytes 110600 | tf_op jit(solution)/shard_map/ppermute | solution.py:1099
  310.0 12.7 %copy-start = (f32[512,768]{1,0:T(8,128)S(1)}, f32[512,768]{1,0:T(8,128)}, u32[]{:S(2)}) copy-start(f32[512,768]{1,0:T(8,128)} %get-tuple-element.39) | copy-start | bytes 4718596

commit v3 on v2

--- a/solution.py
+++ b/solution.py
@@ -42,14 +42,6 @@
 
 def block_of(ref, part, core, order, spans):
     return ref.at[(part, core, order) + tuple(pl.ds(*spans[d]) for d in range(3))]
-
-
-def greet(spot, core):
-    barrier = pltpu.get_barrier_semaphore()
-    others = [(moved(spot, d, by), core) for d in range(3) for by in (1, -1)] + [(spot, 1 - core)]
-    for there, c in others:
-        pl.semaphore_signal(barrier, inc=1, device_id=device_at(there, c), device_id_type=MESH)
-    pl.semaphore_wait(barrier, len(others))
 
 
 class Gather:
@@ -103,14 +95,11 @@
         here = self.spans(o, 0, v)
         self.push(r, o, 0, here, up, src=src)
         self.push(r, o, 1, here, down, src=src)
-
-    def pass_on(self, r, o):
+        self.push(r, o, 2, here, moved(self.spot, ORDERS[o][0], 2), src=src)
+
+    def first_done(self, r, o):
         v, low, high, far, up, down = self.ring(o, 0)
         self.landed(r, o, 0, self.spans(o, 0, low))
-        self.push(r, o, 2, self.spans(o, 0, low), up)
-
-    def first_done(self, r, o):
-        v, low, high, far, up, down = self.ring(o, 0)
         self.landed(r, o, 1, self.spans(o, 0, high))
         self.landed(r, o, 2, self.spans(o, 0, far))
         self.share(r, o, 11, self.spans(o, 1, self.spot[ORDERS[o][1]]))
@@ -118,28 +107,35 @@
     def share(self, r, o, event, spans):
         self.push(r, o, event, spans, self.spot, 1 - self.core)
 
-    def spread(self, r, o, phase):
+    def spread(self, r, o, phase, direct=False):
         v, low, high, far, up, down = self.ring(o, phase)
         event = 3 + 4 * (phase - 1)
         here = self.spans(o, phase, v)
         self.push(r, o, event, here, up)
         self.push(r, o, event + 1, here, down)
-
-    def relay(self, r, o, phase):
+        if direct:
+            self.push(r, o, event + 2, here, moved(self.spot, ORDERS[o][phase], 2))
+
+    def relay(self, r, o, phase, direct=False):
         v, low, high, far, up, down = self.ring(o, phase)
         event, shared = 3 + 4 * (phase - 1), 11 + 3 * (phase - 1)
         self.landed(r, o, event, self.spans(o, phase, low))
-        self.push(r, o, event + 2, self.spans(o, phase, low, 0), up)
+        if not direct:
+            self.push(r, o, event + 2, self.spans(o, phase, low, 0), up)
         self.landed(r, o, event + 1, self.spans(o, phase, high))
-        self.push(r, o, event + 3, self.spans(o, phase, high, 1), down)
+        if not direct:
+            self.push(r, o, event + 3, self.spans(o, phase, high, 1), down)
         self.share(r, o, shared + 1, self.spans(o, phase, low))
         self.share(r, o, shared + 2, self.spans(o, phase, high))
 
-    def finish(self, r, o, phase):
+    def finish(self, r, o, phase, direct=False):
         v, low, high, far, up, down = self.ring(o, phase)
         event, shared = 3 + 4 * (phase - 1), 11 + 3 * (phase - 1)
-        self.landed(r, o, event + 2, self.spans(o, phase, far, 0))
-        self.landed(r, o, event + 3, self.spans(o, phase, far, 1))
+        if direct:
+            self.landed(r, o, event + 2, self.spans(o, phase, far))
+        else:
+            self.landed(r, o, event + 2, self.spans(o, phase, far, 0))
+            self.landed(r, o, event + 3, self.spans(o, phase, far, 1))
         self.share(r, o, shared + 3, self.spans(o, phase, far))
 
     def shared_done(self, r, o):
@@ -200,27 +196,147 @@
     return high, (value - high.astype(jnp.float32)).astype(jnp.bfloat16)
 
 
+def greet_all():
+    barrier = pltpu.get_barrier_semaphore()
+    me = lax.axis_index("wide") * 8 + lax.axis_index("narrow")
+
+    def hello(k, _):
+        there = (me + k) % 128
+        pl.semaphore_signal(barrier, inc=1, device_id=(there // 8, there % 8), device_id_type=MESH)
+        return 0
+
+    lax.fori_loop(1, 128, hello, 0)
+    return lambda: pl.semaphore_wait(barrier, 127)
+
+
+def pack_rows(rows):
+    n = rows.shape[0] // 8
+    left, right = rows[:, :384].reshape(n, 8, 384), rows[:, 384:].reshape(n, 8, 384)
+    return jnp.concatenate([left, right], axis=1).astype(jnp.bfloat16)
+
+
+def unpack_rows(packed):
+    wide_rows = packed.astype(jnp.float32)
+    rows = jnp.concatenate([wide_rows[:, :8], wide_rows[:, 8:]], axis=2)
+    return rows.reshape(-1, 768).astype(jnp.bfloat16)
+
+
+def digits(value):
+    high = jnp.floor(value * 0.015625)
+    return high.astype(jnp.bfloat16), (value - 64.0 * high).astype(jnp.bfloat16)
+
+
+def token_slots(hot_ref, local_ref):
+    hot = hot_ref[...]
+    row = lax.broadcasted_iota(jnp.int32, (512, 512), 0)
+    col = lax.broadcasted_iota(jnp.int32, (512, 512), 1)
+    before = mm((col < row).astype(jnp.bfloat16), hot)
+    lane = lax.broadcasted_iota(jnp.int32, (512, 128), 1).astype(jnp.float32)
+    wide_hot = hot.astype(jnp.float32)
+    rank = jnp.sum(before * wide_hot, axis=1, keepdims=True)
+    slot = jnp.sum(wide_hot * lane, axis=1, keepdims=True) * 8.0 + rank
+    high, low = digits(local_ref[...])
+    zero = jnp.zeros((), jnp.bfloat16)
+    here = lane == rank
+    both = mm_tn(hot, jnp.concatenate([jnp.where(here, high, zero), jnp.where(here, low, zero)], axis=1))
+    return slot, both[:, :128] * 64.0 + both[:, 128:]
+
+
+def slot_hot(slot_ref):
+    lane = lax.broadcasted_iota(jnp.int32, (512, 128), 1).astype(jnp.float32)
+    parts = [(slot_ref[...] == lane + 128.0 * i).astype(jnp.bfloat16) for i in range(8)]
+    return jnp.concatenate(parts, axis=1)
+
+
 def forward_kernel(
-    lens_ref, own_ref, tile_ref, x_ref,
-    w_out, vec_out, h1_out, h2_out, inv_out, nl_out, act_out, gp_out, qkv_out, prob_out, ctx_out, dpool_out, loss_out,
-    w, vecs, tiles, h1, h2, inv, nl, act, gp, qkv, prob, ctx, resid, pooled, rnorm, pool_own, pool_swap, pool_all,
-    left3, right3, stats,
+    lens_ref, sent_ref, halves_ref, hot_ref, local_ref, table_in,
+    w_out, vec_out, h1_out, h2_out, inv_out, nl_out, act_out, gp_out, qkv_out, prob_out, ctx_out, x_out,
+    dpool_out, loss_out, slot_out, asked_out,
+    w, vecs, tiles, h1, h2, inv, nl, act, gp, qkv, prob, ctx, x_ref, resid, pooled, rnorm, pool_own, pool_swap, pool_all,
+    left3, right3, stats, own, near, half_got, table, ids_out, ids_in, ids, asked, rows_out, rows_in, row_mat,
     send_sem, recv_sem, local_sem, pool_send, pool_recv, tile_send, tile_recv, swap_sem, load_sem, save_sem,
+    near_send, near_recv, ids_sem, rows_sem, table_sem,
 ):
     spot, core = where_am_i()
+    me = lax.axis_index("wide") * 8 + lax.axis_index("narrow")
     bf, f32 = jnp.bfloat16, jnp.float32
-    greet(spot, core)
+    all_here = greet_all()
+    table_rows = table_in.shape[0]
+    get_table = pltpu.make_async_copy(table_in, table.at[pl.ds(0, table_rows)], table_sem.at[0])
+    get_table.start()
+    table[pl.ds(table_rows, 4096 - table_rows), :] = jnp.zeros((4096 - table_rows, 768), bf)
+    slot, wanted = token_slots(hot_ref, local_ref)
+    slot_out[...] = jnp.broadcast_to(slot, (512, 128))
+    ids[...] = wanted
+
+    def row_out(i, _):
+        ids_out[i] = ids[pl.ds(i, 1), :]
+        return 0
+
+    lax.fori_loop(0, 128, row_out, 0)
+    all_here()
+
+    mine = spot[0] * 2 + core
+    sent = []
+    for k in range(1, 8):
+        there = (mine + k) % 8
+        copy = pltpu.make_async_remote_copy(
+            src_ref=sent_ref.at[there], dst_ref=near.at[mine], send_sem=near_send.at[k], recv_sem=near_recv.at[k],
+            device_id=(lax.axis_index("wide"), there), device_id_type=MESH,
+        )
+        copy.start()
+        sent.append(copy)
+    copy = pltpu.make_async_remote_copy(
+        src_ref=halves_ref.at[1 - core], dst_ref=half_got, send_sem=near_send.at[0], recv_sem=near_recv.at[0],
+        device_id=device_at(spot, 1 - core), device_id_type=MESH,
+    )
+    copy.start()
+    sent.append(copy)
+
+    def ask(k, _):
+        there = (me + k) % 128
+        pltpu.make_async_remote_copy(
+            src_ref=ids_out.at[there], dst_ref=ids_in.at[(128 - k) % 128],
+            send_sem=ids_sem.at[0], recv_sem=ids_sem.at[1],
+            device_id=(there // 8, there % 8), device_id_type=MESH,
+        ).start()
+        return 0
+
+    lax.fori_loop(1, 128, ask, 0)
+    ids_in[0] = ids_out[me]
+    near[mine] = sent_ref[mine]
+    for k in range(1, 8):
+        ref = near.at[(mine + 8 - k) % 8]
+        pltpu.make_async_copy(ref, ref, near_recv.at[k]).wait()
+    pltpu.make_async_copy(half_got, half_got, near_recv.at[0]).wait()
+    row = lax.broadcasted_iota(jnp.int32, (288, 384), 0)
+    col = lax.broadcasted_iota(jnp.int32, (288, 384), 1)
+    unit, at = row // UNIT, row % UNIT
+    pick = col == at // 6 * UNIT + unit * 6 + at % 6
+    units = mm(pick.astype(bf), near[...].reshape(384, 128)).astype(bf)
+    for r in range(2):
+        for o in range(3):
+            first_row = UNIT * (3 * r + o)
+            own[r, o] = units[first_row : first_row + UNIT].reshape(1, 1, 1, UNIT, 128)
+    kept, got = halves_ref[core].astype(f32), half_got[...].astype(f32)
+    for o in range(3):
+        a, b = kept[24 * o : 24 * o + 24], got[24 * o : 24 * o + 24]
+        upper, lower = jnp.where(core == 0, a, b), jnp.where(core == 0, b, a)
+        own[2, o] = jnp.concatenate([upper, lower], axis=0).astype(bf).reshape(1, 1, 1, UNIT, 128)
+    small = jnp.zeros((16, 128), f32)
+    for j in range(8):
+        small = small + near[j, 32:48, :].astype(f32)
+    tiles[pl.ds(spot[1], 1), pl.ds(spot[2], 1)] = small.astype(bf).reshape(1, 1, 16, 128)
+
     g = Gather(w_out, send_sem, recv_sem, spot, core, (0, 1, 2))
     every = [(r, o) for r in range(3) for o in range(3)]
     keep = []
     for r, o in every:
         here = g.spans(o, 0, spot[ORDERS[o][0]])
-        copy = pltpu.make_async_copy(own_ref.at[r, o], g.block(r, o, here, core), local_sem.at[r, o])
+        copy = pltpu.make_async_copy(own.at[r, o], g.block(r, o, here, core), local_sem.at[r, o])
         copy.start()
         keep.append(copy)
-        g.begin(r, o, own_ref.at[r, o])
-    tiles[pl.ds(spot[1], 1), pl.ds(spot[2], 1)] = tile_ref[...]
-    tile_sent = []
+        g.begin(r, o, own.at[r, o])
 
     def tile_push(event, at, there):
         ref = tiles.at[at]
@@ -229,46 +345,93 @@
             device_id=device_at(there, core), device_id_type=MESH,
         )
         copy.start()
-        tile_sent.append(copy)
-
-    def tile_landed(event, at):
-        ref = tiles.at[at]
-        pltpu.make_async_copy(ref, ref, tile_recv.at[event]).wait()
+        sent.append(copy)
 
     def tile_at(phase, v):
         return (pl.ds(v, 1), pl.ds(spot[2], 1)) if phase == 0 else (pl.ds(0, RING), pl.ds(v, 1))
 
-    def tile_step(phase, step):
-        d = phase + 1
-        v = spot[d]
-        up, down = moved(spot, d, 1), moved(spot, d, -1)
-        if step == 0:
-            tile_push(3 * phase, tile_at(phase, v), up)
-            tile_push(3 * phase + 1, tile_at(phase, v), down)
-        elif step == 1:
-            tile_landed(3 * phase, tile_at(phase, (v - 1) % RING))
-            tile_push(3 * phase + 2, tile_at(phase, (v - 1) % RING), up)
-        else:
-            tile_landed(3 * phase + 1, tile_at(phase, (v + 1) % RING))
-            tile_landed(3 * phase + 2, tile_at(phase, (v + 2) % RING))
-
-    tile_step(0, 0)
-    for r, o in every:
-        g.pass_on(r, o)
-    tile_step(0, 1)
+    def tile_spread(phase):
+        for k, by in enumerate((1, 2, 3)):
+            tile_push(3 * phase + k, tile_at(phase, spot[phase + 1]), moved(spot, phase + 1, by))
+
+    def tile_landed(phase):
+        for k, by in enumerate((1, 2, 3)):
+            ref = tiles.at[tile_at(phase, (spot[phase + 1] + RING - by) % RING)]
+            pltpu.make_async_copy(ref, ref, tile_recv.at[3 * phase + k]).wait()
+
+    tile_spread(0)
     for (r, o), copy in zip(every, keep):
         copy.wait()
         g.first_done(r, o)
-        g.spread(r, o, 1)
-    tile_step(0, 2)
-    tile_step(1, 0)
-    for r, o in every:
-        g.relay(r, o, 1)
-    tile_step(1, 1)
-    for r, o in every:
-        g.finish(r, o, 1)
-        g.spread(r, o, 2)
-    tile_step(1, 2)
+        g.spread(r, o, 1, r == 0)
+    tile_landed(0)
+    tile_spread(1)
+
+    others = ids_in.at[pl.ds(0, 127)]
+    pltpu.make_async_copy(others, others, ids_sem.at[1]).wait()
+
+    def row_in(i, _):
+        ids[pl.ds(i, 1), :] = ids_in[i]
+        return 0
+
+    lax.fori_loop(0, 128, row_in, 0)
+    high, low = digits(ids[...])
+    row = lax.broadcasted_iota(jnp.int32, (1024, 128), 0)
+    col = lax.broadcasted_iota(jnp.int32, (1024, 128), 1)
+    member_of = (row // 8 == col).astype(bf)
+    both = mm(member_of, high) * 64.0 + mm(member_of, low)
+    asked_col = jnp.sum(jnp.where(col == row % 8, both, 0.0), axis=1, keepdims=True) - 1.0
+    asked[...] = jnp.broadcast_to(asked_col, (1024, 128))
+    row = lax.broadcasted_iota(jnp.int32, (128, 1024), 0)
+    col = lax.broadcasted_iota(jnp.int32, (128, 1024), 1)
+    member_of = (col // 8 == row).astype(bf)
+    both = mm_tn(high, member_of) * 64.0 + mm_tn(low, member_of)
+    asked_row = jnp.sum(jnp.where(row == col % 8, both, 0.0), axis=0, keepdims=True) - 1.0
+    asked_out[...] = jnp.broadcast_to(asked_row, (8, 1024))
+    get_table.wait()
+
+    def find(half):
+        col = asked[512 * half : 512 * half + 512, :]
+        lane = lax.broadcasted_iota(jnp.int32, (512, 128), 1).astype(f32)
+
+        def chunk(i, _):
+            first_row = i * 512
+            base = lane + (first_row * 1).astype(f32)
+            hot = jnp.concatenate([(col == base + 128.0 * j).astype(bf) for j in range(4)], axis=1)
+            part = mm(hot, table[pl.ds(pl.multiple_of(first_row, 512), 512), :])
+            resid[...] = jnp.where(i == 0, part, resid[...] + part)
+            return 0
+
+        lax.fori_loop(0, 8, chunk, 0)
+        for q in range(4):
+            rows_out[64 * half + 16 * q : 64 * half + 16 * q + 16] = pack_rows(resid[128 * q : 128 * q + 128, :])
+
+        def answer(k, _):
+            there = (me + k) % 128
+            pltpu.make_async_remote_copy(
+                src_ref=rows_out.at[k], dst_ref=rows_in.at[me], send_sem=rows_sem.at[0], recv_sem=rows_sem.at[1],
+                device_id=(there // 8, there % 8), device_id_type=MESH,
+            ).start()
+            return 0
+
+        lax.fori_loop(max(1, 64 * half), 64 * half + 64, answer, 0)
+
+    find(0)
+    rows_in[me] = rows_out[0]
+    for o in range(3):
+        g.relay(0, o, 1, True)
+    for o in range(3):
+        g.finish(0, o, 1, True)
+        g.spread(0, o, 2)
+    for r in (1, 2):
+        for o in range(3):
+            g.relay(r, o, 1)
+    find(1)
+    for r in (1, 2):
+        for o in range(3):
+            g.finish(r, o, 1)
+            g.spread(r, o, 2)
+    tile_landed(1)
 
     row_at = lax.broadcasted_iota(jnp.int32, (128, 768), 0)
     col_at = lax.broadcasted_iota(jnp.int32, (128, 768), 1)
@@ -278,10 +441,10 @@
         part = tiles[slab // RING, slab % RING]
         pick = (col_at == row_at + UNIT * slab) & (row_at < UNIT)
         all_vec = all_vec + mm(part, pick.astype(bf))
-        pick = (col_at == row_at + 32 * slab) & (row_at < 32)
+        pick = (col_at == row_at - 64 + 32 * slab) & (row_at >= 64) & (row_at < 96)
         all_grp = all_grp + mm(part, pick[:, :512].astype(bf))
-    vecs[...] = all_vec
-    group_row = all_grp[12:13]
+    vecs[...] = jnp.concatenate([all_vec[4:16], all_vec[0:4]], axis=0)
+    group_row = all_grp[4:5]
     saves = []
 
     def save(scratch, out, at):
@@ -309,6 +472,15 @@
 
     save(vecs, vec_out, 0)
     arrive(0)
+    others = rows_in.at[pl.ds(0, 127)]
+    pltpu.make_async_copy(others, others, rows_sem.at[1]).wait()
+    for q in range(8):
+        row_mat[128 * q : 128 * q + 128, :] = unpack_rows(rows_in[16 * q : 16 * q + 16])
+    slots_hot = slot_hot(slot_out)
+    for p in range(3):
+        cut = slice(256 * p, 256 * p + 256)
+        x_ref[:, cut] = mm(slots_hot, row_mat[:, cut]).astype(bf)
+    save(x_ref, x_out, 10)
     arrived(0)
     mask = head_mask()
 
@@ -436,14 +608,12 @@
     for o in range(3):
         q.begin(0, o, None)
     for o in range(3):
-        q.pass_on(0, o)
+        q.first_done(0, o)
+        q.spread(0, o, 1, True)
     for o in range(3):
-        q.first_done(0, o)
-        q.spread(0, o, 1)
+        q.relay(0, o, 1, True)
     for o in range(3):
-        q.relay(0, o, 1)
-    for o in range(3):
-        q.finish(0, o, 1)
+        q.finish(0, o, 1, True)
         q.spread(0, o, 2)
     for o in range(3):
         q.relay(0, o, 2)
@@ -485,7 +655,6 @@
     at_row = lax.broadcasted_iota(jnp.int32, (8, 512), 0) + chip * 8
     at_col = lax.broadcasted_iota(jnp.int32, (8, 512), 1)
     own_pair = at_row == at_col
-    first_rows = (lax.broadcasted_iota(jnp.int32, (16, 8), 0).astype(f32)).astype(bf)
     pick = (lax.broadcasted_iota(jnp.int32, (8, 512), 1) == at_row).astype(bf)
     own_member = mm_nt(pick, member)
     alike = mm(own_member.astype(bf), member) > 0.5
@@ -522,13 +691,16 @@
         dpool_out[s] = rnorm[s] * (d_row - row * inner) / lens_ref[s].astype(f32)
     g.drain()
     q.drain()
-    for copy in tile_sent:
+    for copy in sent:
         copy.wait_send()
+    for sem, ref in ((ids_sem, ids_in), (rows_sem, rows_in)):
+        others = ref.at[pl.ds(0, 127)]
+        pltpu.make_async_copy(others, others, sem.at[0]).wait()
     for copy in saves:
         copy.wait()
 
 
-def forward_pass(lens, own, tile, x):
+def forward_pass(lens, sent, halves, hot, local, table):
     bf, f32 = jnp.bfloat16, jnp.float32
     shapes = [
         ((3, 2, 3, RING, RING, RING, UNIT, 128), bf),
@@ -542,8 +714,11 @@
         ((9, 512, 256), bf),
         ((8, 3, SEQ, 256), f32),
         ((3, 512, 256), bf),
+        ((512, 768), bf),
         ((8, 1, 768), f32),
         ((8, 128), f32),
+        ((512, 128), f32),
+        ((8, 1024), f32),
     ]
     anywhere = pl.BlockSpec(memory_space=pl.ANY)
     vmem = pl.BlockSpec(memory_space=pltpu.VMEM)
@@ -551,13 +726,13 @@
     return pl.pallas_call(
         forward_kernel,
         out_shape=[jax.ShapeDtypeStruct(*s) for s in shapes],
-        in_specs=[pl.BlockSpec(memory_space=pltpu.SMEM), vmem, vmem, vmem],
-        out_specs=[anywhere] * 11 + [vmem] * 2,
+        in_specs=[pl.BlockSpec(memory_space=pltpu.SMEM), vmem, vmem, vmem, vmem, anywhere],
+        out_specs=[anywhere] * 12 + [vmem] * 4,
         scratch_shapes=[
             pltpu.VMEM(*shapes[0]),
             pltpu.VMEM(*shapes[1]),
             pltpu.VMEM((RING, RING, 16, 128), bf),
-            *[pltpu.VMEM(*s) for s in shapes[2:11]],
+            *[pltpu.VMEM(*s) for s in shapes[2:12]],
             pltpu.VMEM((512, 768), f32),
             pltpu.VMEM((8, 1, 768), f32),
             pltpu.VMEM((8, 1, 768), f32),
@@ -567,6 +742,17 @@
             pltpu.VMEM((512, 2304), bf),
             pltpu.VMEM((512, 2304), bf),
             pltpu.VMEM((8, 512), f32),
+            pltpu.VMEM((3, 3, 1, 1, 1, UNIT, 128), bf),
+            pltpu.VMEM((8, UNIT, 128), bf),
+            pltpu.VMEM((80, 128), bf),
+            pltpu.VMEM((4096, 768), bf),
+            pltpu.VMEM((128, 1, 128), f32),
+            pltpu.VMEM((128, 1, 128), f32),
+            pltpu.VMEM((128, 128), f32),
+            pltpu.VMEM((1024, 128), f32),
+            pltpu.VMEM((128, 16, 384), bf),
+            pltpu.VMEM((128, 16, 384), bf),
+            pltpu.VMEM((1024, 768), bf),
             dma((3, 3, 18)),
             dma((3, 3, 18)),
             dma((3, 3)),
@@ -576,13 +762,18 @@
             dma((6,)),
             dma((2,)),
             dma((3, 2, 3)),
-            dma((10,)),
+            dma((11,)),
+            dma((8,)),
+            dma((8,)),
+            dma((2,)),
+            dma((2,)),
+            dma((1,)),
         ],
         compiler_params=pltpu.CompilerParams(
-            collective_id=1, has_side_effects=True, vmem_limit_bytes=60 * 1024 * 1024
+            collective_id=1, has_side_effects=True, vmem_limit_bytes=62 * 1024 * 1024
         ),
         name="forward_pass",
-    )(lens, own.reshape(3, 3, 1, 1, 1, UNIT, 128), tile.reshape(1, 1, 16, 128), x)
+    )(lens, sent, halves, hot, local, table)
 
 
 class Reduce:
@@ -705,13 +896,14 @@
 
 
 def backward_kernel(
-    lens_ref, vec_ref, dpool_ref, x_ref,
+    lens_ref, vec_ref, dpool_ref, x_ref, slot_ref,
     w_in, h1_in, h2_in, inv_in, nl_in, act_in, gp_in, qkv_in, prob_in, ctx_in,
-    token_out, low_out, red_out, vec_out,
-    w, h1, h2, inv, nl, act, gp, qkv, prob, ctx, parts, d2d, d_res, d_low, turned, dvec, vec_slots, *rest,
+    token_out, rows_in, qkv_out, out_out, up_out, down_out, vec_out,
+    w, h1, h2, inv, nl, act, gp, qkv, prob, ctx, parts, d2d, d_res, d_low, turned, dvec, vec_slots, red_out, near_out, near_in, half_in, rows_out, *rest,
 ):
     bufs = rest[:18]
-    send_sem, recv_sem, swap_send, swap_recv, free_sem, vec_send, vec_recv, load_sem, gp_sem, w_sem = rest[18:]
+    send_sem, recv_sem, swap_send, swap_recv, free_sem, vec_send, vec_recv, load_sem, gp_sem, w_sem, near_send, near_recv, rows_sem = rest[18:]
+    me = lax.axis_index("wide") * 8 + lax.axis_index("narrow")
     spot, core = where_am_i()
     bf, f32 = jnp.bfloat16, jnp.float32
 
@@ -737,7 +929,7 @@
     get_w1 = load_w(1, 1)
     get_h1, get_ctx = load(h1_in, h1, 4), load(ctx_in, ctx, 5)
     get_qkv, get_prob = load(qkv_in, qkv, 6), load(prob_in, prob, 7)
-    greet(spot, core)
+    all_here = greet_all()
     red = Reduce(parts, bufs, red_out, send_sem, recv_sem, spot, core)
     swaps = {}
 
@@ -815,6 +1007,7 @@
         return 0
 
     lax.fori_loop(0, RING, down_step, 0)
+    all_here()
     give(2)
     get_w2.wait()
 
@@ -989,8 +1182,23 @@
     token_copy = pltpu.make_async_copy(d_res, token_out, load_sem.at[8])
     token_copy.start()
     d_low[...] = d_res[...].astype(bf)
-    low_copy = pltpu.make_async_copy(d_low, low_out, load_sem.at[9])
-    low_copy.start()
+    slots_hot = slot_hot(slot_ref)
+    for q in range(4):
+        rows = mm_tn(slots_hot[:, 256 * q : 256 * q + 256], d_low[...])
+        rows_out[32 * q : 32 * q + 32] = pack_rows(rows)
+
+    def hand_back(k, _):
+        there = (me + k) % 128
+        pltpu.make_async_remote_copy(
+            src_ref=rows_out.at[there], dst_ref=rows_in.at[(128 - k) % 128],
+            send_sem=rows_sem.at[0], recv_sem=rows_sem.at[1],
+            device_id=(there // 8, there % 8), device_id_type=MESH,
+        ).start()
+        return 0
+
+    lax.fori_loop(1, 128, hand_back, 0)
+    keep_rows = pltpu.make_async_copy(rows_out.at[me], rows_in.at[0], load_sem.at[9])
+    keep_rows.start()
     take(0)
     vec_relay(0)
     third(1, 1)
@@ -1012,13 +1220,58 @@
     vec_out[...] = dvec[4]
     second(0, 2)
     third(0, 2)
+
+    mine = spot[0] * 2 + core
+    for j in range(8):
+        for r in range(2):
+            for o in range(3):
+                at = 6 * (3 * r + o)
+                near_out[j, at : at + 6, :] = red_out[r, o, 6 * j : 6 * j + 6, :]
+    for k in range(1, 8):
+        there = (mine + k) % 8
+        copy = pltpu.make_async_remote_copy(
+            src_ref=near_out.at[there], dst_ref=near_in.at[mine], send_sem=near_send.at[k], recv_sem=near_recv.at[k],
+            device_id=(lax.axis_index("wide"), there), device_id_type=MESH,
+        )
+        copy.start()
+        vec_sent.append(copy)
+    theirs = pl.ds(pl.multiple_of(24 * (1 - core), 8), 24)
+    copy = pltpu.make_async_remote_copy(
+        src_ref=red_out.at[2, :, theirs], dst_ref=half_in, send_sem=near_send.at[0], recv_sem=near_recv.at[0],
+        device_id=device_at(spot, 1 - core), device_id_type=MESH,
+    )
+    copy.start()
+    vec_sent.append(copy)
+    near_in[mine] = near_out[mine]
+    for k in range(1, 8):
+        ref = near_in.at[(mine + 8 - k) % 8]
+        pltpu.make_async_copy(ref, ref, near_recv.at[k]).wait()
+    pltpu.make_async_copy(half_in, half_in, near_recv.at[0]).wait()
+    for c in range(2):
+        for o in range(3):
+            for x in range(RING):
+                n, j = c * 12 + o * 4 + x, 2 * x + c
+                block = near_in[j, 6 * o : 6 * o + 6, :]
+                if n < 18:
+                    qkv_out[:, 128 * n : 128 * n + 128] = block
+                else:
+                    out_out[:, 128 * (n - 18) : 128 * (n - 18) + 128] = block
+                up_out[:, 128 * n : 128 * n + 128] = near_in[j, 18 + 6 * o : 24 + 6 * o, :]
+    ours = pl.ds(pl.multiple_of(24 * core, 8), 24)
+    for o in range(3):
+        a, b = red_out[2, o, ours, :], half_in[o]
+        down_out[:, 128 * o : 128 * o + 128] = jnp.where(core == 0, a, b)
+        down_out[:, 384 + 128 * o : 512 + 128 * o] = jnp.where(core == 0, b, a)
+    others = rows_in.at[pl.ds(0, 127)]
+    pltpu.make_async_copy(others, others, rows_sem.at[1]).wait()
+    pltpu.make_async_copy(others, others, rows_sem.at[0]).wait()
     token_copy.wait()
-    low_copy.wait()
+    keep_rows.wait()
     for copy in red.sent + vec_sent:
         copy.wait_send()
 
 
-def backward_pass(lens, vectors, d_pool, x, w, h1, h2, inv, nl, act, gp, qkv, prob, ctx):
+def backward_pass(lens, vectors, d_pool, x, slots, w, h1, h2, inv, nl, act, gp, qkv, prob, ctx):
     bf, f32 = jnp.bfloat16, jnp.float32
     anywhere = pl.BlockSpec(memory_space=pl.ANY)
     vmem = pl.BlockSpec(memory_space=pltpu.VMEM)
@@ -1041,6 +1294,11 @@
         pltpu.VMEM((768, 512), bf),
         pltpu.VMEM((5, 16, 768), f32),
         pltpu.VMEM((10, 16, 768), f32),
+        pltpu.VMEM((3, 3, UNIT, 128), f32),
+        pltpu.VMEM((8, 40, 128), f32),
+        pltpu.VMEM((8, 40, 128), f32),
+        pltpu.VMEM((3, 24, 128), f32),
+        pltpu.VMEM((128, 16, 384), bf),
         *reduce_buffers(3),
         dma((3, 3, 13)),
         dma((3, 3, 13)),
@@ -1052,123 +1310,100 @@
         dma((10,)),
         dma((2,)),
         dma((3,)),
+        dma((8,)),
+        dma((8,)),
+        dma((2,)),
+    ]
+    shapes = [
+        ((512, 768), f32),
+        ((128, 16, 384), bf),
+        ((6, 2304), f32),
+        ((6, 768), f32),
+        ((6, 3072), f32),
+        ((24, 768), f32),
+        ((16, 768), f32),
     ]
     return pl.pallas_call(
         backward_kernel,
-        out_shape=[
-            jax.ShapeDtypeStruct((512, 768), f32),
-            jax.ShapeDtypeStruct((512, 768), bf),
-            jax.ShapeDtypeStruct((3, 3, UNIT, 128), f32),
-            jax.ShapeDtypeStruct((16, 768), f32),
-        ],
-        in_specs=[pl.BlockSpec(memory_space=pltpu.SMEM), vmem, vmem, vmem] + [anywhere] * 10,
-        out_specs=[anywhere, anywhere, vmem, vmem],
+        out_shape=[jax.ShapeDtypeStruct(*s) for s in shapes],
+        in_specs=[pl.BlockSpec(memory_space=pltpu.SMEM)] + [vmem] * 4 + [anywhere] * 10,
+        out_specs=[anywhere] * 2 + [vmem] * 5,
         scratch_shapes=scratch,
         compiler_params=pltpu.CompilerParams(
-            collective_id=2, has_side_effects=True, vmem_limit_bytes=63 * 1024 * 1024
+            collective_id=2, has_side_effects=True, vmem_limit_bytes=64 * 1024 * 1024 - 65536
         ),
         name="backward_pass",
-    )(lens, vectors, d_pool, x, w, h1, h2, inv, nl, act, gp, qkv, prob, ctx)
-
-
-def own_units(w_qkv, w_out, w_up, w_down, gains, biases, groups, core):
-    first = jnp.concatenate([w_qkv, w_out], axis=1)
-    both = jnp.stack([first, w_up]).reshape(2, 6, 2, 3, RING, 128)
-    out_going = both.transpose(4, 2, 0, 3, 1, 5).reshape(8, 36, 128)
-    extra = jnp.concatenate([gains.reshape(-1), biases.reshape(-1), groups.astype(jnp.bfloat16)])
-    extra = jnp.broadcast_to(jnp.pad(extra, (0, 52))[None, None], (8, 1, 128))
-    out_going = jnp.concatenate([out_going, extra], axis=1)
-    rows = lax.all_to_all(out_going, "narrow", split_axis=0, concat_axis=0, tiled=True)
-    units = rows[:, :36].reshape(8, 2, 3, 6, 128).transpose(1, 2, 0, 3, 4).reshape(2, 3, UNIT, 128)
-    vectors = rows[:, 36, :72].reshape(8, 12, 6).transpose(1, 0, 2).reshape(12, UNIT)
-    named = rows[:, 36, 72:76].reshape(1, 32)
-    tile = jnp.concatenate(
-        [jnp.pad(vectors, ((0, 0), (0, 80))), jnp.pad(named, ((0, 3), (0, 96)))], axis=0
+    )(lens, vectors, d_pool, x, slots, w, h1, h2, inv, nl, act, gp, qkv, prob, ctx)
+
+
+TABLE_STEP = 560
+
+
+def table_kernel(rows_ref, asked_ref, out_ref, rows):
+    at = pl.program_id(0)
+
+    @pl.when(at == 0)
+    def _():
+        for q in range(8):
+            rows[128 * q : 128 * q + 128, :] = unpack_rows(rows_ref[16 * q : 16 * q + 16])
+
+    name = (lax.broadcasted_iota(jnp.int32, (TABLE_STEP, 1024), 0) + at * TABLE_STEP).astype(jnp.float32)
+    out_ref[...] = mm((name == asked_ref[0:1, :]).astype(jnp.bfloat16), rows[...])
+
+
+def table_sums(rows, asked, table_rows):
+    return pl.pallas_call(
+        table_kernel,
+        out_shape=jax.ShapeDtypeStruct((table_rows, 768), jnp.float32),
+        grid=(table_rows // TABLE_STEP,),
+        in_specs=[
+            pl.BlockSpec((128, 16, 384), lambda i: (0, 0, 0)),
+            pl.BlockSpec((8, 1024), lambda i: (0, 0)),
+        ],
+        out_specs=pl.BlockSpec((TABLE_STEP, 768), lambda i: (i, 0)),
+        scratch_shapes=[pltpu.VMEM((1024, 768), jnp.bfloat16)],
+        compiler_params=pltpu.CompilerParams(vmem_limit_bytes=40 * 1024 * 1024),
+        name="table_sums",
+    )(rows, asked)
+
+
+def shards(token_ids, lengths, groups, table, w_qkv, w_out, w_up, w_down, gains, biases):
+    bf, f32 = jnp.bfloat16, jnp.float32
+    flat_ids = token_ids.reshape(-1)
+    table_rows = table.shape[0]
+    rank_at = lax.axis_index(("wide", "narrow"))
+    owner = flat_ids // table_rows
+    hot = (owner[:, None] == jnp.arange(128)[None, :]).astype(bf)
+    local = jnp.broadcast_to((flat_ids - owner * table_rows + 1).astype(f32)[:, None], (512, 128))
+    first = jnp.concatenate([w_qkv[0], w_out[0]], axis=1)
+    units = jnp.stack([first, w_up[0]]).reshape(2, 6, 2, 3, RING, 128)
+    units = units.transpose(4, 2, 0, 3, 1, 5).reshape(8, 36, 128)
+    vectors = jnp.concatenate([gains[0], biases[0]])
+    named = jnp.concatenate([groups.astype(bf)[None], jnp.zeros((11, 4), bf)])
+    spread = jnp.concatenate(
+        [jnp.tile(vectors, (1, 8)), jnp.zeros((12, 16), bf), jnp.tile(named, (1, 8)), jnp.zeros((12, 32), bf)], axis=1
     )
-    halves = w_down.reshape(24, 2, 3, 128).transpose(1, 2, 0, 3)
-    keep = lax.dynamic_index_in_dim(halves, core, 0, keepdims=False)
-    give = lax.dynamic_index_in_dim(halves, 1 - core, 0, keepdims=False)
-    got = swapped(give)
-    low_rows = jnp.where(core == 0, keep, got)
-    high_rows = jnp.where(core == 0, got, keep)
-    down = jnp.concatenate([low_rows, high_rows], axis=1)
-    return jnp.concatenate([units, down[None]], axis=0), tile
-
-
-def swapped(value):
-    return lax.ppermute(value, "narrow", [(i, i ^ 1) for i in range(8)])
-
-
-def own_rows(reduced, core):
-    out_going = reduced[:2].reshape(2, 3, 8, 6, 128).transpose(2, 0, 1, 3, 4)
-    rows = lax.all_to_all(out_going, "narrow", split_axis=0, concat_axis=0, tiled=True)
-    rows = rows.reshape(RING, 2, 2, 3, 6, 128).transpose(2, 4, 1, 3, 0, 5).reshape(2, 6, 3072)
-    halves = reduced[2].reshape(3, 2, 24, 128).transpose(1, 0, 2, 3)
-    keep = lax.dynamic_index_in_dim(halves, core, 0, keepdims=False)
-    give = lax.dynamic_index_in_dim(halves, 1 - core, 0, keepdims=False)
-    got = swapped(give)
-    low_cols = jnp.where(core == 0, keep, got)
-    high_cols = jnp.where(core == 0, got, keep)
-    down = jnp.concatenate([low_cols, high_cols]).transpose(1, 0, 2).reshape(24, 768)
-    return rows[0, :, :2304], rows[0, :, 2304:], rows[1], down
-
-
-def shards(token_ids, lengths, groups, table, w_qkv, w_out, w_up, w_down, gains, biases):
-    pair_count = token_ids.shape[0]
-    vocab_rows = table.shape[0]
-    model_width = table.shape[1]
-    flat_ids = token_ids.reshape(-1)
-    token_count = flat_ids.shape[0]
-    device_total = lax.axis_size(("wide", "narrow"))
-    rank_at = lax.axis_index(("wide", "narrow"))
-    slot_cap = max(2, 2 * token_count // device_total)
-    owner_of = flat_ids // vocab_rows
-    local_of = flat_ids - owner_of * vocab_rows
-    owner_hits = (owner_of[:, None] == jnp.arange(device_total)[None, :]).astype(jnp.int32)
-    rank_in = jnp.sum(jnp.cumsum(owner_hits, axis=0) * owner_hits, axis=1) - 1
-    slot_of = owner_of * slot_cap + rank_in
-    id_slots = jnp.full((device_total * slot_cap,), -1, jnp.int32).at[slot_of].set(local_of)
-    id_slots = id_slots.reshape(device_total, slot_cap)
-    asked = lax.all_to_all(id_slots, ("wide", "narrow"), split_axis=0, concat_axis=0, tiled=True)
-    valid = asked >= 0
-    found = jnp.take(table, jnp.clip(asked, 0, vocab_rows - 1), axis=0)
-    found = jnp.where(valid[..., None], found, jnp.zeros((), table.dtype))
-    returned = lax.all_to_all(found, ("wide", "narrow"), split_axis=0, concat_axis=0, tiled=True)
-    sent_lengths = lengths.reshape(-1)
-
-    core = lax.axis_index("narrow") % 2
-    own, tile = own_units(w_qkv[0], w_out[0], w_up[0], w_down[0], gains[0], biases[0], groups, core)
-    x_low = returned.reshape(-1, model_width)[slot_of]
-    kept = forward_pass(sent_lengths, own, tile, x_low)
-    gathered, vectors, h1, h2, inv, norm_low, act, gate, qkv, prob, ctx, d_pool, loss_tile = kept
-    loss_terms = loss_tile[:4, :2]
-    token_grads, sent_rows, reduced, d_vectors = backward_pass(
-        sent_lengths, vectors, d_pool, x_low, gathered, h1, h2, inv, norm_low, act, gate, qkv, prob, ctx
+    lane = jnp.arange(128)
+    place = jnp.where(lane < 48, lane // 6, jnp.where(lane < 64, 8, (lane - 64) // 4))
+    spread = jnp.where((place == rank_at % 8)[None, :], spread, jnp.zeros((), bf))
+    sent = jnp.concatenate([units, jnp.broadcast_to(spread[None], (8, 12, 128))], axis=1)
+    halves = w_down[0].reshape(24, 2, 3, 128).transpose(1, 2, 0, 3).reshape(2, 72, 128)
+    halves = jnp.pad(halves, ((0, 0), (0, 8), (0, 0)))
+    lens = lengths.reshape(-1)
+    kept = forward_pass(lens, sent, halves, hot, local, table)
+    w, vecs, h1, h2, inv, nl, act, gate, qkv, prob, ctx, x, d_pool, loss_tile, slots, asked = kept
+    token_grads, row_grads, d_qkv, d_out, d_up, d_down, d_vectors = backward_pass(
+        lens, vecs, d_pool, x, slots, w, h1, h2, inv, nl, act, gate, qkv, prob, ctx
     )
-    d_matrices = own_rows(reduced, core)
     d_vectors = lax.dynamic_slice_in_dim(d_vectors[:12], rank_at * 6, 6, 1)
-    grad_slots = (
-        jnp.zeros((device_total * slot_cap, model_width), jnp.bfloat16).at[slot_of].set(sent_rows)
-    )
-    grad_slots = grad_slots.reshape(device_total, slot_cap, model_width)
-    arrived = lax.all_to_all(
-        grad_slots, ("wide", "narrow"), split_axis=0, concat_axis=0, tiled=True
-    )
-    target_slot = jnp.where(asked >= 0, asked, vocab_rows).reshape(-1)
-    table_grads = (
-        jnp.zeros((vocab_rows, model_width), jnp.float32)
-        .at[target_slot]
-        .add(arrived.reshape(-1, model_width).astype(jnp.float32), mode="drop")
-    )
-    token_grads = token_grads.reshape(pair_count, 2, SEQ, model_width)
     return (
-        loss_terms,
-        token_grads,
-        table_grads,
-        d_matrices[0][None],
-        d_matrices[1][None],
-        d_matrices[2][None],
-        d_matrices[3][None],
+        loss_tile[:4, :2],
+        token_grads.reshape(token_ids.shape + (768,)),
+        table_sums(row_grads, asked, table_rows),
+        d_qkv[None],
+        d_out[None],
+        d_up[None],
+        d_down[None],
         d_vectors[None, :2],
         d_vectors[None, 2:],
     )

time: 325 us -> 277 us (0.85)
  Pallas kernels: 188 us -> 255 us
  waiting for transfers between devices: 45.1 us -> 0 us
  starting transfers between devices: 38.6 us -> 0 us
  local copies, waits for them, and re-layouts: 32.9 us -> 16.8 us
  other arithmetic: 18.3 us -> 3.88 us
    all_to_all x5 -> x0, waiting for transfers between devices: 45 us -> none  [the longest x1 21 us: shards(): lax.all_to_all(found, ('wide', 'narrow'), split_axis=0, concat_axis=0, ti...]
    pallas_call x1 -> x2, Pallas kernels: 76.3 us -> 113 us  [the longest x1 104 us: backward_pass(): pl.pallas_call(backward_kernel, out_shape=[jax.ShapeDtypeStruct(*s) for s...]
    all_to_all x5 -> x0, starting transfers between devices: 36.1 us -> none  [the longest x1 11.5 us: shards(): lax.all_to_all(id_slots, ('wide', 'narrow'), split_axis=0, concat_axis=0,...]
    pallas_call x1, Pallas kernels: 111 us -> 142 us  [forward_pass(): pl.pallas_call(forward_kernel, out_shape=[jax.ShapeDtypeStruct(*s) for s...]
    scatter-add x1 -> x0, other arithmetic: 12.6 us -> none  [shards(): table_grads = jnp.zeros((vocab_rows, model_width), jnp.float32).at[target...]
    gather x2 -> x0, local copies, waits for them, and re-layouts: 10.7 us -> none  [the longest x1 7.96 us: shards(): found = jnp.take(table, jnp.clip(asked, 0, vocab_rows - 1), axis=0)]
    scatter x2 -> x0, local copies, waits for them, and re-layouts: 6.81 us -> none  [the longest x1 4.37 us: shards(): jnp.zeros((device_total * slot_cap, model_width), jnp.bfloat16).at[slot_of]]
    unnamed x28 -> x23, local copies, waits for them, and re-layouts: 2.71 us -> 8.16 us
  transfers between devices with their start and end apart: 7 -> 0, of which waited for: 5 -> 0; matrix products, arithmetic and copies ran while one was open for 8% -> 0% of each run, Pallas kernels for 0% -> 0%
where the time goes in v3:
time: 277 us
  Pallas kernels  255 us (92%)
  local copies, waits for them, and re-layouts  16.8 us (6%)
  other arithmetic  3.88 us (1%)
    pallas_call x1, Pallas kernels, forward_pass(): pl.pallas_call(forward_kernel, out_shape=[jax.ShapeDtypeStruct(*s) for s...  142 us
    pallas_call x1, Pallas kernels, backward_pass(): pl.pallas_call(backward_kernel, out_shape=[jax.ShapeDtypeStruct(*s) for s...  104 us
    pallas_call x1, Pallas kernels, table_sums(): pl.pallas_call(table_kernel, out_shape=jax.ShapeDtypeStruct((table_rows,...  9.16 us
    unnamed x23, local copies, waits for them, and re-layouts  8.16 us

profile of v3, /device:TPU:1, one launch (start us, length us, event | category | flops | bytes accessed | tf_op | source)
XLA Modules:
  0.0 276.6 jit_solution(5476463002265347371)
XLA Ops:
  0.6 0.8 copy.31
  1.4 0.6 reshape.153.lens_ref
  2.0 0.7 convert_bitcast_fusion
  2.7 0.1 copy.48
  2.8 0.1 copy.37
  2.9 0.8 copy.34
  3.6 0.8 pad_maximum_fusion.3
  4.4 0.1 copy.35
  4.5 0.1 concatenate.26
  4.6 0.1 pad.11.clone
  4.7 0.1 pad.9.clone
  4.8 0.1 maximum_select_fusion
  4.9 0.8 stack.9
  5.8 0.8 pad_maximum_fusion.2
  6.6 0.1 pad_maximum_fusion.1
  6.8 0.7 pad_maximum_fusion.sent_ref
  7.4 0.8 reshape_squeeze.3
  8.2 0.6 pad.5.halves_ref
  8.9 0.8 reshape.156
  9.7 0.8 fusion.hot_ref
  10.4 0.8 broadcast_in_dim.66.local_ref
  11.3 141.8 %forward_pass.1 = (bf16[3,2,3,4,4,4,48,128]{7,6,5,4,3,2,1,0:T(8,128)(2,1)}, f32[16,768]{1,0:T(8,128)}, f32[512,768]{1,0:T(8,128)}, f32[512,768]{1,0:T(8,128)}, f...) custom-call(s32[8]{0:T(128)} %reshape.153.lens_ref, ...), custom_call_target="tpu_custom_call" | custom-call | tf_op jit(solution)/shard_map/forward_pass/pallas_call | solution.py:726
  153.1 0.7 slice.12
  153.8 0.7 copy.41
  154.5 104.2 %backward_pass.1 = (f32[512,768]{1,0:T(8,128)}, bf16[128,16,384]{2,1,0:T(8,128)(2,1)}, f32[6,2304]{1,0:T(8,128)}, f32[6,768]{1,0:T(8,128)}, f32[6,3072]{1,0:T(8,...) custom-call(s32[8]{0:T(128)} %reshape.153.lens_ref, f32[16,768]{1,0:T(8,128)} %get-tuple-element.33.vec_ref, ...), custom_call_target="tpu_custom_call" | custom-call | tf_op jit(solution)/shard_map/backward_pass/pallas_call | solution.py:1326
  258.6 0.0 copy-start
  258.6 1.4 copy-done
  260.0 0.0 copy-start.1
  260.0 0.8 copy-done.1
  260.8 0.0 copy-start.5
  260.8 0.0 copy-start.6
  260.8 0.0 copy-start.3
  260.8 0.0 copy-start.2
  260.8 9.2 %table_sums.1 = f32[3920,768]{1,0:T(8,128)} custom-call(bf16[128,16,384]{2,1,0:T(8,128)(2,1)S(1)} %copy-done, f32[8,1024]{1,0:T(8,128)S(1)} %copy-done.1), custom_call_target="tpu_custom_call" | custom-call | tf_op jit(solution)/shard_map/table_sums/pallas_call | solution.py:1355
  270.0 0.0 copy-start.4
  270.0 0.0 copy-done.5
  270.0 0.7 copy.42
  270.6 0.0 copy-done.6
  270.6 0.6 copy.43
  271.3 0.0 copy-done.3
  271.3 0.7 copy.44
  272.0 1.3 dynamic-slice_bitcast_fusion.1
  273.3 0.8 dynamic-slice_bitcast_fusion
  274.1 0.7 copy.45
  274.8 0.0 copy-done.2
  274.8 1.1 copy.51
  275.9 0.0 copy-done.4
  275.9 0.6 copy.52
  (13 shorter events, 0.2 us)
Async XLA Ops:
  258.6 1.4 copy-start
  260.0 0.8 copy-start.1
  260.8 9.2 %copy-start.5 = (f32[6,2304]{1,0:T(8,128)S(1)}, f32[6,2304]{1,0:T(8,128)}, u32[]{:S(2)}) copy-start(f32[6,2304]{1,0:T(8,128)} %get-tuple-element.50) | copy-start | bytes 165892
  260.8 9.9 %copy-start.6 = (f32[6,768]{1,0:T(8,128)S(1)}, f32[6,768]{1,0:T(8,128)}, u32[]{:S(2)}) copy-start(f32[6,768]{1,0:T(8,128)} %get-tuple-element.51) | copy-start | bytes 55300
  260.8 10.5 %copy-start.3 = (f32[6,3072]{1,0:T(8,128)S(1)}, f32[6,3072]{1,0:T(8,128)}, u32[]{:S(2)}) copy-start(f32[6,3072]{1,0:T(8,128)} %get-tuple-element.52) | copy-start | bytes 221188
  260.8 14.0 %copy-start.2 = (f32[512,768]{1,0:T(8,128)S(1)}, f32[512,768]{1,0:T(8,128)}, u32[]{:S(2)}) copy-start(f32[512,768]{1,0:T(8,128)} %get-tuple-element.47) | copy-start | bytes 4718596
  270.0 6.0 %copy-start.4 = (f32[24,768]{1,0:T(8,128)S(1)}, f32[24,768]{1,0:T(8,128)}, u32[]{:S(2)}) copy-start(f32[24,768]{1,0:T(8,128)} %get-tuple-element.53) | copy-start | bytes 221188

commit v4 on v3

--- a/solution.py
+++ b/solution.py
@@ -45,13 +45,22 @@
 
 
 class Gather:
-    def __init__(self, out, send_sem, recv_sem, spot, core, dims):
+    def __init__(self, out, fifteen, send_sem, recv_sem, spot, core, dims):
         self.out, self.send_sem, self.recv_sem = out, send_sem, recv_sem
         self.spot, self.core, self.dims = spot, core, dims
+        self.fifteen = fifteen
         self.sent = []
 
     def block(self, r, o, spans, core):
         return self.out.at[(r, core, o) + tuple(pl.ds(*spans[d]) for d in self.dims)]
+
+    def here(self, o):
+        return {d: (self.spot[d], 1) for d in range(3)}
+
+    def plane(self, o, at, half=None):
+        first, second, ring = ORDERS[o]
+        spans = {first: (0, RING) if half is None else (2 * half, 2), second: (0, RING), ring: (at, 1)}
+        return spans
 
     def push(self, r, o, event, spans, there, core=None, src=None):
         dst = self.block(r, o, spans, self.core)
@@ -64,90 +73,77 @@
             device_id_type=MESH,
         )
         copy.start()
-        self.sent.append(copy)
+        return copy
 
     def landed(self, r, o, event, spans, core=None):
         dst = self.block(r, o, spans, self.core if core is None else core)
         pltpu.make_async_copy(dst, dst, self.recv_sem.at[r, o, event]).wait()
 
-    def spans(self, o, phase, at, half=None):
-        order = ORDERS[o]
-        spans = {}
-        for k, d in enumerate(order):
-            if k < phase:
-                spans[d] = (0, RING)
-            elif k == phase:
-                spans[d] = (at, 1)
-            else:
-                spans[d] = (self.spot[d], 1)
-        if half is not None:
-            spans[order[0]] = (2 * half, 2)
-        return spans
-
-    def ring(self, o, phase):
-        d = ORDERS[o][phase]
+    def begin(self, r, o, src):
+        first, second, ring = ORDERS[o]
+        here = self.here(o)
+
+        def one(k, _):
+            there = moved(moved(self.spot, first, k % RING), second, k // RING)
+            self.push(r, o, 0, here, there, src=src)
+            return 0
+
+        lax.fori_loop(1, 16, one, 0)
+
+    def plane_done(self, r, o, sem):
+        pltpu.make_async_copy(self.fifteen, self.fifteen, sem.at[r, o, 0]).wait()
+
+    def planes(self, r, o):
+        self.plane_done(r, o, self.recv_sem)
+        self.share(r, o, 5, self.plane(o, self.spot[ORDERS[o][2]]))
+
+    def ring(self, o):
+        d = ORDERS[o][2]
         v = self.spot[d]
         up, down = moved(self.spot, d, 1), moved(self.spot, d, -1)
         return v, (v - 1) % RING, (v + 1) % RING, (v + 2) % RING, up, down
 
-    def begin(self, r, o, src):
-        v, low, high, far, up, down = self.ring(o, 0)
-        here = self.spans(o, 0, v)
-        self.push(r, o, 0, here, up, src=src)
-        self.push(r, o, 1, here, down, src=src)
-        self.push(r, o, 2, here, moved(self.spot, ORDERS[o][0], 2), src=src)
-
-    def first_done(self, r, o):
-        v, low, high, far, up, down = self.ring(o, 0)
-        self.landed(r, o, 0, self.spans(o, 0, low))
-        self.landed(r, o, 1, self.spans(o, 0, high))
-        self.landed(r, o, 2, self.spans(o, 0, far))
-        self.share(r, o, 11, self.spans(o, 1, self.spot[ORDERS[o][1]]))
-
     def share(self, r, o, event, spans):
-        self.push(r, o, event, spans, self.spot, 1 - self.core)
-
-    def spread(self, r, o, phase, direct=False):
-        v, low, high, far, up, down = self.ring(o, phase)
-        event = 3 + 4 * (phase - 1)
-        here = self.spans(o, phase, v)
-        self.push(r, o, event, here, up)
-        self.push(r, o, event + 1, here, down)
+        self.sent.append(self.push(r, o, event, spans, self.spot, 1 - self.core))
+
+    def spread(self, r, o, direct=False):
+        v, low, high, far, up, down = self.ring(o)
+        here = self.plane(o, v)
+        self.sent.append(self.push(r, o, 1, here, up))
+        self.sent.append(self.push(r, o, 2, here, down))
         if direct:
-            self.push(r, o, event + 2, here, moved(self.spot, ORDERS[o][phase], 2))
-
-    def relay(self, r, o, phase, direct=False):
-        v, low, high, far, up, down = self.ring(o, phase)
-        event, shared = 3 + 4 * (phase - 1), 11 + 3 * (phase - 1)
-        self.landed(r, o, event, self.spans(o, phase, low))
-        if not direct:
-            self.push(r, o, event + 2, self.spans(o, phase, low, 0), up)
-        self.landed(r, o, event + 1, self.spans(o, phase, high))
-        if not direct:
-            self.push(r, o, event + 3, self.spans(o, phase, high, 1), down)
-        self.share(r, o, shared + 1, self.spans(o, phase, low))
-        self.share(r, o, shared + 2, self.spans(o, phase, high))
-
-    def finish(self, r, o, phase, direct=False):
-        v, low, high, far, up, down = self.ring(o, phase)
-        event, shared = 3 + 4 * (phase - 1), 11 + 3 * (phase - 1)
-        if direct:
-            self.landed(r, o, event + 2, self.spans(o, phase, far))
-        else:
-            self.landed(r, o, event + 2, self.spans(o, phase, far, 0))
-            self.landed(r, o, event + 3, self.spans(o, phase, far, 1))
-        self.share(r, o, shared + 3, self.spans(o, phase, far))
+            self.sent.append(self.push(r, o, 3, here, moved(self.spot, ORDERS[o][2], 2)))
+
+    def relay(self, r, o):
+        v, low, high, far, up, down = self.ring(o)
+        self.landed(r, o, 1, self.plane(o, low))
+        self.sent.append(self.push(r, o, 3, self.plane(o, low, 0), up))
+        self.landed(r, o, 2, self.plane(o, high))
+        self.sent.append(self.push(r, o, 4, self.plane(o, high, 1), down))
+        self.share(r, o, 6, self.plane(o, low))
+        self.share(r, o, 7, self.plane(o, high))
+
+    def finish(self, r, o):
+        v, low, high, far, up, down = self.ring(o)
+        self.landed(r, o, 3, self.plane(o, far, 0))
+        self.landed(r, o, 4, self.plane(o, far, 1))
+        self.share(r, o, 8, self.plane(o, far))
+
+    def collect(self, r, o):
+        v, low, high, far, up, down = self.ring(o)
+        for k, at in enumerate((low, high, far)):
+            self.landed(r, o, 1 + k, self.plane(o, at))
+            self.share(r, o, 6 + k, self.plane(o, at))
 
     def shared_done(self, r, o):
-        other = 1 - self.core
-        self.landed(r, o, 11, self.spans(o, 1, self.spot[ORDERS[o][1]]), other)
-        for phase in (1, 2):
-            v, low, high, far, up, down = self.ring(o, phase)
-            shared = 11 + 3 * (phase - 1)
-            for k, at in enumerate((low, high, far)):
-                self.landed(r, o, shared + 1 + k, self.spans(o, phase, at), other)
-
-    def drain(self):
+        v, low, high, far, up, down = self.ring(o)
+        for k, at in enumerate((v, low, high, far)):
+            self.landed(r, o, 5 + k, self.plane(o, at), 1 - self.core)
+
+    def drain(self, rounds):
+        for r in range(rounds):
+            for o in range(3):
+                self.plane_done(r, o, self.send_sem)
         for copy in self.sent:
             copy.wait_send()
 
@@ -226,20 +222,32 @@
     return high.astype(jnp.bfloat16), (value - 64.0 * high).astype(jnp.bfloat16)
 
 
-def token_slots(hot_ref, local_ref):
-    hot = hot_ref[...]
+def token_slots(ids_ref, table_rows):
+    f32, bf = jnp.float32, jnp.bfloat16
+    sents = jnp.concatenate([ids_ref[s // 2, s % 2 : s % 2 + 1, :] for s in range(8)], axis=0)
+    row = lax.broadcasted_iota(jnp.int32, (512, 8), 0)
+    col = lax.broadcasted_iota(jnp.int32, (512, 8), 1)
+    member_of = (row // SEQ == col).astype(bf)
+    wide_ids = jnp.zeros((512, SEQ), f32)
+    for shift in (0, 7, 14):
+        digit = ((sents >> shift) & 127).astype(f32).astype(bf)
+        wide_ids = wide_ids + mm(member_of, digit) * float(1 << shift)
+    row = lax.broadcasted_iota(jnp.int32, (512, SEQ), 0)
+    col = lax.broadcasted_iota(jnp.int32, (512, SEQ), 1)
+    name = jnp.sum(jnp.where(row % SEQ == col, wide_ids, 0.0), axis=1, keepdims=True)
+    owner = jnp.floor((name + 0.5) * (1.0 / table_rows))
+    local = name - owner * float(table_rows) + 1.0
+    lane = lax.broadcasted_iota(jnp.int32, (512, 128), 1).astype(f32)
+    hot = (lane == owner).astype(bf)
     row = lax.broadcasted_iota(jnp.int32, (512, 512), 0)
     col = lax.broadcasted_iota(jnp.int32, (512, 512), 1)
-    before = mm((col < row).astype(jnp.bfloat16), hot)
-    lane = lax.broadcasted_iota(jnp.int32, (512, 128), 1).astype(jnp.float32)
-    wide_hot = hot.astype(jnp.float32)
-    rank = jnp.sum(before * wide_hot, axis=1, keepdims=True)
-    slot = jnp.sum(wide_hot * lane, axis=1, keepdims=True) * 8.0 + rank
-    high, low = digits(local_ref[...])
-    zero = jnp.zeros((), jnp.bfloat16)
+    before = mm((col < row).astype(bf), hot)
+    rank = jnp.sum(jnp.where(lane == owner, before, 0.0), axis=1, keepdims=True)
+    high, low = digits(jnp.broadcast_to(local, (512, 128)))
+    zero = jnp.zeros((), bf)
     here = lane == rank
     both = mm_tn(hot, jnp.concatenate([jnp.where(here, high, zero), jnp.where(here, low, zero)], axis=1))
-    return slot, both[:, :128] * 64.0 + both[:, 128:]
+    return owner * 8.0 + rank, both[:, :128] * 64.0 + both[:, 128:]
 
 
 def slot_hot(slot_ref):
@@ -249,23 +257,25 @@
 
 
 def forward_kernel(
-    lens_ref, sent_ref, halves_ref, hot_ref, local_ref, table_in,
+    lens_ref, groups_ref, ids_ref, wq_ref, wo_ref, wu_ref, wd_ref, gains_ref, bias_ref, table_in,
     w_out, vec_out, h1_out, h2_out, inv_out, nl_out, act_out, gp_out, qkv_out, prob_out, ctx_out, x_out,
     dpool_out, loss_out, slot_out, asked_out,
     w, vecs, tiles, h1, h2, inv, nl, act, gp, qkv, prob, ctx, x_ref, resid, pooled, rnorm, pool_own, pool_swap, pool_all,
-    left3, right3, stats, own, near, half_got, table, ids_out, ids_in, ids, asked, rows_out, rows_in, row_mat,
+    left3, right3, stats, own, sent_ref, near, halves_ref, half_got, table, ids_out, ids_in, ids, asked, rows_out, rows_in,
+    row_mat, units_size, pool_size,
     send_sem, recv_sem, local_sem, pool_send, pool_recv, tile_send, tile_recv, swap_sem, load_sem, save_sem,
     near_send, near_recv, ids_sem, rows_sem, table_sem,
 ):
     spot, core = where_am_i()
     me = lax.axis_index("wide") * 8 + lax.axis_index("narrow")
+    mine = spot[0] * 2 + core
     bf, f32 = jnp.bfloat16, jnp.float32
     all_here = greet_all()
     table_rows = table_in.shape[0]
     get_table = pltpu.make_async_copy(table_in, table.at[pl.ds(0, table_rows)], table_sem.at[0])
     get_table.start()
     table[pl.ds(table_rows, 4096 - table_rows), :] = jnp.zeros((4096 - table_rows, 768), bf)
-    slot, wanted = token_slots(hot_ref, local_ref)
+    slot, wanted = token_slots(ids_ref, table_rows)
     slot_out[...] = jnp.broadcast_to(slot, (512, 128))
     ids[...] = wanted
 
@@ -274,9 +284,32 @@
         return 0
 
     lax.fori_loop(0, 128, row_out, 0)
+
+    for c in range(2):
+        for o in range(3):
+            for x in range(RING):
+                n, j = c * 12 + o * 4 + x, 2 * x + c
+                source = wq_ref if n < 18 else wo_ref
+                cut = slice(128 * (n % 18), 128 * (n % 18) + 128)
+                sent_ref[j, 6 * o : 6 * o + 6, :] = source[0, :, cut].astype(f32)
+                sent_ref[j, 18 + 6 * o : 24 + 6 * o, :] = wu_ref[0, :, 128 * n : 128 * n + 128].astype(f32)
+    lane = lax.broadcasted_iota(jnp.int32, (8, 128), 1)
+    place = (lane == 6 * mine + lax.broadcasted_iota(jnp.int32, (8, 128), 0)).astype(bf)[0:6]
+    named = jnp.zeros((1, 128), f32)
+    for p in range(4):
+        named = named + jnp.where(lane[0:1] == 64 + 4 * mine + p, groups_ref[p].astype(f32), 0.0)
+    gain_rows, bias_rows = mm(gains_ref[0], place), mm_tn(bias_ref[0], place)
+    for j in range(8):
+        sent_ref[j, 36:38, :] = gain_rows
+        sent_ref[j, 38:48, :] = bias_rows
+        sent_ref[j, 36:37, :] = sent_ref[j, 36:37, :] + named
+    for o in range(3):
+        a, b = wd_ref[0, :, 128 * o : 128 * o + 128], wd_ref[0, :, 384 + 128 * o : 512 + 128 * o]
+        a, b = a.astype(f32), b.astype(f32)
+        halves_ref[0, o] = jnp.where(core == 0, a, b)
+        halves_ref[1, o] = jnp.where(core == 0, b, a)
     all_here()
 
-    mine = spot[0] * 2 + core
     sent = []
     for k in range(1, 8):
         there = (mine + k) % 8
@@ -287,7 +320,7 @@
         copy.start()
         sent.append(copy)
     copy = pltpu.make_async_remote_copy(
-        src_ref=halves_ref.at[1 - core], dst_ref=half_got, send_sem=near_send.at[0], recv_sem=near_recv.at[0],
+        src_ref=halves_ref.at[1], dst_ref=half_got, send_sem=near_send.at[0], recv_sem=near_recv.at[0],
         device_id=device_at(spot, 1 - core), device_id_type=MESH,
     )
     copy.start()
@@ -313,27 +346,25 @@
     col = lax.broadcasted_iota(jnp.int32, (288, 384), 1)
     unit, at = row // UNIT, row % UNIT
     pick = col == at // 6 * UNIT + unit * 6 + at % 6
-    units = mm(pick.astype(bf), near[...].reshape(384, 128)).astype(bf)
+    units = mm(pick.astype(bf), near[...].reshape(384, 128).astype(bf)).astype(bf)
     for r in range(2):
         for o in range(3):
             first_row = UNIT * (3 * r + o)
             own[r, o] = units[first_row : first_row + UNIT].reshape(1, 1, 1, UNIT, 128)
-    kept, got = halves_ref[core].astype(f32), half_got[...].astype(f32)
     for o in range(3):
-        a, b = kept[24 * o : 24 * o + 24], got[24 * o : 24 * o + 24]
+        a, b = halves_ref[0, o], half_got[o]
         upper, lower = jnp.where(core == 0, a, b), jnp.where(core == 0, b, a)
         own[2, o] = jnp.concatenate([upper, lower], axis=0).astype(bf).reshape(1, 1, 1, UNIT, 128)
     small = jnp.zeros((16, 128), f32)
     for j in range(8):
-        small = small + near[j, 32:48, :].astype(f32)
+        small = small + near[j, 32:48, :]
     tiles[pl.ds(spot[1], 1), pl.ds(spot[2], 1)] = small.astype(bf).reshape(1, 1, 16, 128)
 
-    g = Gather(w_out, send_sem, recv_sem, spot, core, (0, 1, 2))
+    g = Gather(w_out, units_size, send_sem, recv_sem, spot, core, (0, 1, 2))
     every = [(r, o) for r in range(3) for o in range(3)]
     keep = []
     for r, o in every:
-        here = g.spans(o, 0, spot[ORDERS[o][0]])
-        copy = pltpu.make_async_copy(own.at[r, o], g.block(r, o, here, core), local_sem.at[r, o])
+        copy = pltpu.make_async_copy(own.at[r, o], g.block(r, o, g.here(o), core), local_sem.at[r, o])
         copy.start()
         keep.append(copy)
         g.begin(r, o, own.at[r, o])
@@ -360,12 +391,8 @@
             pltpu.make_async_copy(ref, ref, tile_recv.at[3 * phase + k]).wait()
 
     tile_spread(0)
-    for (r, o), copy in zip(every, keep):
+    for copy in keep:
         copy.wait()
-        g.first_done(r, o)
-        g.spread(r, o, 1, r == 0)
-    tile_landed(0)
-    tile_spread(1)
 
     others = ids_in.at[pl.ds(0, 127)]
     pltpu.make_async_copy(others, others, ids_sem.at[1]).wait()
@@ -418,19 +445,17 @@
 
     find(0)
     rows_in[me] = rows_out[0]
+    tile_landed(0)
+    tile_spread(1)
     for o in range(3):
-        g.relay(0, o, 1, True)
+        g.planes(0, o)
+        g.spread(0, o)
+    find(1)
     for o in range(3):
-        g.finish(0, o, 1, True)
-        g.spread(0, o, 2)
+        g.relay(0, o)
     for r in (1, 2):
         for o in range(3):
-            g.relay(r, o, 1)
-    find(1)
-    for r in (1, 2):
-        for o in range(3):
-            g.finish(r, o, 1)
-            g.spread(r, o, 2)
+            g.planes(r, o)
     tile_landed(1)
 
     row_at = lax.broadcasted_iota(jnp.int32, (128, 768), 0)
@@ -455,11 +480,9 @@
     def load(r, o, c):
         return pltpu.make_async_copy(w_out.at[r, c, o], w.at[r, c, o], load_sem.at[r, c, o])
 
-    def arrive(r):
+    def collect(r):
         for o in range(3):
-            g.relay(r, o, 2)
-        for o in range(3):
-            g.finish(r, o, 2)
+            g.collect(r, o)
             load(r, o, core).start()
 
     def arrived(r):
@@ -471,9 +494,13 @@
             load(r, o, 1).wait()
 
     save(vecs, vec_out, 0)
-    arrive(0)
+    for o in range(3):
+        g.finish(0, o)
+        load(0, o, core).start()
     others = rows_in.at[pl.ds(0, 127)]
     pltpu.make_async_copy(others, others, rows_sem.at[1]).wait()
+    for o in range(3):
+        g.spread(1, o, True)
     for q in range(8):
         row_mat[128 * q : 128 * q + 128, :] = unpack_rows(rows_in[16 * q : 16 * q + 16])
     slots_hot = slot_hot(slot_out)
@@ -493,13 +520,14 @@
         return 0
 
     lax.fori_loop(0, 9, qkv_step, 0)
+    for o in range(3):
+        g.spread(2, o, True)
     save(qkv, qkv_out, 1)
-    arrive(1)
 
     def attend(s, _):
         rows = pl.ds(pl.multiple_of(s * SEQ, SEQ), SEQ)
         slot = lax.broadcasted_iota(jnp.int32, (SEQ, 256), 0)
-        live = slot < lens_ref[s]
+        live = slot < lens_ref[s % 2, s // 2]
         for p in range(3):
             query, key_part, value = qkv[p, rows, :], qkv[3 + p, rows, :], qkv[6 + p, rows, :]
             scores = mm_nt(key_part, spread_heads(query, mask)) * 0.125
@@ -510,7 +538,9 @@
             ctx[p, rows, :] = gather_heads(mm_tn(probs.astype(bf), value), mask).astype(bf)
         return 0
 
-    lax.fori_loop(0, 8, attend, 0)
+    lax.fori_loop(0, 4, attend, 0)
+    collect(1)
+    lax.fori_loop(4, 8, attend, 0)
     save(prob, prob_out, 2)
     save(ctx, ctx_out, 3)
     context = jnp.concatenate([ctx[0], ctx[1], ctx[2]], axis=1)
@@ -534,7 +564,7 @@
     save(h1, h1_out, 4)
     save(nl, nl_out, 5)
     arrived(1)
-    arrive(2)
+    collect(2)
 
     def up_step(n2, _):
         weight = panel(w, 1, n2)
@@ -574,8 +604,8 @@
         h2[rows, :] = scaled
         inv[1, rows, :] = jnp.broadcast_to(inverse, (SEQ, 128))
         state = scaled * vecs[1:2, :] + vecs[7:8, :]
-        live = lax.broadcasted_iota(jnp.int32, (SEQ, 768), 0) < lens_ref[s]
-        mean_vec = jnp.sum(jnp.where(live, state, 0.0), axis=0, keepdims=True) / lens_ref[s].astype(f32)
+        live = lax.broadcasted_iota(jnp.int32, (SEQ, 768), 0) < lens_ref[s % 2, s // 2]
+        mean_vec = jnp.sum(jnp.where(live, state, 0.0), axis=0, keepdims=True) / lens_ref[s % 2, s // 2].astype(f32)
         r = lax.rsqrt(jnp.sum(mean_vec * mean_vec, axis=1, keepdims=True) + pool_eps)
         pooled[s] = mean_vec * r
         rnorm[s] = jnp.broadcast_to(r, (1, 768))
@@ -600,7 +630,7 @@
     kind = jnp.concatenate(
         [jnp.where(first, sources, got), jnp.where(first, got, targets)], axis=0
     )
-    q = Gather(pool_all, pool_send, pool_recv, spot, core, (1, 2, 0))
+    q = Gather(pool_all, pool_size, pool_send, pool_recv, spot, core, (1, 2, 0))
     for o in range(3):
         unit = jnp.concatenate([kind[:, 256 * o : 256 * o + 128], kind[:, 256 * o + 128 : 256 * o + 256]], axis=0)
         here = (pl.ds(spot[1], 1), pl.ds(spot[2], 1), pl.ds(spot[0], 1))
@@ -608,17 +638,10 @@
     for o in range(3):
         q.begin(0, o, None)
     for o in range(3):
-        q.first_done(0, o)
-        q.spread(0, o, 1, True)
+        q.planes(0, o)
+        q.spread(0, o, True)
     for o in range(3):
-        q.relay(0, o, 1, True)
-    for o in range(3):
-        q.finish(0, o, 1, True)
-        q.spread(0, o, 2)
-    for o in range(3):
-        q.relay(0, o, 2)
-    for o in range(3):
-        q.finish(0, o, 2)
+        q.collect(0, o)
     for o in range(3):
         q.shared_done(0, o)
 
@@ -681,16 +704,17 @@
         grad = mm(mix_high, high_cols) + mm(mix_high, low_cols) + mm(mix_low, high_cols)
         grads.append(logit_scale * jnp.where(first, grad[0:4], grad[4:8]))
         terms.append(jnp.where(first, (lse - diagonal)[0:4], (lse - diagonal)[4:8]))
+    row = lax.broadcasted_iota(jnp.int32, (4, 128), 0)
     lane = lax.broadcasted_iota(jnp.int32, (4, 128), 1)
-    both = jnp.where(lane == 0, terms[0], jnp.where(lane == 1, terms[1], 0.0))
-    loss_out[...] = jnp.concatenate([both, jnp.zeros((4, 128), f32)], axis=0)
+    rows = [jnp.sum(jnp.where(row == lane, terms[k], 0.0), axis=0, keepdims=True) for k in range(2)]
+    loss_out[...] = jnp.concatenate(rows + [jnp.zeros((6, 128), f32)], axis=0)
     for s in range(8):
         d_row = grads[s % 2][s // 2 : s // 2 + 1, :]
         row = pooled[s]
         inner = jnp.sum(row * d_row, axis=1, keepdims=True)
-        dpool_out[s] = rnorm[s] * (d_row - row * inner) / lens_ref[s].astype(f32)
-    g.drain()
-    q.drain()
+        dpool_out[s] = rnorm[s] * (d_row - row * inner) / lens_ref[s % 2, s // 2].astype(f32)
+    g.drain(3)
+    q.drain(1)
     for copy in sent:
         copy.wait_send()
     for sem, ref in ((ids_sem, ids_in), (rows_sem, rows_in)):
@@ -700,7 +724,7 @@
         copy.wait()
 
 
-def forward_pass(lens, sent, halves, hot, local, table):
+def forward_pass(lengths, groups, ids, w_qkv, w_out, w_up, w_down, gains, biases, table):
     bf, f32 = jnp.bfloat16, jnp.float32
     shapes = [
         ((3, 2, 3, RING, RING, RING, UNIT, 128), bf),
@@ -726,7 +750,7 @@
     return pl.pallas_call(
         forward_kernel,
         out_shape=[jax.ShapeDtypeStruct(*s) for s in shapes],
-        in_specs=[pl.BlockSpec(memory_space=pltpu.SMEM), vmem, vmem, vmem, vmem, anywhere],
+        in_specs=[pl.BlockSpec(memory_space=pltpu.SMEM)] * 2 + [vmem] * 7 + [anywhere],
         out_specs=[anywhere] * 12 + [vmem] * 4,
         scratch_shapes=[
             pltpu.VMEM(*shapes[0]),
@@ -743,8 +767,10 @@
             pltpu.VMEM((512, 2304), bf),
             pltpu.VMEM((8, 512), f32),
             pltpu.VMEM((3, 3, 1, 1, 1, UNIT, 128), bf),
-            pltpu.VMEM((8, UNIT, 128), bf),
-            pltpu.VMEM((80, 128), bf),
+            pltpu.VMEM((8, UNIT, 128), f32),
+            pltpu.VMEM((8, UNIT, 128), f32),
+            pltpu.VMEM((2, 3, 24, 128), f32),
+            pltpu.VMEM((3, 24, 128), f32),
             pltpu.VMEM((4096, 768), bf),
             pltpu.VMEM((128, 1, 128), f32),
             pltpu.VMEM((128, 1, 128), f32),
@@ -753,11 +779,13 @@
             pltpu.VMEM((128, 16, 384), bf),
             pltpu.VMEM((128, 16, 384), bf),
             pltpu.VMEM((1024, 768), bf),
-            dma((3, 3, 18)),
-            dma((3, 3, 18)),
+            pltpu.VMEM((15, UNIT, 128), bf),
+            pltpu.VMEM((15, 16, 128), f32),
+            dma((3, 3, 9)),
+            dma((3, 3, 9)),
             dma((3, 3)),
-            dma((1, 3, 18)),
-            dma((1, 3, 18)),
+            dma((1, 3, 9)),
+            dma((1, 3, 9)),
             dma((6,)),
             dma((6,)),
             dma((2,)),
@@ -773,50 +801,40 @@
             collective_id=1, has_side_effects=True, vmem_limit_bytes=62 * 1024 * 1024
         ),
         name="forward_pass",
-    )(lens, sent, halves, hot, local, table)
+    )(lengths, groups, ids, w_qkv, w_out, w_up, w_down, gains, biases, table)
 
 
 class Reduce:
-    def __init__(self, parts, bufs, out, send_sem, recv_sem, spot, core):
-        self.parts, self.bufs, self.out = parts, bufs, out
+    def __init__(self, parts, bufs, plane, out, send_sem, recv_sem, spot, core):
+        self.parts, self.bufs, self.plane_in, self.out = parts, bufs, plane, out
         self.send_sem, self.recv_sem = send_sem, recv_sem
         self.spot, self.core = spot, core
         self.sent = []
 
-    def copy(self, src, dst, r, o, event, there, core):
+    def copy(self, src, dst, r, o, event, there):
         copy = pltpu.make_async_remote_copy(
             src_ref=src,
             dst_ref=dst,
             send_sem=self.send_sem.at[r, o, event],
             recv_sem=self.recv_sem.at[r, o, event],
-            device_id=device_at(there, core),
+            device_id=device_at(there, self.core),
             device_id_type=MESH,
         )
         copy.start()
-        self.sent.append(copy)
+        return copy
 
     def landed(self, dst, r, o, event):
         pltpu.make_async_copy(dst, dst, self.recv_sem.at[r, o, event]).wait()
 
-    def spans(self, o, phase, at, half=None):
-        order = ORDERS[o]
-        spans = {}
-        for k, d in enumerate(order):
-            if k < phase:
-                spans[d] = (self.spot[d], 1)
-            elif k == phase:
-                spans[d] = (at, 1)
-            else:
-                spans[d] = (0, RING)
-        if half is not None:
-            spans[order[phase + 1]] = (2 * half, 2)
-        return spans
+    def spans(self, o, at, half=None):
+        ring, first, second = ORDERS[o]
+        return {ring: (at, 1), first: (0, RING) if half is None else (2 * half, 2), second: (0, RING)}
 
     def mine(self, r, o, spans):
         return block_of(self.parts, r, self.core, o, spans)
 
-    def slot(self, r, o, phase, which):
-        return self.bufs[(o * 3 + phase) * 2 + which // 2].at[r, which % 2]
+    def slot(self, r, o, which):
+        return self.bufs[o * 2].at[r, which] if which < 3 else self.bufs[o * 2 + 1].at[0, which - 3]
 
     def add_into(self, into, others):
         sizes = into.shape[:3]
@@ -834,57 +852,72 @@
 
         lax.fori_loop(0, sizes[0] * sizes[1], one, 0)
 
-    def first(self, r, o, phase):
-        d = ORDERS[o][phase]
+    def first(self, r, o):
+        d = ORDERS[o][0]
+        if r > 0:
+            for by in (1, 3, 2):
+                there = moved(self.spot, d, by)
+                src = self.mine(r, o, self.spans(o, there[d]))
+                self.sent.append(self.copy(src, self.slot(r, o, by - 1), r, o, by - 1, there))
+            return
         across = (self.spot[d] + 2) % RING
-        event = 1 + 4 * phase
-        if phase < 2:
-            for half, by in ((0, 1), (1, -1)):
-                src = self.mine(r, o, self.spans(o, phase, across, half))
-                self.copy(src, self.slot(r, o, phase, half), r, o, event + half, moved(self.spot, d, by), self.core)
-        else:
-            src = self.mine(r, o, self.spans(o, phase, across))
-            self.copy(src, self.slot(r, o, phase, 0), r, o, event, moved(self.spot, d, 1), self.core)
-
-    def second(self, r, o, phase):
-        d = ORDERS[o][phase]
-        event = 1 + 4 * phase
+        for half, by in ((0, 1), (1, -1)):
+            src = self.mine(r, o, self.spans(o, across, half))
+            self.sent.append(self.copy(src, self.slot(r, o, 3 + half), r, o, 2 + 3 * half, moved(self.spot, d, by)))
+
+    def second(self, r, o):
+        d = ORDERS[o][0]
         for half, by in ((0, 1), (1, -1)):
             at = (self.spot[d] + by) % RING
-            if phase < 2 or half == 0:
-                view = self.slot(r, o, phase, half)
-                self.landed(view, r, o, event + half)
-                self.add_into(self.mine(r, o, self.spans(o, phase, at, half if phase < 2 else None)), [view])
-            src = self.mine(r, o, self.spans(o, phase, at))
-            self.copy(src, self.slot(r, o, phase, 2 + half), r, o, event + 2 + half, moved(self.spot, d, by), self.core)
-
-    def third(self, r, o, phase):
-        d = ORDERS[o][phase]
-        event = 1 + 4 * phase
-        a, b = self.slot(r, o, phase, 2), self.slot(r, o, phase, 3)
-        self.landed(a, r, o, event + 2)
-        self.landed(b, r, o, event + 3)
-        here = self.mine(r, o, self.spans(o, phase, self.spot[d]))
-        if phase < 2:
-            self.add_into(here, [a, b])
-        else:
-            total = here[0, 0, 0].astype(jnp.float32) + a[0, 0, 0].astype(jnp.float32)
-            self.out[r, o] = total + b[0, 0, 0].astype(jnp.float32)
+            view = self.slot(r, o, 3 + half)
+            self.landed(view, r, o, 2 + 3 * half)
+            self.add_into(self.mine(r, o, self.spans(o, at, half)), [view])
+            src = self.mine(r, o, self.spans(o, at))
+            self.sent.append(self.copy(src, self.slot(r, o, half), r, o, half, moved(self.spot, d, by)))
+
+    def third(self, r, o):
+        ring, first, second = ORDERS[o]
+        views = [self.slot(r, o, k) for k in range(3 if r > 0 else 2)]
+        for k, view in enumerate(views):
+            self.landed(view, r, o, k)
+        self.add_into(self.mine(r, o, self.spans(o, self.spot[ring])), views)
+
+        def one(k, _):
+            there = moved(moved(self.spot, first, k % RING), second, k // RING)
+            src = self.mine(r, o, {d: (there[d], 1) for d in range(3)})
+            self.copy(src, self.plane_in.at[r, o, pl.ds(k, 1), pl.ds(0, 1), pl.ds(0, 1)], r, o, 4, there)
+            return 0
+
+        lax.fori_loop(1, 16, one, 0)
+
+    def fourth(self, r, o):
+        others = self.plane_in.at[r, o, pl.ds(1, 15)]
+        self.landed(others, r, o, 4)
+        here = self.mine(r, o, {d: (self.spot[d], 1) for d in range(3)})
+        total = here[0, 0, 0].astype(jnp.float32)
+        for k in range(1, 16):
+            total = total + self.plane_in[r, o, k, 0, 0].astype(jnp.float32)
+        self.out[r, o] = total
+
+    def drain(self):
+        for r in range(3):
+            for o in range(3):
+                others = self.plane_in.at[r, o, pl.ds(1, 15)]
+                pltpu.make_async_copy(others, others, self.send_sem.at[r, o, 4]).wait()
+        for copy in self.sent:
+            copy.wait_send()
 
 
 def reduce_buffers(rounds):
     bufs = []
     for o in range(3):
-        for phase in range(3):
-            order = ORDERS[o]
-            sizes = [RING] * 3
-            for k in range(phase + 1):
-                sizes[order[k]] = 1
-            half = list(sizes)
-            if phase < 2:
-                half[order[phase + 1]] = 2
-            for s in (half, sizes):
-                bufs.append(pltpu.VMEM((rounds, 2, *s, UNIT, 128), jnp.bfloat16))
+        ring, first, second = ORDERS[o]
+        sizes = [RING] * 3
+        sizes[ring] = 1
+        half = list(sizes)
+        half[first] = 2
+        bufs.append(pltpu.VMEM((rounds, 3, *sizes, UNIT, 128), jnp.bfloat16))
+        bufs.append(pltpu.VMEM((1, 2, *half, UNIT, 128), jnp.bfloat16))
     return bufs
 
 
@@ -901,8 +934,8 @@
     token_out, rows_in, qkv_out, out_out, up_out, down_out, vec_out,
     w, h1, h2, inv, nl, act, gp, qkv, prob, ctx, parts, d2d, d_res, d_low, turned, dvec, vec_slots, red_out, near_out, near_in, half_in, rows_out, *rest,
 ):
-    bufs = rest[:18]
-    send_sem, recv_sem, swap_send, swap_recv, free_sem, vec_send, vec_recv, load_sem, gp_sem, w_sem, near_send, near_recv, rows_sem = rest[18:]
+    bufs, plane_in, rest = rest[:6], rest[6], rest[7:]
+    send_sem, recv_sem, swap_send, swap_recv, free_sem, vec_send, vec_recv, load_sem, gp_sem, w_sem, near_send, near_recv, rows_sem = rest
     me = lax.axis_index("wide") * 8 + lax.axis_index("narrow")
     spot, core = where_am_i()
     bf, f32 = jnp.bfloat16, jnp.float32
@@ -930,7 +963,7 @@
     get_h1, get_ctx = load(h1_in, h1, 4), load(ctx_in, ctx, 5)
     get_qkv, get_prob = load(qkv_in, qkv, 6), load(prob_in, prob, 7)
     all_here = greet_all()
-    red = Reduce(parts, bufs, red_out, send_sem, recv_sem, spot, core)
+    red = Reduce(parts, bufs, plane_in, red_out, send_sem, recv_sem, spot, core)
     swaps = {}
 
     def give(r):
@@ -950,19 +983,21 @@
             view = d2d.at[r % 2, o]
             pltpu.make_async_copy(view, view, swap_recv.at[r, o]).wait()
             red.add_into(parts.at[r, core, o], [view])
-            red.first(r, o, 0)
+            red.first(r, o)
         if r == 2:
             pl.semaphore_signal(free_sem, inc=1, device_id=device_at(spot, 1 - core), device_id_type=MESH)
 
-    def second(r, phase):
+    def second(r):
         for o in range(3):
-            red.second(r, o, phase)
-
-    def third(r, phase):
+            red.second(r, o)
+
+    def third(r):
         for o in range(3):
-            red.third(r, o, phase)
-            if phase < 2:
-                red.first(r, o, phase + 1)
+            red.third(r, o)
+
+    def fourth(r):
+        for o in range(3):
+            red.fourth(r, o)
 
     dvec[0] = jnp.zeros((16, 768), f32)
 
@@ -977,7 +1012,7 @@
 
     def norm_two_step(s, _):
         rows = pl.ds(pl.multiple_of(s * SEQ, SEQ), SEQ)
-        live = lax.broadcasted_iota(jnp.int32, (SEQ, 768), 0) < lens_ref[s]
+        live = lax.broadcasted_iota(jnp.int32, (SEQ, 768), 0) < lens_ref[s % 2, s // 2]
         grad = jnp.where(live, jnp.broadcast_to(dpool_ref[s], (SEQ, 768)), 0.0)
         scaled = h2[rows, :]
         inverse = inv[1, rows, 0:1]
@@ -1048,7 +1083,6 @@
 
     lax.fori_loop(0, 12, up_step, 0)
     give(1)
-    second(2, 0)
     get_w1.wait()
 
     def six_blocks(at, n):
@@ -1068,7 +1102,6 @@
 
     lax.fori_loop(0, RING, up_back_step, 0)
     take(1)
-    third(2, 0)
     get_h1.wait()
 
     def norm_one_step(s, _):
@@ -1084,7 +1117,6 @@
         return 0
 
     lax.fori_loop(0, 8, norm_one_step, 0)
-    second(1, 0)
     get_ctx.wait()
     turned[...] = jnp.concatenate([ctx[0], ctx[1], ctx[2]], axis=1).T
     get_w0.wait()
@@ -1096,8 +1128,7 @@
             n = 18 + 2 * p + k
             parts[0, n // 12, n // 4 % 3, n % 4] = block[:, 128 * k : 128 * k + 128].reshape(RING, RING, UNIT, 128)
         ctx[p] = mm_nt(d_low[...], weight[cut, :]).astype(bf)
-    second(2, 1)
-    third(1, 0)
+    third(2)
     get_qkv.wait()
     get_prob.wait()
     mask = head_mask()
@@ -1139,36 +1170,17 @@
         pltpu.make_async_copy(ref, ref, vec_recv.at[event]).wait()
 
     def vec_start(d):
-        vec_push(1 + 3 * d, dvec.at[d + 1], moved(spot, d, 1), core)
-        vec_push(2 + 3 * d, dvec.at[d + 1], moved(spot, d, -1), core)
-
-    def vec_relay(d):
-        vec_landed(1 + 3 * d)
-        vec_push(3 + 3 * d, vec_slots.at[1 + 3 * d], moved(spot, d, 1), core)
+        for by in (1, 2, 3):
+            vec_push(3 * d + by, dvec.at[d + 1], moved(spot, d, by), core)
 
     def vec_add(d):
-        vec_landed(2 + 3 * d)
-        vec_landed(3 + 3 * d)
-        sides = vec_slots[1 + 3 * d] + vec_slots[2 + 3 * d]
-        dvec[d + 2] = (dvec[d + 1] + sides) + vec_slots[3 + 3 * d]
+        for by in (1, 2, 3):
+            vec_landed(3 * d + by)
+        sides = vec_slots[1 + 3 * d] + vec_slots[3 + 3 * d]
+        dvec[d + 2] = (dvec[d + 1] + sides) + vec_slots[2 + 3 * d]
 
     vec_push(0, dvec.at[0], spot, 1 - core)
-    turned[...] = x_ref[...].T
-
-    def qkv_step(n2, _):
-        block = mm(turned[...], qkv[n2]).astype(bf)
-        c, o, x = n2 // 6, n2 // 2 % 3, n2 % 2 * 2
-        for k in range(2):
-            parts[0, c, o, x + k] = block[:, 128 * k : 128 * k + 128].reshape(RING, RING, UNIT, 128)
-        return 0
-
-    lax.fori_loop(0, 9, qkv_step, 0)
-    give(0)
-    third(2, 1)
-    second(1, 1)
-    vec_landed(0)
-    dvec[1] = dvec[0] + vec_slots[0]
-    vec_start(0)
+    third(1)
 
     def input_step(t, _):
         low = jnp.concatenate([qkv[3 * t], qkv[3 * t + 1], qkv[3 * t + 2]], axis=1)
@@ -1199,27 +1211,32 @@
     lax.fori_loop(1, 128, hand_back, 0)
     keep_rows = pltpu.make_async_copy(rows_out.at[me], rows_in.at[0], load_sem.at[9])
     keep_rows.start()
+    turned[...] = x_ref[...].T
+
+    def qkv_step(n2, _):
+        block = mm(turned[...], qkv[n2]).astype(bf)
+        c, o, x = n2 // 6, n2 // 2 % 3, n2 % 2 * 2
+        for k in range(2):
+            parts[0, c, o, x + k] = block[:, 128 * k : 128 * k + 128].reshape(RING, RING, UNIT, 128)
+        return 0
+
+    lax.fori_loop(0, 9, qkv_step, 0)
+    give(0)
+    vec_landed(0)
+    dvec[1] = dvec[0] + vec_slots[0]
+    vec_start(0)
+    fourth(2)
     take(0)
-    vec_relay(0)
-    third(1, 1)
-    second(2, 2)
     vec_add(0)
     vec_start(1)
-    second(0, 0)
-    vec_relay(1)
-    second(1, 2)
-    third(2, 2)
-    third(0, 0)
+    fourth(1)
+    second(0)
     vec_add(1)
     vec_start(2)
-    second(0, 1)
-    vec_relay(2)
-    third(1, 2)
-    third(0, 1)
+    third(0)
     vec_add(2)
     vec_out[...] = dvec[4]
-    second(0, 2)
-    third(0, 2)
+    fourth(0)
 
     mine = spot[0] * 2 + core
     for j in range(8):
@@ -1267,7 +1284,8 @@
     pltpu.make_async_copy(others, others, rows_sem.at[0]).wait()
     token_copy.wait()
     keep_rows.wait()
-    for copy in red.sent + vec_sent:
+    red.drain()
+    for copy in vec_sent:
         copy.wait_send()
 
 
@@ -1300,8 +1318,9 @@
         pltpu.VMEM((3, 24, 128), f32),
         pltpu.VMEM((128, 16, 384), bf),
         *reduce_buffers(3),
-        dma((3, 3, 13)),
-        dma((3, 3, 13)),
+        pltpu.VMEM((3, 3, 16, 1, 1, UNIT, 128), bf),
+        dma((3, 3, 6)),
+        dma((3, 3, 6)),
         dma((3, 3)),
         dma((3, 3)),
         pltpu.SemaphoreType.REGULAR,
@@ -1339,73 +1358,77 @@
 TABLE_STEP = 560
 
 
-def table_kernel(rows_ref, asked_ref, out_ref, rows):
+def table_kernel(
+    rows_ref, asked_ref, qkv_ref, out_ref, up_ref, down_ref, vec_ref, loss_ref, token_ref,
+    table_out, token_out, qkv_out, proj_out, up_out, down_out, gain_out, bias_out, loss_out, rows,
+):
     at = pl.program_id(0)
+    token_out[...] = token_ref[...]
 
     @pl.when(at == 0)
     def _():
         for q in range(8):
             rows[128 * q : 128 * q + 128, :] = unpack_rows(rows_ref[16 * q : 16 * q + 16])
+        for i in range(6):
+            qkv_out[i] = qkv_ref[i : i + 1, :]
+            proj_out[i] = out_ref[i : i + 1, :]
+            up_out[i] = up_ref[i : i + 1, :]
+        down_out[0] = down_ref[...]
+        me = lax.axis_index("wide") * 8 + lax.axis_index("narrow")
+        turned = pltpu.roll(vec_ref[...], 768 - 6 * me, 1)[:, :128]
+        gain_out[0] = turned[0:2, 0:6]
+        across = turned.T
+        for i in range(6):
+            bias_out[i] = across[i : i + 1, 2:12]
+        loss_out[...] = loss_ref[0:2, 0:4]
 
     name = (lax.broadcasted_iota(jnp.int32, (TABLE_STEP, 1024), 0) + at * TABLE_STEP).astype(jnp.float32)
-    out_ref[...] = mm((name == asked_ref[0:1, :]).astype(jnp.bfloat16), rows[...])
-
-
-def table_sums(rows, asked, table_rows):
+    table_out[...] = mm((name == asked_ref[0:1, :]).astype(jnp.bfloat16), rows[...])
+
+
+def table_sums(rows, asked, d_qkv, d_out, d_up, d_down, vectors, loss, tokens, table_rows):
+    f32 = jnp.float32
+    ins = (rows, asked, d_qkv, d_out, d_up, d_down, vectors, loss)
+    outs = [(6, 1, 2304), (6, 1, 768), (6, 1, 3072), (1, 24, 768), (1, 2, 6), (6, 1, 10), (2, 4)]
+    steps = table_rows // TABLE_STEP
+    token_step = -(-512 // steps // 8) * 8
+
+    def whole(shape):
+        return pl.BlockSpec(shape, lambda i: (0,) * len(shape))
+
+    token_block = pl.BlockSpec((token_step, 768), lambda i: (i, 0))
     return pl.pallas_call(
         table_kernel,
-        out_shape=jax.ShapeDtypeStruct((table_rows, 768), jnp.float32),
-        grid=(table_rows // TABLE_STEP,),
-        in_specs=[
-            pl.BlockSpec((128, 16, 384), lambda i: (0, 0, 0)),
-            pl.BlockSpec((8, 1024), lambda i: (0, 0)),
-        ],
-        out_specs=pl.BlockSpec((TABLE_STEP, 768), lambda i: (i, 0)),
+        out_shape=[jax.ShapeDtypeStruct(s, f32) for s in [(table_rows, 768), (512, 768)] + outs],
+        grid=(steps,),
+        in_specs=[whole(v.shape) for v in ins] + [token_block],
+        out_specs=[pl.BlockSpec((TABLE_STEP, 768), lambda i: (i, 0)), token_block] + [whole(s) for s in outs],
         scratch_shapes=[pltpu.VMEM((1024, 768), jnp.bfloat16)],
-        compiler_params=pltpu.CompilerParams(vmem_limit_bytes=40 * 1024 * 1024),
+        compiler_params=pltpu.CompilerParams(vmem_limit_bytes=63 * 1024 * 1024),
         name="table_sums",
-    )(rows, asked)
+    )(*ins, tokens)
 
 
 def shards(token_ids, lengths, groups, table, w_qkv, w_out, w_up, w_down, gains, biases):
-    bf, f32 = jnp.bfloat16, jnp.float32
-    flat_ids = token_ids.reshape(-1)
-    table_rows = table.shape[0]
-    rank_at = lax.axis_index(("wide", "narrow"))
-    owner = flat_ids // table_rows
-    hot = (owner[:, None] == jnp.arange(128)[None, :]).astype(bf)
-    local = jnp.broadcast_to((flat_ids - owner * table_rows + 1).astype(f32)[:, None], (512, 128))
-    first = jnp.concatenate([w_qkv[0], w_out[0]], axis=1)
-    units = jnp.stack([first, w_up[0]]).reshape(2, 6, 2, 3, RING, 128)
-    units = units.transpose(4, 2, 0, 3, 1, 5).reshape(8, 36, 128)
-    vectors = jnp.concatenate([gains[0], biases[0]])
-    named = jnp.concatenate([groups.astype(bf)[None], jnp.zeros((11, 4), bf)])
-    spread = jnp.concatenate(
-        [jnp.tile(vectors, (1, 8)), jnp.zeros((12, 16), bf), jnp.tile(named, (1, 8)), jnp.zeros((12, 32), bf)], axis=1
-    )
-    lane = jnp.arange(128)
-    place = jnp.where(lane < 48, lane // 6, jnp.where(lane < 64, 8, (lane - 64) // 4))
-    spread = jnp.where((place == rank_at % 8)[None, :], spread, jnp.zeros((), bf))
-    sent = jnp.concatenate([units, jnp.broadcast_to(spread[None], (8, 12, 128))], axis=1)
-    halves = w_down[0].reshape(24, 2, 3, 128).transpose(1, 2, 0, 3).reshape(2, 72, 128)
-    halves = jnp.pad(halves, ((0, 0), (0, 8), (0, 0)))
-    lens = lengths.reshape(-1)
-    kept = forward_pass(lens, sent, halves, hot, local, table)
+    lens = lengths.T
+    kept = forward_pass(lens, groups, token_ids, w_qkv, w_out, w_up, w_down, gains, jnp.swapaxes(biases, 1, 2), table)
     w, vecs, h1, h2, inv, nl, act, gate, qkv, prob, ctx, x, d_pool, loss_tile, slots, asked = kept
     token_grads, row_grads, d_qkv, d_out, d_up, d_down, d_vectors = backward_pass(
         lens, vecs, d_pool, x, slots, w, h1, h2, inv, nl, act, gate, qkv, prob, ctx
     )
-    d_vectors = lax.dynamic_slice_in_dim(d_vectors[:12], rank_at * 6, 6, 1)
+    table_rows = table.shape[0]
+    sums = table_sums(row_grads, asked, d_qkv, d_out, d_up, d_down, d_vectors, loss_tile, token_grads, table_rows)
+    table_grads, token_grads, d_qkv, d_out, d_up, d_down, d_gains, d_biases, loss_terms = sums
     return (
-        loss_tile[:4, :2],
+        loss_terms.T,
         token_grads.reshape(token_ids.shape + (768,)),
-        table_sums(row_grads, asked, table_rows),
-        d_qkv[None],
-        d_out[None],
-        d_up[None],
-        d_down[None],
-        d_vectors[None, :2],
-        d_vectors[None, 2:],
+        table_grads,
+        jnp.swapaxes(d_qkv, 0, 1),
+        jnp.swapaxes(d_out, 0, 1),
+        jnp.swapaxes(d_up, 0, 1),
+        d_down,
+        d_gains,
+        jnp.transpose(d_biases, (1, 2, 0)),
     )
 
 

time: 277 us -> 235 us (0.85)
  Pallas kernels: 255 us -> 234 us
  local copies, waits for them, and re-layouts: 16.8 us -> 0 us
  other arithmetic: 3.88 us -> 0 us
    pallas_call x1, Pallas kernels: 142 us -> 128 us  [forward_pass(): pl.pallas_call(forward_kernel, out_shape=[jax.ShapeDtypeStruct(*s) for s...]
    pallas_call x1, Pallas kernels: 104 us -> 94.9 us  [backward_pass(): pl.pallas_call(backward_kernel, out_shape=[jax.ShapeDtypeStruct(*s) for s...]
    unnamed x23 -> x0, local copies, waits for them, and re-layouts: 8.16 us -> none
    broadcast_in_dim x6 -> x0, local copies, waits for them, and re-layouts: 2.97 us -> none  [the longest x1 1.33 us: shards(): d_vectors[None, :2]]
where the time goes in v4:
time: 235 us
  Pallas kernels  234 us (100%)
    pallas_call x1, Pallas kernels, forward_pass(): pl.pallas_call(forward_kernel, out_shape=[jax.ShapeDtypeStruct(*s) for s...  128 us
    pallas_call x1, Pallas kernels, backward_pass(): pl.pallas_call(backward_kernel, out_shape=[jax.ShapeDtypeStruct(*s) for s...  94.9 us
    pallas_call x1, Pallas kernels, table_sums(): pl.pallas_call(table_kernel, out_shape=[jax.ShapeDtypeStruct(s, f32) for...  11.4 us

profile of v4, /device:TPU:1, one launch (start us, length us, event | category | flops | bytes accessed | tf_op | source)
XLA Modules:
  0.0 235.0 jit_solution(15846270866115617706)
XLA Ops:
  0.6 127.8 %forward_pass.1 = (bf16[3,2,3,4,4,4,48,128]{7,6,5,4,3,2,1,0:T(8,128)(2,1)}, f32[16,768]{1,0:T(8,128)}, f32[512,768]{1,0:T(8,128)}, f32[512,768]{1,0:T(8,128)}, f...) custom-call(s32[2,4]{1,0:T(2,128)} %bitcast.8, ...), custom_call_target="tpu_custom_call" | custom-call | tf_op jit(solution)/shard_map/forward_pass/pallas_call | solution.py:750
  128.5 94.9 %backward_pass.1 = (f32[512,768]{1,0:T(8,128)}, bf16[128,16,384]{2,1,0:T(8,128)(2,1)}, f32[6,2304]{1,0:T(8,128)}, f32[6,768]{1,0:T(8,128)}, f32[6,3072]{1,0:T(8,...) custom-call(s32[2,4]{1,0:T(2,128)} %bitcast.9, f32[16,768]{1,0:T(8,128)} %get-tuple-element.41.vec_ref, ...), custom_call_target="tpu_custom_call" | custom-call | tf_op jit(solution)/shard_map/backward_pass/pallas_call | solution.py:1345
  223.3 11.4 %table_sums.1 = (f32[3920,768]{1,0:T(8,128)}, f32[512,768]{1,0:T(8,128)}, f32[6,1,2304]{2,1,0:T(1,128)}, f32[6,1,768]{2,1,0:T(1,128)}, f32[6,1,3072]{2,1,0:T(1,1...) custom-call(bf16[128,16,384]{2,1,0:T(8,128)(2,1)} %get-tuple-element.55.rows_ref, ...), custom_call_target="tpu_custom_call" | custom-call | tf_op jit(solution)/shard_map/table_sums/pallas_call | solution.py:1400

commit v5 on v4

--- a/solution.py
+++ b/solution.py
@@ -250,10 +250,25 @@
     return owner * 8.0 + rank, both[:, :128] * 64.0 + both[:, 128:]
 
 
+def two_digits(value, base):
+    high = jnp.floor((value + 0.5) * (1.0 / base))
+    return high.astype(jnp.bfloat16), (value - base * high).astype(jnp.bfloat16)
+
+
+def hot_tiles(high, low_hot, first, count):
+    zero = jnp.zeros((), jnp.bfloat16)
+    return [jnp.where(high == (first + i).astype(jnp.bfloat16), low_hot, zero) for i in range(count)]
+
+
+def lane_names(rows):
+    return lax.broadcasted_iota(jnp.int32, (rows, 128), 1).astype(jnp.float32).astype(jnp.bfloat16)
+
+
 def slot_hot(slot_ref):
-    lane = lax.broadcasted_iota(jnp.int32, (512, 128), 1).astype(jnp.float32)
-    parts = [(slot_ref[...] == lane + 128.0 * i).astype(jnp.bfloat16) for i in range(8)]
-    return jnp.concatenate(parts, axis=1)
+    high, low = two_digits(slot_ref[...], 128.0)
+    zero = jnp.zeros((), jnp.bfloat16)
+    low_hot = jnp.where(low == lane_names(512), jnp.ones((), jnp.bfloat16), zero)
+    return jnp.concatenate(hot_tiles(high, low_hot, jnp.float32(0.0), 8), axis=1)
 
 
 def forward_kernel(
@@ -263,7 +278,7 @@
     w, vecs, tiles, h1, h2, inv, nl, act, gp, qkv, prob, ctx, x_ref, resid, pooled, rnorm, pool_own, pool_swap, pool_all,
     left3, right3, stats, own, sent_ref, near, halves_ref, half_got, table, ids_out, ids_in, ids, asked, rows_out, rows_in,
     row_mat, units_size, pool_size,
-    send_sem, recv_sem, local_sem, pool_send, pool_recv, tile_send, tile_recv, swap_sem, load_sem, save_sem,
+    send_sem, recv_sem, local_sem, pool_send, pool_recv, tile_send, tile_recv, swap_sem, save_sem,
     near_send, near_recv, ids_sem, rows_sem, table_sem,
 ):
     spot, core = where_am_i()
@@ -360,14 +375,15 @@
         small = small + near[j, 32:48, :]
     tiles[pl.ds(spot[1], 1), pl.ds(spot[2], 1)] = small.astype(bf).reshape(1, 1, 16, 128)
 
-    g = Gather(w_out, units_size, send_sem, recv_sem, spot, core, (0, 1, 2))
+    g = Gather(w, units_size, send_sem, recv_sem, spot, core, (0, 1, 2))
     every = [(r, o) for r in range(3) for o in range(3)]
     keep = []
     for r, o in every:
         copy = pltpu.make_async_copy(own.at[r, o], g.block(r, o, g.here(o), core), local_sem.at[r, o])
         copy.start()
         keep.append(copy)
-        g.begin(r, o, own.at[r, o])
+        if r < 2:
+            g.begin(r, o, own.at[r, o])
 
     def tile_push(event, at, there):
         ref = tiles.at[at]
@@ -418,14 +434,12 @@
     get_table.wait()
 
     def find(half):
-        col = asked[512 * half : 512 * half + 512, :]
-        lane = lax.broadcasted_iota(jnp.int32, (512, 128), 1).astype(f32)
+        high, low = two_digits(asked[512 * half : 512 * half + 512, :], 128.0)
+        low_hot = jnp.where(low == lane_names(512), jnp.ones((), bf), jnp.zeros((), bf))
 
         def chunk(i, _):
-            first_row = i * 512
-            base = lane + (first_row * 1).astype(f32)
-            hot = jnp.concatenate([(col == base + 128.0 * j).astype(bf) for j in range(4)], axis=1)
-            part = mm(hot, table[pl.ds(pl.multiple_of(first_row, 512), 512), :])
+            hot = jnp.concatenate(hot_tiles(high, low_hot, (4 * i).astype(f32), 4), axis=1)
+            part = mm(hot, table[pl.ds(pl.multiple_of(i * 512, 512), 512), :])
             resid[...] = jnp.where(i == 0, part, resid[...] + part)
             return 0
 
@@ -453,9 +467,8 @@
     find(1)
     for o in range(3):
         g.relay(0, o)
-    for r in (1, 2):
-        for o in range(3):
-            g.planes(r, o)
+    for o in range(3):
+        g.planes(1, o)
     tile_landed(1)
 
     row_at = lax.broadcasted_iota(jnp.int32, (128, 768), 0)
@@ -477,30 +490,24 @@
         copy.start()
         saves.append(copy)
 
-    def load(r, o, c):
-        return pltpu.make_async_copy(w_out.at[r, c, o], w.at[r, c, o], load_sem.at[r, c, o])
-
     def collect(r):
         for o in range(3):
             g.collect(r, o)
-            load(r, o, core).start()
 
     def arrived(r):
         for o in range(3):
             g.shared_done(r, o)
-            load(r, o, 1 - core).start()
-        for o in range(3):
-            load(r, o, 0).wait()
-            load(r, o, 1).wait()
+        save(w.at[r], w_out.at[r], 11 + r)
 
     save(vecs, vec_out, 0)
     for o in range(3):
         g.finish(0, o)
-        load(0, o, core).start()
     others = rows_in.at[pl.ds(0, 127)]
     pltpu.make_async_copy(others, others, rows_sem.at[1]).wait()
     for o in range(3):
         g.spread(1, o, True)
+    for o in range(3):
+        g.begin(2, o, own.at[2, o])
     for q in range(8):
         row_mat[128 * q : 128 * q + 128, :] = unpack_rows(rows_in[16 * q : 16 * q + 16])
     slots_hot = slot_hot(slot_out)
@@ -520,8 +527,6 @@
         return 0
 
     lax.fori_loop(0, 9, qkv_step, 0)
-    for o in range(3):
-        g.spread(2, o, True)
     save(qkv, qkv_out, 1)
 
     def attend(s, _):
@@ -540,6 +545,9 @@
 
     lax.fori_loop(0, 4, attend, 0)
     collect(1)
+    for o in range(3):
+        g.planes(2, o)
+        g.spread(2, o, True)
     lax.fori_loop(4, 8, attend, 0)
     save(prob, prob_out, 2)
     save(ctx, ctx_out, 3)
@@ -564,7 +572,6 @@
     save(h1, h1_out, 4)
     save(nl, nl_out, 5)
     arrived(1)
-    collect(2)
 
     def up_step(n2, _):
         weight = panel(w, 1, n2)
@@ -580,7 +587,9 @@
             gp[n2, part, :] = upper + pre * (jnp.exp(-0.5 * pre * pre) * 0.3989422804014327)
         return 0
 
-    lax.fori_loop(0, 12, up_step, 0)
+    lax.fori_loop(0, 4, up_step, 0)
+    collect(2)
+    lax.fori_loop(4, 12, up_step, 0)
     save(act, act_out, 6)
     save(gp, gp_out, 7)
     arrived(2)
@@ -789,8 +798,7 @@
             dma((6,)),
             dma((6,)),
             dma((2,)),
-            dma((3, 2, 3)),
-            dma((11,)),
+            dma((14,)),
             dma((8,)),
             dma((8,)),
             dma((2,)),
@@ -854,7 +862,7 @@
 
     def first(self, r, o):
         d = ORDERS[o][0]
-        if r > 0:
+        if True:
             for by in (1, 3, 2):
                 there = moved(self.spot, d, by)
                 src = self.mine(r, o, self.spans(o, there[d]))
@@ -877,7 +885,7 @@
 
     def third(self, r, o):
         ring, first, second = ORDERS[o]
-        views = [self.slot(r, o, k) for k in range(3 if r > 0 else 2)]
+        views = [self.slot(r, o, k) for k in range(3)]
         for k, view in enumerate(views):
             self.landed(view, r, o, k)
         self.add_into(self.mine(r, o, self.spans(o, self.spot[ring])), views)
@@ -919,6 +927,16 @@
         bufs.append(pltpu.VMEM((rounds, 3, *sizes, UNIT, 128), jnp.bfloat16))
         bufs.append(pltpu.VMEM((1, 2, *half, UNIT, 128), jnp.bfloat16))
     return bufs
+
+
+TABLE_STEP = 784
+TABLE_BASE = 112
+
+
+def asked_digits(asked_ref):
+    high, low = two_digits(jnp.broadcast_to(asked_ref[0:1, :], (TABLE_BASE, 1024)), float(TABLE_BASE))
+    name = lax.broadcasted_iota(jnp.int32, (TABLE_BASE, 1024), 0).astype(jnp.float32).astype(jnp.bfloat16)
+    return high, jnp.where(low == name, jnp.ones((), jnp.bfloat16), jnp.zeros((), jnp.bfloat16))
 
 
 def norm_back(grad, scaled, inverse, gain):
@@ -1069,7 +1087,6 @@
 
     lax.fori_loop(0, RING, pre_step, 0)
     get_w0 = load_w(0, 0)
-    take(2)
     get_nl.wait()
     turned_nl = nl[...].T
     turned[:, :] = turned_nl
@@ -1083,6 +1100,7 @@
 
     lax.fori_loop(0, 12, up_step, 0)
     give(1)
+    take(2)
     get_w1.wait()
 
     def six_blocks(at, n):
@@ -1101,7 +1119,6 @@
         return 0
 
     lax.fori_loop(0, RING, up_back_step, 0)
-    take(1)
     get_h1.wait()
 
     def norm_one_step(s, _):
@@ -1117,6 +1134,7 @@
         return 0
 
     lax.fori_loop(0, 8, norm_one_step, 0)
+    take(1)
     get_ctx.wait()
     turned[...] = jnp.concatenate([ctx[0], ctx[1], ctx[2]], axis=1).T
     get_w0.wait()
@@ -1128,7 +1146,6 @@
             n = 18 + 2 * p + k
             parts[0, n // 12, n // 4 % 3, n % 4] = block[:, 128 * k : 128 * k + 128].reshape(RING, RING, UNIT, 128)
         ctx[p] = mm_nt(d_low[...], weight[cut, :]).astype(bf)
-    third(2)
     get_qkv.wait()
     get_prob.wait()
     mask = head_mask()
@@ -1154,7 +1171,9 @@
             dvec[0, 3:4, cut] = dvec[0, 3:4, cut] + total(low_value.astype(f32))
         return 0
 
-    lax.fori_loop(0, 8, attend_back, 0)
+    lax.fori_loop(0, 4, attend_back, 0)
+    third(2)
+    lax.fori_loop(4, 8, attend_back, 0)
     vec_sent = []
 
     def vec_push(event, src, there, c):
@@ -1180,8 +1199,8 @@
         dvec[d + 2] = (dvec[d + 1] + sides) + vec_slots[2 + 3 * d]
 
     vec_push(0, dvec.at[0], spot, 1 - core)
+
     third(1)
-
     def input_step(t, _):
         low = jnp.concatenate([qkv[3 * t], qkv[3 * t + 1], qkv[3 * t + 2]], axis=1)
         weight = six_blocks(0, 6 * t)
@@ -1213,15 +1232,17 @@
     keep_rows.start()
     turned[...] = x_ref[...].T
 
-    def qkv_step(n2, _):
+    def qkv_step(i, _):
+        n2 = (i + 6 * (1 - core)) % 9
         block = mm(turned[...], qkv[n2]).astype(bf)
         c, o, x = n2 // 6, n2 // 2 % 3, n2 % 2 * 2
         for k in range(2):
             parts[0, c, o, x + k] = block[:, 128 * k : 128 * k + 128].reshape(RING, RING, UNIT, 128)
         return 0
 
-    lax.fori_loop(0, 9, qkv_step, 0)
+    lax.fori_loop(0, 6, qkv_step, 0)
     give(0)
+    lax.fori_loop(6, 9, qkv_step, 0)
     vec_landed(0)
     dvec[1] = dvec[0] + vec_slots[0]
     vec_start(0)
@@ -1230,7 +1251,6 @@
     vec_add(0)
     vec_start(1)
     fourth(1)
-    second(0)
     vec_add(1)
     vec_start(2)
     third(0)
@@ -1355,9 +1375,6 @@
     )(lens, vectors, d_pool, x, slots, w, h1, h2, inv, nl, act, gp, qkv, prob, ctx)
 
 
-TABLE_STEP = 560
-
-
 def table_kernel(
     rows_ref, asked_ref, qkv_ref, out_ref, up_ref, down_ref, vec_ref, loss_ref, token_ref,
     table_out, token_out, qkv_out, proj_out, up_out, down_out, gain_out, bias_out, loss_out, rows,
@@ -1382,8 +1399,10 @@
             bias_out[i] = across[i : i + 1, 2:12]
         loss_out[...] = loss_ref[0:2, 0:4]
 
-    name = (lax.broadcasted_iota(jnp.int32, (TABLE_STEP, 1024), 0) + at * TABLE_STEP).astype(jnp.float32)
-    table_out[...] = mm((name == asked_ref[0:1, :]).astype(jnp.bfloat16), rows[...])
+    high, low_hot = asked_digits(asked_ref)
+    first = (at * (TABLE_STEP // TABLE_BASE)).astype(jnp.float32)
+    hot = jnp.concatenate(hot_tiles(high, low_hot, first, TABLE_STEP // TABLE_BASE), axis=0)
+    table_out[...] = mm(hot, rows[...])
 
 
 def table_sums(rows, asked, d_qkv, d_out, d_up, d_down, vectors, loss, tokens, table_rows):

time: 235 us -> 226 us (0.962)
  Pallas kernels: 234 us -> 225 us
    pallas_call x1, Pallas kernels: 128 us -> 120 us  [forward_pass(): pl.pallas_call(forward_kernel, out_shape=[jax.ShapeDtypeStruct(*s) for s...]
where the time goes in v5:
time: 226 us
  Pallas kernels  225 us (100%)
    pallas_call x1, Pallas kernels, forward_pass(): pl.pallas_call(forward_kernel, out_shape=[jax.ShapeDtypeStruct(*s) for s...  120 us
    pallas_call x1, Pallas kernels, backward_pass(): pl.pallas_call(backward_kernel, out_shape=[jax.ShapeDtypeStruct(*s) for s...  94 us
    pallas_call x1, Pallas kernels, table_sums(): pl.pallas_call(table_kernel, out_shape=[jax.ShapeDtypeStruct(s, f32) for...  11 us

profile of v5, /device:TPU:1, one launch (start us, length us, event | category | flops | bytes accessed | tf_op | source)
XLA Modules:
  0.0 225.9 jit_solution(8005697747795069929)
XLA Ops:
  0.6 120.0 %forward_pass.1 = (bf16[3,2,3,4,4,4,48,128]{7,6,5,4,3,2,1,0:T(8,128)(2,1)}, f32[16,768]{1,0:T(8,128)}, f32[512,768]{1,0:T(8,128)}, f32[512,768]{1,0:T(8,128)}, f...) custom-call(s32[2,4]{1,0:T(2,128)} %bitcast.8, ...), custom_call_target="tpu_custom_call" | custom-call | tf_op jit(solution)/shard_map/forward_pass/pallas_call | solution.py:759
  120.7 94.0 %backward_pass.1 = (f32[512,768]{1,0:T(8,128)}, bf16[128,16,384]{2,1,0:T(8,128)(2,1)}, f32[6,2304]{1,0:T(8,128)}, f32[6,768]{1,0:T(8,128)}, f32[6,3072]{1,0:T(8,...) custom-call(s32[2,4]{1,0:T(2,128)} %bitcast.9, f32[16,768]{1,0:T(8,128)} %get-tuple-element.41.vec_ref, ...), custom_call_target="tpu_custom_call" | custom-call | tf_op jit(solution)/shard_map/backward_pass/pallas_call | solution.py:1365
  214.7 11.0 %table_sums.1 = (f32[3920,768]{1,0:T(8,128)}, f32[512,768]{1,0:T(8,128)}, f32[6,1,2304]{2,1,0:T(1,128)}, f32[6,1,768]{2,1,0:T(1,128)}, f32[6,1,3072]{2,1,0:T(1,1...) custom-call(bf16[128,16,384]{2,1,0:T(8,128)(2,1)} %get-tuple-element.55.rows_ref, ...), custom_call_target="tpu_custom_call" | custom-call | tf_op jit(solution)/shard_map/table_sums/pallas_call | solution.py:1419

commit v6 on v5

--- a/solution.py
+++ b/solution.py
@@ -1098,7 +1098,7 @@
             parts[1, c, o, x + k] = block[:, 128 * k : 128 * k + 128].reshape(RING, RING, UNIT, 128)
         return 0
 
-    lax.fori_loop(0, 12, up_step, 0)
+    lax.fori_loop(0, 12, up_step, 0, unroll=3)
     give(1)
     take(2)
     get_w1.wait()
@@ -1240,9 +1240,9 @@
             parts[0, c, o, x + k] = block[:, 128 * k : 128 * k + 128].reshape(RING, RING, UNIT, 128)
         return 0
 
-    lax.fori_loop(0, 6, qkv_step, 0)
+    lax.fori_loop(0, 6, qkv_step, 0, unroll=3)
     give(0)
-    lax.fori_loop(6, 9, qkv_step, 0)
+    lax.fori_loop(6, 9, qkv_step, 0, unroll=3)
     vec_landed(0)
     dvec[1] = dvec[0] + vec_slots[0]
     vec_start(0)

time: 226 us -> 225 us (level)
  no operation moved by 1% of the time
where the time goes in v6:
time: 225 us
  Pallas kernels  224 us (100%)
    pallas_call x1, Pallas kernels, forward_pass(): pl.pallas_call(forward_kernel, out_shape=[jax.ShapeDtypeStruct(*s) for s...  120 us
    pallas_call x1, Pallas kernels, backward_pass(): pl.pallas_call(backward_kernel, out_shape=[jax.ShapeDtypeStruct(*s) for s...  92.6 us
    pallas_call x1, Pallas kernels, table_sums(): pl.pallas_call(table_kernel, out_shape=[jax.ShapeDtypeStruct(s, f32) for...  11 us

profile of v6, /device:TPU:1, one launch (start us, length us, event | category | flops | bytes accessed | tf_op | source)
XLA Modules:
  0.0 224.5 jit_solution(15808951087505973051)
XLA Ops:
  0.6 120.0 %forward_pass.1 = (bf16[3,2,3,4,4,4,48,128]{7,6,5,4,3,2,1,0:T(8,128)(2,1)}, f32[16,768]{1,0:T(8,128)}, f32[512,768]{1,0:T(8,128)}, f32[512,768]{1,0:T(8,128)}, f...) custom-call(s32[2,4]{1,0:T(2,128)} %bitcast.8, ...), custom_call_target="tpu_custom_call" | custom-call | tf_op jit(solution)/shard_map/forward_pass/pallas_call | solution.py:759
  120.7 92.6 %backward_pass.1 = (f32[512,768]{1,0:T(8,128)}, bf16[128,16,384]{2,1,0:T(8,128)(2,1)}, f32[6,2304]{1,0:T(8,128)}, f32[6,768]{1,0:T(8,128)}, f32[6,3072]{1,0:T(8,...) custom-call(s32[2,4]{1,0:T(2,128)} %bitcast.9, f32[16,768]{1,0:T(8,128)} %get-tuple-element.41.vec_ref, ...), custom_call_target="tpu_custom_call" | custom-call | tf_op jit(solution)/shard_map/backward_pass/pallas_call | solution.py:1365
  213.3 11.0 %table_sums.1 = (f32[3920,768]{1,0:T(8,128)}, f32[512,768]{1,0:T(8,128)}, f32[6,1,2304]{2,1,0:T(1,128)}, f32[6,1,768]{2,1,0:T(1,128)}, f32[6,1,3072]{2,1,0:T(1,1...) custom-call(bf16[128,16,384]{2,1,0:T(8,128)(2,1)} %get-tuple-element.55.rows_ref, ...), custom_call_target="tpu_custom_call" | custom-call | tf_op jit(solution)/shard_map/table_sums/pallas_call | solution.py:1419
